TPU v7x, 32 devices: a whole 2x2x4 slice. The times are simulated.
32 devices in a mesh: wide: 8 (over z, x), narrow: 4 (over y, core).
Axes of the slice: x: 2, y: 2, z: 4, core: 2. Of those that a mesh axis runs over, the one named last changes fastest.
Arguments:
- data_x: bfloat16 [8192, 1024], P(('wide', 'narrow')), may hold values from -6 to 6
- data_group: int32 [8192], P(('wide', 'narrow')), may hold values from 0 to 7
- batch_x: bfloat16 [64, 1024], P(('wide', 'narrow')), may hold values from -6 to 6
- batch_group: int32 [64], P('wide'), may hold values from 0 to 7
- batch_index: int32 [64], P('wide'), may hold values from 0 to 8191
- prec_index: int32 [64], P('wide'), may hold values from 0 to 15
- prec_table: float32 [16], replicated, may hold values from 0.5 to 4
- targets: float32 [64, 16], P('wide'), may hold values from -6 to 6
- omega: bfloat16 [2048, 2048], replicated, may hold values from -0.125 to 0.125
- phase: float32 [2048], replicated, may hold values from -3.140625 to 3.140625
- prior_w: float32 [2048, 16], replicated, may hold values from -6 to 6
- w1_master: float32 [1024, 2048], P(None, 'narrow'), may hold values from -0.1875 to 0.1875
- w1_moment: float32 [1024, 2048], P(None, 'narrow'), may hold values from -6.1035156e-05 to 6.1035156e-05
- w1_second: float32 [1024, 2048], P(None, 'narrow'), may hold values from 1.5894572e-12 to 6.3578288e-12
- w2_master: float32 [2048, 2048], P(None, 'narrow'), may hold values from -0.125 to 0.125
- w2_moment: float32 [2048, 2048], P(None, 'narrow'), may hold values from -6.1035156e-05 to 6.1035156e-05
- w2_second: float32 [2048, 2048], P(None, 'narrow'), may hold values from 1.5894572e-12 to 6.3578288e-12
- alpha: float32 [8192, 16], P(('wide', 'narrow')), may hold values from -4 to 4
- alpha_moment: float32 [8192, 16], P(('wide', 'narrow')), may hold values from -4.5776367e-05 to 4.5776367e-05
- alpha_second: float32 [8192, 16], P(('wide', 'narrow')), may hold values from 7.6293946e-13 to 3.0517578e-12
Outputs:
- loss_sum: float32 [], replicated
- weight_total: float32 [], replicated
- norm_sq: float32 [], replicated
- w1_moment_new: float32 [1024, 2048], P(None, 'narrow')
- w1_second_new: float32 [1024, 2048], P(None, 'narrow')
- w1_new: float32 [1024, 2048], P(None, 'narrow')
- w1_copy: bfloat16 [1024, 2048], P(None, 'narrow')
- w2_moment_new: float32 [2048, 2048], P(None, 'narrow')
- w2_second_new: float32 [2048, 2048], P(None, 'narrow')
- w2_new: float32 [2048, 2048], P(None, 'narrow')
- w2_copy: bfloat16 [2048, 2048], P(None, 'narrow')
- alpha_moment_new: float32 [8192, 16], P(('wide', 'narrow'))
- alpha_second_new: float32 [8192, 16], P(('wide', 'narrow'))
- alpha_new: float32 [8192, 16], P(('wide', 'narrow'))
All inputs are finite; a program needn't handle non-finite values.
Results may differ from a plain program's by a relative error of at most 0.0065.
Values may be sent and summed in bfloat16 or wider, within the bound.
A program may use at most 320 MiB of HBM per device.

v0:
```python
import math

import jax
import jax.numpy as jnp
from jax import lax
from jax.sharding import PartitionSpec as P

FEAT = 2048
MFEAT = 2048
STEP_NUM = 10


HIGH = lax.Precision.HIGHEST


def precise(left, right):
    return jnp.dot(left, right, precision=HIGH, preferred_element_type=jnp.float32)


def adamw(weight, grad, moment, second, rate, decay):
    moment_new = 0.9 * moment + 0.1 * grad
    second_new = 0.999 * second + 0.001 * grad * grad
    m_hat = moment_new / (1.0 - 0.9**STEP_NUM)
    v_hat = second_new / (1.0 - 0.999**STEP_NUM)
    new = weight - rate * (m_hat / (jnp.sqrt(v_hat) + 1e-08) + decay * weight)
    return (moment_new, second_new, new)


def on_device(
    data_x,
    data_group,
    batch_x,
    batch_group,
    batch_index,
    prec_index,
    prec_table,
    targets,
    omega,
    phase,
    prior_w,
    w1_master,
    w1_moment,
    w1_second,
    w2_master,
    w2_moment,
    w2_second,
    alpha,
    alpha_moment,
    alpha_second,
):
    wide_count = lax.axis_size("wide")
    narrow_count = lax.axis_size("narrow")
    narrow_idx = lax.axis_index("narrow")
    rows_dev = data_x.shape[0]
    bat_own = batch_x.shape[0]
    w1_full, w2_full = (
        lax.all_gather(w1_master.astype(jnp.bfloat16), "narrow", axis=1, tiled=True),
        lax.all_gather(w2_master.astype(jnp.bfloat16), "narrow", axis=1, tiled=True),
    )
    all_rows = jnp.concatenate([data_x, batch_x], axis=0)
    pre_act = jnp.dot(all_rows, w1_full, preferred_element_type=jnp.float32)
    hid_act = jax.nn.gelu(pre_act).astype(jnp.bfloat16)
    feats = jnp.dot(hid_act, w2_full, preferred_element_type=jnp.float32).astype(jnp.bfloat16)
    table_hits = prec_index[:, None] == jnp.arange(prec_table.shape[0], dtype=jnp.int32)[None, :]
    noise_prec = jnp.sum(jnp.where(table_hits, prec_table[None, :], 0.0), axis=1)
    weight_total = lax.psum(jnp.sum(noise_prec), "wide")
    feat_cols = lax.all_gather(feats[:rows_dev], "wide", axis=0, tiled=True)
    alpha_cols = lax.all_gather(alpha, "wide", axis=0, tiled=True)
    group_cols = lax.all_gather(data_group, "wide", axis=0, tiled=True)
    batch_feat = lax.all_gather(feats[rows_dev:], "narrow", axis=0, tiled=True)
    col_count = feat_cols.shape[0]
    col_pos = jnp.arange(col_count, dtype=jnp.int32)
    col_ids = (col_pos // rows_dev * narrow_count + narrow_idx) * rows_dev + col_pos % rows_dev
    scores = jnp.einsum("if,jf->ij", batch_feat, feat_cols, preferred_element_type=jnp.float32)
    pmask = (0.5 + (batch_group[:, None] == group_cols[None, :]).astype(jnp.float32)) / FEAT
    nugget = jnp.where(batch_index[:, None] == col_ids[None, :], 1.0 / noise_prec[:, None], 0.0)
    amat = pmask * scores + nugget
    kalpha = lax.psum(precise(amat, alpha_cols), "narrow")
    scale_rff = math.sqrt(2.0 / MFEAT)
    angle_all = jnp.dot(batch_feat, omega, preferred_element_type=jnp.float32) + phase[None, :]
    prior = scale_rff * precise(jnp.cos(angle_all), prior_w)
    resid = targets - prior - kalpha
    loss_part = 0.5 * jnp.sum(noise_prec * jnp.sum(resid * resid, axis=1))
    grad_resid = noise_prec[:, None] * resid / weight_total
    alpha_grad = lax.psum_scatter(
        precise(amat.T, -grad_resid), "wide", scatter_dimension=0, tiled=True
    )
    dscore = (pmask * precise(-grad_resid, alpha_cols.T)).astype(jnp.bfloat16)
    dbatch_part = jnp.dot(dscore, feat_cols, preferred_element_type=jnp.float32)
    dbatch_own = lax.psum_scatter(
        dbatch_part.astype(jnp.bfloat16), "narrow", scatter_dimension=0, tiled=True
    ).astype(jnp.float32)
    start_row = narrow_idx * bat_own
    grad_own = lax.dynamic_slice_in_dim(grad_resid, start_row, bat_own, 0)
    angle_own = lax.dynamic_slice_in_dim(angle_all, start_row, bat_own, 0)
    dzeta = (scale_rff * jnp.sin(angle_own) * precise(grad_own, prior_w.T)).astype(jnp.bfloat16)
    dbatch_own = dbatch_own + jnp.einsum(
        "im,fm->if", dzeta, omega, preferred_element_type=jnp.float32
    )
    ddata_own = lax.psum_scatter(
        jnp.einsum("ic,if->cf", dscore, batch_feat, preferred_element_type=jnp.float32),
        "wide",
        scatter_dimension=0,
        tiled=True,
    )
    dfeat = jnp.concatenate([ddata_own, dbatch_own], axis=0).astype(jnp.bfloat16)
    dhid = jnp.einsum("rf,hf->rh", dfeat, w2_full, preferred_element_type=jnp.float32)
    gelu_out, gelu_back = jax.vjp(jax.nn.gelu, pre_act)
    dpre = gelu_back(dhid)[0].astype(jnp.bfloat16)
    w2_grad = jnp.einsum("rh,rf->hf", hid_act, dfeat, preferred_element_type=jnp.float32)
    w1_grad = jnp.einsum("rd,rh->dh", all_rows, dpre, preferred_element_type=jnp.float32)
    w1_shard, w2_shard = (
        lax.psum_scatter(
            w1_grad.astype(jnp.bfloat16), "narrow", scatter_dimension=1, tiled=True
        ).astype(jnp.float32),
        lax.psum_scatter(
            w2_grad.astype(jnp.bfloat16), "narrow", scatter_dimension=1, tiled=True
        ).astype(jnp.float32),
    )
    w1_shard, w2_shard = lax.psum((w1_shard, w2_shard), "wide")
    local_sq = (jnp.sum(w1_shard * w1_shard) + jnp.sum(w2_shard * w2_shard)) / wide_count
    local_sq = local_sq + jnp.sum(alpha_grad * alpha_grad)
    norm_sq, loss_sum = lax.psum((local_sq, loss_part / narrow_count), ("wide", "narrow"))
    clip = jnp.minimum(1.0, 0.1 / jnp.sqrt(norm_sq))
    w1_mn, w1_sn, w1_new = adamw(w1_master, clip * w1_shard, w1_moment, w1_second, 0.03, 0.01)
    w2_mn, w2_sn, w2_new = adamw(w2_master, clip * w2_shard, w2_moment, w2_second, 0.03, 0.01)
    al_mn, al_sn, al_new = adamw(alpha, clip * alpha_grad, alpha_moment, alpha_second, 0.2, 0.0)
    return (
        loss_sum,
        weight_total,
        norm_sq,
        w1_mn,
        w1_sn,
        w1_new,
        w1_new.astype(jnp.bfloat16),
        w2_mn,
        w2_sn,
        w2_new,
        w2_new.astype(jnp.bfloat16),
        al_mn,
        al_sn,
        al_new,
    )


def solution(mesh):
    return jax.shard_map(
        on_device,
        mesh=mesh,
        in_specs=(
            P(("wide", "narrow"), None),
            P(("wide", "narrow")),
            P(("wide", "narrow"), None),
            P("wide"),
            P("wide"),
            P("wide"),
            P(),
            P("wide", None),
            P(),
            P(),
            P(),
            P(None, "narrow"),
            P(None, "narrow"),
            P(None, "narrow"),
            P(None, "narrow"),
            P(None, "narrow"),
            P(None, "narrow"),
            P(("wide", "narrow"), None),
            P(("wide", "narrow"), None),
            P(("wide", "narrow"), None),
        ),
        out_specs=(
            P(),
            P(),
            P(),
            P(None, "narrow"),
            P(None, "narrow"),
            P(None, "narrow"),
            P(None, "narrow"),
            P(None, "narrow"),
            P(None, "narrow"),
            P(None, "narrow"),
            P(None, "narrow"),
            P(("wide", "narrow"), None),
            P(("wide", "narrow"), None),
            P(("wide", "narrow"), None),
        ),
        check_vma=False,
    )
```

profile of v0, /device:TPU:0, one launch (start us, length us, event | category | flops | bytes accessed | tf_op | source)
XLA Modules:
  0.0 1048.0 jit_solution(2706199674995974733)
XLA Ops:
  7.2 2.7 convert_element_type.49
  10.0 0.0 all-gather.8.cloned.1.call-start
  10.0 3.8 convert_element_type.51
  13.9 1.0 copy-done.7
  14.9 32.5 %all-gather.6.cloned.1.call-done = bf16[1024,2048]{1,0:T(8,128)(2,1)} async-done(((bf16[1024,512]{1,0:T(8,128)(2,1)}), bf16[1024,2048]{1,0:T(8,128)(2,1)}) %all-gather.6.cloned.1.call-update) | async-done | bytes 4194320 | tf_op jit(solution)/shard_map/all_gather | solution.py:57
  47.4 4.8 fusion.55
  52.2 55.6 %all-gather.8.cloned.1.call-done = bf16[2048,2048]{1,0:T(8,128)(2,1)} async-done(((bf16[2048,512]{1,0:T(8,128)(2,1)}), bf16[2048,2048]{1,0:T(8,128)(2,1)}) %all-gather.8.cloned.1.call-update) | async-done | bytes 8388624 | tf_op jit(solution)/shard_map/all_gather | solution.py:58
  107.8 6.7 convolution_convert_fusion.2
  114.6 1.0 slice.9
  115.7 0.0 reduce-scatter.5.cloned.1.call-start
  115.7 0.7 select_reduce_fusion
  116.4 22.5 %psum.44 = f32[]{:T(128)} all-reduce(f32[]{:T(128)} %get-tuple-element.14), channel_id=1, replica_groups=mesh['wide'=8,'narrow'=4] {'wide'}, use_global_device_ids=true, to_apply=%region_6.7 | all-reduce | flops 1 | bytes 8 | tf_op jit(solution)/shard_map/psum | solution.py:66
  138.9 16.6 %all-gather.1 = s32[8,1,256]{2,1,0:T(1,128)S(1)} all-gather(s32[1,1,256]{2,1,0:T(1,128)S(1)} %bitcast.28), channel_id=1, replica_groups=mesh['wide'=8,'narrow'=4] {'wide'}, dimensions={0}, use_global_device_ids=true | all-gather | bytes 9216 | tf_op jit(solution)/shard_map/all_gather | solution.py:69
  155.5 31.6 %all_gather.23 = f32[2048,16]{0,1:T(8,128)S(1)} all-gather(f32[256,16]{0,1:T(8,128)S(1)} %copy-done.8), channel_id=1, replica_groups=mesh['wide'=8,'narrow'=4] {'wide'}, dimensions={0}, use_global_device_ids=true | all-gather | bytes 147456 | tf_op jit(solution)/shard_map/all_gather | solution.py:68
  187.1 5.2 all-gather
  192.3 4.6 convolution_add_fusion
  196.9 45.1 %all-gather.10.cloned.1.call-done = bf16[2048,2048]{1,0:T(8,128)(2,1)} async-done(((bf16[256,2048]{1,0:T(8,128)(2,1)}), bf16[2048,2048]{1,0:T(8,128)(2,1)}) %all-gather.10.cloned.1.call-update) | async-done | bytes 8388624 | tf_op jit(solution)/shard_map/all_gather | solution.py:67
  242.1 5.7 fusion.1
  247.8 0.2 fusion.56
  248.0 6.2 psum.42
  254.2 1.2 multiply_divide_fusion
  255.4 0.2 fusion.2
  255.6 8.1 fusion.57
  263.7 0.0 reduce-scatter.11.cloned.1.call-start
  263.8 0.6 copy-done.20
  264.4 0.6 dynamic-slice
  265.6 4.6 convolution_convert_fusion.3
  270.2 11.6 %all-reduce = bf16[8,2048]{1,0:T(8,128)(2,1)S(1)} all-reduce(bf16[8,2048]{1,0:T(8,128)(2,1)S(1)} %convolution_convert_fusion.3), channel_id=3, replica_groups=mesh['wide'=8,'narrow'=4] {'narrow'}, use_global_device_ids=true, to_apply=%region_8.9.clone | all-reduce | flops 16384 | bytes 65536
  281.8 0.3 fusion.3
  282.1 1.0 fusion.36
  283.2 5.7 fusion.4
  288.9 255.8 %reduce-scatter.5.cloned.1.call-done = f32[256,2048]{1,0:T(8,128)} async-done(((f32[2048,2048]{1,0:T(8,128)}), f32[256,2048]{1,0:T(8,128)}) %reduce-scatter.5.cloned.1.call-update) | async-done | bytes 2097168 | tf_op jit(solution)/shard_map/reduce_scatter | solution.py:100
  544.7 1.7 convert.6
  546.4 9.8 convolution_convert_fusion.1
  556.3 9.0 convolution_convert_fusion
  565.3 0.6 multiply_reduce_fusion.4
  566.5 42.6 %reduce-scatter.11.cloned.1.call-done = f32[256,16]{0,1:T(8,128)} async-done(((f32[2048,16]{0,1:T(8,128)}), f32[256,16]{0,1:T(8,128)}) %reduce-scatter.11.cloned.1.call-update) | async-done | bytes 16400 | tf_op jit(solution)/shard_map/reduce_scatter | solution.py:85
  609.1 1.3 multiply_reduce_fusion.2
  610.5 45.3 %reduce-scatter.7.cloned.1.call-done = bf16[1024,512]{1,0:T(8,128)(2,1)} async-done(((bf16[1024,2048]{1,0:T(8,128)(2,1)}), bf16[1024,512]{1,0:T(8,128)(2,1)}) %reduce-scatter.7.cloned.1.call-update) | async-done | bytes 1048592 | tf_op jit(solution)/shard_map/reduce_scatter | solution.py:113
  655.8 74.4 %reduce-scatter.9.cloned.1.call-done = bf16[2048,512]{1,0:T(8,128)(2,1)} async-done(((bf16[2048,2048]{1,0:T(8,128)(2,1)}), bf16[2048,512]{1,0:T(8,128)(2,1)}) %reduce-scatter.9.cloned.1.call-update) | async-done | bytes 2097168 | tf_op jit(solution)/shard_map/reduce_scatter | solution.py:116
  730.2 246.8 %all-reduce.4 = (f32[1024,512]{1,0:T(8,128)}, f32[2048,512]{1,0:T(8,128)}) all-reduce(bf16[1024,512]{1,0:T(8,128)(2,1)} %reduce-scatter.7.cloned.1.call-done, bf16[2048,512]{1,0:T(8,128)(2,1)} %reduce-scatter.9.cloned.1.call-done), channel_id=1, replica_groups=mesh['wide'=8,'narrow'=4] {'wide'}, use_global_device_ids=true, to_apply=%region_10.11 | all-reduce | flops 1572864 | bytes 9437184 | tf_op jit(solution)/shard_map/psum | solution.py:120
  977.0 4.0 multiply_reduce_fusion
  981.0 1.1 multiply_reduce_fusion.1
  984.1 38.5 %all-reduce.1 = (f32[]{:T(128)}, f32[]{:T(128)}) all-reduce(f32[]{:T(128)S(6)} %div.87, f32[]{:T(128)S(6)} %add.152), channel_id=1, replica_groups=mesh['wide'=8,'narrow'=4] {'wide','narrow'}, use_global_device_ids=true, to_apply=%region_4.5 | all-reduce | flops 2 | bytes 16 | tf_op jit(solution)/shard_map/psum | solution.py:123
  1023.3 7.5 fusion.53
  1030.9 1.6 copy-done.6
  1032.4 8.1 fusion.51
  1040.5 0.6 multiply_subtract_fusion.2
  (56 shorter events, 0.5 us)
Async XLA Ops:
  7.2 247.0 %copy-start = (f32[2048,16]{0,1:T(8,128)S(1)}, f32[2048,16]{0,1:T(8,128)}, u32[]{:S(2)}) copy-start(f32[2048,16]{0,1:T(8,128)} %param.30) | copy-start | bytes 393220
  7.2 40.2 %all-gather.6.cloned.1.call-start = ((), (), s32[]{:S(2)}) async-start(), calls=%async_computation.4 | async-start | bytes 5242880 | tf_op jit(solution)/shard_map/all_gather | solution.py:57
  10.0 97.9 %all-gather.8.cloned.1.call-start = ((), (), s32[]{:S(2)}) async-start(), calls=%async_computation.5 | async-start | bytes 10485760 | tf_op jit(solution)/shard_map/all_gather | solution.py:58
  13.8 1.0 copy-start.7
  13.8 1.1 copy-start.14
  13.8 228.2 %all-gather.10.cloned.1.call-start = ((), (), s32[]{:S(2)}) async-start(), calls=%async_computation.6 | async-start | bytes 9437184 | tf_op jit(solution)/shard_map/all_gather | solution.py:67
  114.5 1.2 copy-start.18
  114.6 1.2 copy-start.19
  114.6 24.3 %copy-start.16 = (s32[256]{0:T(256)S(1)}, s32[256]{0:T(256)}, u32[]{:S(2)}) copy-start(s32[256]{0:T(256)} %param.21) | copy-start | bytes 3076
  114.6 40.9 %copy-start.8 = (f32[256,16]{0,1:T(8,128)S(1)}, f32[256,16]{0,1:T(8,128)}, u32[]{:S(2)}) copy-start(f32[256,16]{0,1:T(8,128)} %param.37) | copy-start | bytes 49156
  114.6 77.7 %copy-start.12 = (f32[2048]{0:T(1024)S(1)}, f32[2048]{0:T(1024)}, u32[]{:S(2)}) copy-start(f32[2048]{0:T(1024)} %param.29) | copy-start | bytes 24580
  115.7 429.0 %reduce-scatter.5.cloned.1.call-start = ((), (), s32[]{:S(2)}) async-start(), calls=%async_computation.7 | async-start | bytes 18874368 | tf_op jit(solution)/shard_map/reduce_scatter | solution.py:100
  192.3 49.8 %copy-start.15 = (s32[8]{0:T(128)S(1)}, s32[8]{0:T(128)}, u32[]{:S(2)}) copy-start(s32[8]{0:T(128)} %param.23) | copy-start | bytes 100
  192.3 49.8 %copy-start.17 = (s32[8]{0:T(128)S(1)}, s32[8]{0:T(128)}, u32[]{:S(2)}) copy-start(s32[8]{0:T(128)} %param.24) | copy-start | bytes 100
  242.1 12.1 %copy-start.13 = (f32[8,16]{1,0:T(8,128)S(1)}, f32[8,16]{1,0:T(8,128)}, u32[]{:S(2)}) copy-start(f32[8,16]{1,0:T(8,128)} %param.27) | copy-start | bytes 1540
  263.7 0.7 copy-start.20
  263.7 345.4 %reduce-scatter.11.cloned.1.call-start = ((), (), s32[]{:S(2)}) async-start(), calls=%async_computation.10 | async-start | bytes 147456 | tf_op jit(solution)/shard_map/reduce_scatter | solution.py:85
  283.1 372.7 %reduce-scatter.7.cloned.1.call-start = ((), (), s32[]{:S(2)}) async-start(), calls=%async_computation.8 | async-start | bytes 5242880 | tf_op jit(solution)/shard_map/reduce_scatter | solution.py:113
  556.2 173.9 %reduce-scatter.9.cloned.1.call-start = ((), (), s32[]{:S(2)}) async-start(), calls=%async_computation.9 | async-start | bytes 10485760 | tf_op jit(solution)/shard_map/reduce_scatter | solution.py:116
  977.0 4.0 copy-start.5
  977.0 46.3 %copy-start.4 = (f32[1024,512]{1,0:T(8,128)S(1)}, f32[1024,512]{1,0:T(8,128)}, u32[]{:S(2)}) copy-start(f32[1024,512]{1,0:T(8,128)} %param.31) | copy-start | bytes 6291460
  1023.3 7.6 copy-start.2
  1023.3 7.6 copy-start.3
  1023.3 9.1 copy-start.6
  1032.4 8.1 copy-start.9
  1032.4 8.1 copy-start.10
  1032.4 8.1 copy-start.11
  1032.4 8.7 copy-start.1
Sparse Core Ops, SparseCore 0:
  10.2 37.1 all-gather.5
  49.5 58.2 all-gather.7
  115.8 126.2 all-gather.9
  263.9 280.7 reduce-scatter.4
  548.8 60.3 reduce-scatter.10
  612.3 43.4 reduce-scatter.6
  658.4 71.7 reduce-scatter.8
where the time goes:
time: 1050 us
  waiting for transfers between devices  551 us (52%)
  blocking collectives  379 us (36%)
  matrix products  61.9 us (6%)
  other arithmetic  32.2 us (3%)
  between operations  18.3 us (2%)
    reduce_scatter x1, waiting for transfers between devices, on_device(): lax.psum_scatter(jnp.einsum('ic,if->cf', dscore, batch_feat, preferred_el...  256 us
    psum x1, blocking collectives, on_device(): w1_shard, w2_shard = lax.psum((w1_shard, w2_shard), 'wide')  247 us
    reduce_scatter x1, waiting for transfers between devices, on_device(): lax.psum_scatter(w2_grad.astype(jnp.bfloat16), 'narrow', scatter_dimensio...  74.4 us
    all_gather x1, waiting for transfers between devices, on_device(): lax.all_gather(w2_master.astype(jnp.bfloat16), 'narrow', axis=1, tiled=True)  55.6 us
    reduce_scatter x1, waiting for transfers between devices, on_device(): lax.psum_scatter(w1_grad.astype(jnp.bfloat16), 'narrow', scatter_dimensio...  45.3 us
    all_gather x1, waiting for transfers between devices, on_device(): feat_cols = lax.all_gather(feats[:rows_dev], 'wide', axis=0, tiled=True)  45.1 us
    reduce_scatter x1, waiting for transfers between devices, on_device(): lax.psum_scatter(precise(amat.T, -grad_resid), 'wide', scatter_dimension=...  42.6 us
    psum x1, blocking collectives, on_device(): lax.psum((local_sq, loss_part / narrow_count), ('wide', 'narrow'))  38.5 us
  transfers between devices with their start and end apart: 7, of which 7 were waited for; matrix products, arithmetic and copies ran while one was open for 5% of the time, Pallas kernels for 0%

commit v1 on v0

v1 whole, which is shorter than its diff:
```python
import math

import jax
import jax.numpy as jnp
from jax import lax
from jax.sharding import PartitionSpec as P

STEP_NUM = 10
HIGH = lax.Precision.HIGHEST
GC = math.sqrt(2.0 / math.pi)


def precise(left, right):
    return jnp.dot(left, right, precision=HIGH, preferred_element_type=jnp.float32)


def mm(left, right):
    return jnp.dot(left, right, preferred_element_type=jnp.float32)


def adamw(weight, grad, moment, second, rate, decay):
    moment_new = 0.9 * moment + 0.1 * grad
    second_new = 0.999 * second + 0.001 * grad * grad
    m_hat = moment_new / (1.0 - 0.9**STEP_NUM)
    v_hat = second_new / (1.0 - 0.999**STEP_NUM)
    new = weight - rate * (m_hat / (jnp.sqrt(v_hat) + 1e-08) + decay * weight)
    return (moment_new, second_new, new)


def gelu_pair(pre):
    t = jnp.tanh(GC * (pre + 0.044715 * pre * pre * pre))
    out = 0.5 * pre * (1.0 + t)
    grad = 0.5 * (1.0 + t) + 0.5 * pre * (1.0 - t * t) * (GC * (1.0 + 3 * 0.044715 * pre * pre))
    return out, grad


def on_device(
    data_x, data_group, batch_x, batch_group, batch_index, prec_index, prec_table, targets,
    omega, phase, prior_w, w1_master, w1_moment, w1_second, w2_master, w2_moment, w2_second,
    alpha, alpha_moment, alpha_second,
):
    bf = jnp.bfloat16
    wide = lax.axis_size("wide")
    narrow = lax.axis_size("narrow")
    wi = lax.axis_index("wide")
    ni = lax.axis_index("narrow")
    feat, mfeat = omega.shape
    w1b, w2b = w1_master.astype(bf), w2_master.astype(bf)
    fown = w2b.shape[1]
    xg = lax.all_gather(data_x, "narrow", axis=0, tiled=True)
    xb = lax.all_gather(batch_x, ("wide", "narrow"), axis=0, tiled=True)
    hits = prec_index[:, None] == jnp.arange(prec_table.shape[0], dtype=jnp.int32)[None, :]
    prec_own = jnp.sum(jnp.where(hits, prec_table[None, :], 0.0), axis=1)
    meta_own = jnp.concatenate(
        [batch_group[:, None].astype(jnp.float32), batch_index[:, None].astype(jnp.float32), prec_own[:, None], targets], axis=1)
    meta = lax.all_gather(meta_own, "wide", axis=0, tiled=True)
    dmeta = lax.all_gather(jnp.concatenate([alpha, data_group[:, None].astype(jnp.float32)], axis=1), "narrow", axis=0, tiled=True)
    alpha_g, group_g = dmeta[:, :-1], dmeta[:, -1]
    bgroup, bindex, prec, targ = meta[:, 0], meta[:, 1], meta[:, 2], meta[:, 3:]
    weight_total = jnp.sum(prec)
    batch = xb.shape[0]
    rows = xg.shape[0]

    pre_b = mm(xb, w1b)
    hb, gb = gelu_pair(pre_b)
    hid_b = lax.all_gather(hb.astype(bf), "narrow", axis=1, tiled=True)
    bfeat = mm(hid_b, w2b).astype(bf)
    om_own = lax.dynamic_slice_in_dim(omega, ni * fown, fown, 0)
    gpart = jnp.einsum("if,hf->ih", bfeat, w2b, preferred_element_type=jnp.float32)
    zpart = mm(bfeat, om_own)
    both = jnp.concatenate([gpart.reshape(batch, narrow, -1), zpart.reshape(batch, narrow, -1)], axis=2)
    both = lax.psum_scatter(both, "narrow", scatter_dimension=1, tiled=True)[:, 0]
    hown = gpart.shape[1] // narrow
    gmat = both[:, :hown].astype(bf)
    mown = mfeat // narrow
    angle = both[:, hown:] + lax.dynamic_slice_in_dim(phase, ni * mown, mown, 0)[None, :]
    pw_own = lax.dynamic_slice_in_dim(prior_w, ni * mown, mown, 0)
    scale_rff = math.sqrt(2.0 / mfeat)

    pre = mm(xg, w1b)
    hd, gd = gelu_pair(pre)
    hid = hd.astype(bf)
    scores = jnp.einsum("ih,jh->ij", gmat, hid, preferred_element_type=jnp.float32)
    pmask = (0.5 + (bgroup[:, None] == group_g[None, :]).astype(jnp.float32)) / feat
    cols = (wi * rows + jnp.arange(rows, dtype=jnp.int32)).astype(jnp.float32)
    nug = jnp.where((bindex[:, None] == cols[None, :]) & (ni == 0), 1.0 / prec[:, None], 0.0)
    amat = pmask * scores + nug
    ksum = lax.psum(precise(amat, alpha_g) + (scale_rff / wide) * precise(jnp.cos(angle), pw_own), ("wide", "narrow"))
    resid = targ - ksum
    loss_sum = 0.5 * jnp.sum(prec * jnp.sum(resid * resid, axis=1))
    gr = prec[:, None] * resid / weight_total
    agrad = lax.psum_scatter(precise(amat.T, -gr), "narrow", scatter_dimension=0, tiled=True)
    dscore = (pmask * precise(-gr, alpha_g.T)).astype(bf)
    dz = (scale_rff * jnp.sin(angle) * precise(gr, pw_own.T)).astype(bf)
    u_own = lax.psum(mm(dscore, hid), "wide").astype(bf)
    uz = lax.all_gather(jnp.stack([u_own, dz]), "narrow", axis=2, tiled=True)
    umat, dzeta = uz[0], uz[1]
    dbatch = (mm(umat, w2b) + jnp.einsum("im,fm->if", dzeta, om_own, preferred_element_type=jnp.float32)).astype(bf)
    dhid_b = lax.psum_scatter(
        jnp.einsum("if,hf->ih", dbatch, w2b, preferred_element_type=jnp.float32), "narrow", scatter_dimension=1, tiled=True)
    dpre_b = (dhid_b * gb).astype(bf)
    w2_grad = jnp.einsum("ih,if->hf", hid_b, dbatch, preferred_element_type=jnp.float32) + jnp.einsum(
        "ih,if->hf", umat, bfeat, preferred_element_type=jnp.float32)
    dhid = jnp.einsum("ij,ih->jh", dscore, gmat, preferred_element_type=jnp.float32)
    dpre = (dhid * gd).astype(bf)
    w1p = jnp.einsum("jd,jh->dh", xg, dpre, preferred_element_type=jnp.float32).astype(bf)
    w1_grad = lax.psum(w1p, "wide").astype(jnp.float32) + jnp.einsum("id,ih->dh", xb, dpre_b, preferred_element_type=jnp.float32)

    local_sq = (jnp.sum(w1_grad * w1_grad) + jnp.sum(w2_grad * w2_grad)) / wide + jnp.sum(agrad * agrad)
    norm_sq = lax.psum(local_sq, ("wide", "narrow"))
    clip = jnp.minimum(1.0, 0.1 / jnp.sqrt(norm_sq))
    w1_mn, w1_sn, w1_new = adamw(w1_master, clip * w1_grad, w1_moment, w1_second, 0.03, 0.01)
    w2_mn, w2_sn, w2_new = adamw(w2_master, clip * w2_grad, w2_moment, w2_second, 0.03, 0.01)
    al_mn, al_sn, al_new = adamw(alpha, clip * agrad, alpha_moment, alpha_second, 0.2, 0.0)
    return (
        loss_sum, weight_total, norm_sq,
        w1_mn, w1_sn, w1_new, w1_new.astype(bf),
        w2_mn, w2_sn, w2_new, w2_new.astype(bf),
        al_mn, al_sn, al_new,
    )


def solution(mesh):
    both = P(("wide", "narrow"))
    both2 = P(("wide", "narrow"), None)
    col = P(None, "narrow")
    return jax.shard_map(
        on_device,
        mesh=mesh,
        in_specs=(both2, both, both2, P("wide"), P("wide"), P("wide"), P(), P("wide", None), P(), P(), P())
        + (col,) * 6 + (both2,) * 3,
        out_specs=(P(), P(), P()) + (col,) * 8 + (both2,) * 3,
        check_vma=False,
    )
```

time: 1050 us -> 388 us (0.37)
  waiting for transfers between devices: 551 us -> 74.8 us
  blocking collectives: 379 us -> 207 us
  matrix products: 61.9 us -> 39.4 us
  local copies, waits for them, and re-layouts: 4.91 us -> 20.2 us
    reduce_scatter x4 -> x3, waiting for transfers between devices: 418 us -> 24.3 us  [the longest x1 24.3 us: on_device(): lax.psum_scatter(jnp.einsum('if,hf->ih', dbatch, w2b, preferred_element_t...]
    psum x4 -> x3, blocking collectives: 314 us -> 115 us  [the longest x1 39.4 us: on_device(): norm_sq = lax.psum(local_sq, ('wide', 'narrow'))]
    all_gather x3 -> x1, waiting for transfers between devices: 133 us -> 0.01 us  [on_device(): xg = lax.all_gather(data_x, 'narrow', axis=0, tiled=True)]
    psum x0 -> x1, waiting for transfers between devices: none -> 49.7 us  [on_device(): lax.psum(w1p, 'wide').astype(jnp.float32)]
    all_gather x3 -> x5, blocking collectives: 53.3 us -> 92.1 us  [the longest x1 43.8 us: on_device(): xb = lax.all_gather(batch_x, ('wide', 'narrow'), axis=0, tiled=True)]
    dot_general x9 -> x14, matrix products: 58.9 us -> 32.3 us  [the longest x6 12.6 us: mm(): return jnp.dot(left, right, preferred_element_type=jnp.float32)]
    unnamed x46 -> x65, local copies, waits for them, and re-layouts: 3.86 us -> 18.5 us
    unnamed x1 -> x0, blocking collectives: 11.6 us -> none
  transfers between devices with their start and end apart: 7 -> 5, of which waited for: 7 -> 2; matrix products, arithmetic and copies ran while one was open for 5% -> 11% of each run, Pallas kernels for 0% -> 0%
where the time goes in v1:
time: 388 us; the launch traced here: 387 us
  blocking collectives  207 us (53%)
  waiting for transfers between devices  74.8 us (19%)
  matrix products  39.4 us (10%)
  other arithmetic  27.5 us (7%)
  local copies, waits for them, and re-layouts  20.2 us (5%)
  between operations  18.5 us (5%)
    psum x1, waiting for transfers between devices, on_device(): lax.psum(w1p, 'wide').astype(jnp.float32)  49.7 us
    all_gather x1, blocking collectives, on_device(): xb = lax.all_gather(batch_x, ('wide', 'narrow'), axis=0, tiled=True)  43.8 us
    psum x1, blocking collectives, on_device(): norm_sq = lax.psum(local_sq, ('wide', 'narrow'))  39.4 us
    psum x1, blocking collectives, on_device(): u_own = lax.psum(mm(dscore, hid), 'wide').astype(bf)  38.2 us
    psum x1, blocking collectives, on_device(): lax.psum(precise(amat, alpha_g) + scale_rff / wide * precise(jnp.cos(angl...  36.9 us
    all_gather x1, blocking collectives, on_device(): meta = lax.all_gather(meta_own, 'wide', axis=0, tiled=True)  30.4 us
    reduce_scatter x1, waiting for transfers between devices, on_device(): lax.psum_scatter(jnp.einsum('if,hf->ih', dbatch, w2b, preferred_element_t...  24.3 us
    unnamed x65, local copies, waits for them, and re-layouts  18.5 us
  transfers between devices with their start and end apart: 5, of which 2 were waited for; matrix products, arithmetic and copies ran while one was open for 11% of the time, Pallas kernels for 0%

profile of v1, /device:TPU:0, one launch (start us, length us, event | category | flops | bytes accessed | tf_op | source)
XLA Modules:
  0.0 387.3 jit_solution(7706738427149166895)
XLA Ops:
  7.2 0.7 all-gather.3.cloned.1.call-update
  8.0 2.5 convert_element_type.86
  10.5 43.8 %all-gather = bf16[32,2,1024]{2,1,0:T(2,128)(2,1)S(1)} all-gather(bf16[1,2,1024]{2,1,0:T(2,128)(2,1)S(1)} %bitcast.64), channel_id=1, replica_groups=mesh['wide'=8,'narrow'=4] {'wide','narrow'}, dimensions={0}, use_global_device_ids=true | all-gather | bytes 135168 | tf_op jit(solution)/shard_map/all_gather | solution.py:51
  54.3 2.6 multiply_convert_fusion.1
  56.9 5.8 %all_gather.21 = bf16[64,2048]{1,0:T(8,128)(2,1)S(1)} all-gather(bf16[64,512]{1,0:T(8,128)(2,1)S(1)} %get-tuple-element.90), channel_id=1, replica_groups=mesh['wide'=8,'narrow'=4] {'narrow'}, dimensions={1}, use_global_device_ids=true | all-gather | bytes 327680 | tf_op jit(solution)/shard_map/all_gather | solution.py:66
  63.3 2.1 fusion.12
  65.4 0.7 fusion.74
  66.3 1.1 pad_maximum_fusion
  67.9 5.3 %all_gather.19 = f32[1024,17]{0,1:T(8,128)S(1)} all-gather(f32[256,17]{0,1:T(8,128)S(1)} %pad_maximum_fusion.2), channel_id=1, replica_groups=mesh['wide'=8,'narrow'=4] {'narrow'}, dimensions={0}, use_global_device_ids=true | all-gather | bytes 87040 | tf_op jit(solution)/shard_map/all_gather | solution.py:57
  73.3 0.6 copy-done.11
  73.9 1.3 dynamic_slice.10
  75.3 30.4 %all_gather.18 = f32[64,19]{1,0:T(8,128)S(1)} all-gather(f32[8,19]{1,0:T(8,128)S(1)} %pad_maximum_fusion.3), channel_id=1, replica_groups=mesh['wide'=8,'narrow'=4] {'wide'}, dimensions={0}, use_global_device_ids=true | all-gather | bytes 5472 | tf_op jit(solution)/shard_map/all_gather | solution.py:56
  105.9 0.8 slice_reduce_fusion.2
  106.7 5.1 %multiply_convert_fusion = (bf16[1024,512]{1,0:T(8,128)(2,1)S(1)}, f32[1024,512]{1,0:T(8,128)}) fusion(bf16[1024,1024]{1,0:T(8,128)(2,1)} %all-gather.3.cloned.1.call-done, f32[1024,512]{1,0:T(8,128)} %param.31), kind=kOutput, calls=%fused_computation.22 | convolution fusion | flops 1078984704 | bytes 7340032 | tf_op jit(solution)/shard_map/dot_general | solution.py:18
  111.8 1.4 fusion.15
  113.2 0.7 copy-done.3
  113.9 1.1 fusion.47
  115.0 1.6 fusion.20
  116.6 36.9 %psum.28 = f32[64,16]{0,1:T(8,128)} all-reduce(f32[64,16]{0,1:T(8,128)S(1)} %fusion.20), channel_id=1, replica_groups=mesh['wide'=8,'narrow'=4] {'wide','narrow'}, use_global_device_ids=true, to_apply=%region_2.3 | all-reduce | flops 1024 | bytes 8192 | tf_op jit(solution)/shard_map/psum | solution.py:88
  153.5 1.9 multiply_divide_fusion
  155.4 1.9 fusion.16
  157.3 1.8 fusion.52
  159.2 1.9 fusion.75
  161.1 5.9 %fusion.14 = bf16[1024,512]{0,1:T(8,128)(2,1)} fusion(bf16[1024,1024]{1,0:T(8,128)(2,1)} %all-gather.3.cloned.1.call-done, f32[1024,512]{1,0:T(8,128)} %get-tuple-element.89, bf16[64,1024]{1,0:T(8,128)(2,1)} %fusion.16, f32[64,1024]{1,0:T(8,128)} %bitcast.59), kind=kOutput, calls=%fused_computation.28 | convolution fusion | flops 1151336448 | bytes 5439488 | tf_op jit(solution)/shard_map/jd,jh->dh/dot_general | solution.py:106
  167.0 38.2 %all-reduce.4 = bf16[64,512]{1,0:T(8,128)(2,1)S(1)} all-reduce(f32[64,512]{1,0:T(8,128)S(1)} %copy-done.9), channel_id=1, replica_groups=mesh['wide'=8,'narrow'=4] {'wide'}, use_global_device_ids=true, to_apply=%region_7.8 | all-reduce | flops 32768 | bytes 196608 | tf_op jit(solution)/shard_map/psum | solution.py:95
  205.3 0.7 fusion.19
  206.0 6.7 %all_gather.23 = bf16[2,64,2048]{2,1,0:T(8,128)(2,1)S(1)} all-gather(bf16[2,64,512]{2,1,0:T(8,128)(2,1)S(1)} %pad_maximum_fusion.1), channel_id=1, replica_groups=mesh['wide'=8,'narrow'=4] {'narrow'}, dimensions={2}, use_global_device_ids=true | all-gather | bytes 655360 | tf_op jit(solution)/shard_map/all_gather | solution.py:96
  212.7 2.4 fusion.10
  215.1 0.5 fusion.17
  215.6 1.5 fusion.76
  217.2 1.9 copy.82
  219.1 2.9 copy.79
  222.0 2.9 copy.80
  224.9 0.6 multiply_reduce_fusion.4
  225.5 0.7 fusion.77
  226.4 3.3 multiply_reduce_fusion
  229.7 1.3 multiply_reduce_fusion.2
  231.0 49.7 %all-reduce.3.cloned.1.call-done = bf16[1024,512]{0,1:T(8,128)(2,1)} async-done(((bf16[1024,512]{0,1:T(8,128)(2,1)}), bf16[1024,512]{0,1:T(8,128)(2,1)}) %all-reduce.3.cloned.1.call-update) | async-done | bytes 1048592 | tf_op jit(solution)/shard_map/psum | solution.py:107
  280.7 24.3 %reduce-scatter.6.cloned.1.call-done = f32[64,512]{1,0:T(8,128)} async-done(((f32[64,2048]{1,0:T(8,128)}), f32[64,512]{1,0:T(8,128)}) %reduce-scatter.6.cloned.1.call-update) | async-done | bytes 131088 | tf_op jit(solution)/shard_map/reduce_scatter | solution.py:99
  305.0 3.7 multiply_reduce_fusion.1
  311.3 39.4 %psum.31 = f32[]{:T(128)} all-reduce(f32[]{:T(128)S(6)} %add.156), channel_id=1, replica_groups=mesh['wide'=8,'narrow'=4] {'wide','narrow'}, use_global_device_ids=true, to_apply=%region_13.14 | all-reduce | flops 1 | bytes 8 | tf_op jit(solution)/shard_map/psum | solution.py:110
  351.4 7.0 %fusion.72 = (bf16[1024,512]{0,1:T(8,128)(2,1)S(1)}, f32[1024,512]{0,1:T(8,128)}, f32[1024,512]{0,1:T(8,128)}, f32[1024,512]{0,1:T(8,128)}) fusion(f32[1024,512]{0,1:T(8,128)S(1)} %copy.82, f32[1024,512]{0,1:T(8,128)} %get-tuple-element.93, f32[]{:T(128)S(6)} %min.3, f32[1024,512]{0,1:T(8,128)} %copy.80, f32[1024,512]{0,1:T(8,128)} %copy.79), kind=kLoop, calls=%fused_computation.121 | loop fusion | flops 8912896 | bytes 15728644 | tf_op jit(solution)/shard_map/convert_element_type | solution.py:117
  358.4 2.9 copy.83
  361.3 3.0 copy.84
  364.3 1.8 copy.85
  366.1 1.3 copy.86
  367.4 11.5 %fusion.70 = (bf16[2048,512]{1,0:T(8,128)(2,1)}, f32[2048,512]{1,0:T(8,128)}, f32[2048,512]{1,0:T(8,128)}, f32[2048,512]{1,0:T(8,128)}) fusion(f32[2048,512]{1,0:T(8,128)} %param.34, f32[2048,512]{1,0:T(8,128)} %get-tuple-element.95, f32[]{:T(128)S(6)} %min.3, f32[2048,512]{1,0:T(8,128)} %param.36, f32[2048,512]{1,0:T(8,128)} %param.35), kind=kLoop, calls=%fused_computation.120 | loop fusion | flops 17825792 | bytes 31457284 | tf_op jit(solution)/shard_map/convert_element_type | solution.py:118
  379.0 0.6 multiply_subtract_fusion.2
  (83 shorter events, 1.8 us)
Async XLA Ops:
  7.2 107.8 %copy-start = (f32[2048,16]{0,1:T(8,128)S(1)}, f32[2048,16]{0,1:T(8,128)}, u32[]{:S(2)}) copy-start(f32[2048,16]{0,1:T(8,128)} %param.30) | copy-start | bytes 393220
  7.2 99.5 %all-gather.3.cloned.1.call-start = ((), (), s32[]{:S(2)}) async-start(), calls=%async_computation.4 | async-start | bytes 2621440 | tf_op jit(solution)/shard_map/all_gather | solution.py:50
  7.9 103.9 %reduce-scatter.4.cloned.1.call-start = ((), (), s32[]{:S(2)}) async-start(), calls=%async_computation.3 | async-start | bytes 1310720 | tf_op jit(solution)/shard_map/reduce_scatter | solution.py:72
  8.0 2.5 copy-start.19
  54.3 8.9 %copy-start.4 = (bf16[64,1024]{1,0:T(8,128)(2,1)}, bf16[64,1024]{1,0:T(8,128)(2,1)S(1)}, u32[]{:S(2)}) copy-start(bf16[64,1024]{1,0:T(8,128)(2,1)S(1)} %reshape.49) | copy-start | bytes 393220
  63.2 2.9 copy-start.6
  66.2 1.2 copy-start.24
  66.2 1.3 copy-start.25
  66.2 1.4 copy-start.26
  66.3 1.4 copy-start.27
  66.3 1.6 copy-start.22
  66.3 1.6 copy-start.13
  66.3 9.0 %copy-start.20 = (f32[8,16]{1,0:T(8,128)S(1)}, f32[8,16]{1,0:T(8,128)}, u32[]{:S(2)}) copy-start(f32[8,16]{1,0:T(8,128)} %param.27) | copy-start | bytes 1540
  67.4 162.3 %reduce-scatter.8.cloned.1.call-start = ((), (), s32[]{:S(2)}) async-start(), calls=%async_computation.7 | async-start | bytes 81920 | tf_op jit(solution)/shard_map/reduce_scatter | solution.py:92
  73.3 0.6 copy-start.11
  73.9 37.9 %copy-start.16 = (f32[1024,1]{0,1:T(1,128)}, f32[1024,1]{0,1:T(1,128)S(1)}, u32[]{:S(2)}) copy-start(f32[1024,1]{0,1:T(1,128)S(1)} %slice.44) | copy-start | bytes 12292
  113.2 0.7 copy-start.3
  161.1 119.6 %all-reduce.3.cloned.1.call-start = ((), (), s32[]{:S(2)}) async-start(), calls=%async_computation.5 | async-start | bytes 2097152 | tf_op jit(solution)/shard_map/psum | solution.py:107
  161.1 5.9 %copy-start.9 = (f32[64,512]{1,0:T(8,128)S(1)}, f32[64,512]{1,0:T(8,128)}, u32[]{:S(2)}) copy-start(f32[64,512]{1,0:T(8,128)} %fusion.75) | copy-start | bytes 393220
  161.1 44.1 %copy-start.8 = (f32[64,1,1024]{2,0,1:T(8,128)S(1)}, f32[64,1,1024]{2,0,1:T(8,128)}, u32[]{:S(2)}) copy-start(f32[64,1,1024]{2,0,1:T(8,128)} %reduce-scatter.4.cloned.1.call-done) | copy-start | bytes 786436
  161.1 44.1 %copy-start.15 = (f32[512]{0:T(512)S(1)}, f32[512]{0:T(512)}, u32[]{:S(2)}) copy-start(f32[512]{0:T(512)} %dynamic_slice.10) | copy-start | bytes 6148
  206.0 99.1 %reduce-scatter.6.cloned.1.call-start = ((), (), s32[]{:S(2)}) async-start(), calls=%async_computation.6 | async-start | bytes 655360 | tf_op jit(solution)/shard_map/reduce_scatter | solution.py:99
  222.0 2.9 copy-start.21
  222.0 2.9 copy-start.23
  225.5 0.8 copy-start.7
  226.3 78.7 %copy-start.5 = (bf16[64,1024]{1,0:T(8,128)(2,1)S(1)}, bf16[64,1024]{1,0:T(8,128)(2,1)}, u32[]{:S(2)}) copy-start(bf16[64,1024]{1,0:T(8,128)(2,1)} %copy-done.4) | copy-start | bytes 393220
  226.3 78.7 %copy-start.10 = (f32[64,512]{1,0:T(8,128)S(1)}, f32[64,512]{1,0:T(8,128)}, u32[]{:S(2)}) copy-start(f32[64,512]{1,0:T(8,128)} %get-tuple-element.91) | copy-start | bytes 393220
  361.3 3.0 copy-start.2
  367.4 11.5 %copy-start.12 = (f32[256,16]{0,1:T(8,128)S(1)}, f32[256,16]{0,1:T(8,128)}, u32[]{:S(2)}) copy-start(f32[256,16]{0,1:T(8,128)} %reduce-scatter.8.cloned.1.call-done) | copy-start | bytes 49156
  367.4 11.5 %copy-start.14 = (f32[256,16]{0,1:T(8,128)S(1)}, f32[256,16]{0,1:T(8,128)}, u32[]{:S(2)}) copy-start(f32[256,16]{0,1:T(8,128)} %param.37) | copy-start | bytes 49156
  367.4 11.5 %copy-start.17 = (f32[256,16]{0,1:T(8,128)S(1)}, f32[256,16]{0,1:T(8,128)}, u32[]{:S(2)}) copy-start(f32[256,16]{0,1:T(8,128)} %param.39) | copy-start | bytes 49156
  367.4 11.5 %copy-start.18 = (f32[256,16]{0,1:T(8,128)S(1)}, f32[256,16]{0,1:T(8,128)}, u32[]{:S(2)}) copy-start(f32[256,16]{0,1:T(8,128)} %param.38) | copy-start | bytes 49156
  367.4 12.2 %copy-start.1 = (f32[2048,16]{0,1:T(8,128)S(1)}, f32[2048,16]{0,1:T(8,128)}, u32[]{:S(2)}) copy-start(f32[2048,16]{0,1:T(8,128)} %param.30) | copy-start | bytes 393220
Sparse Core Ops, SparseCore 0:
  9.6 25.7 all-gather.2
  67.5 21.1 reduce-scatter.3
  161.2 20.1 reduce-scatter.7
  206.1 74.5 all-reduce.2
  283.8 21.2 reduce-scatter.5

commit v2 on v1

v2 whole, which is shorter than its diff:
```python
import math
from types import SimpleNamespace

import jax
import jax.numpy as jnp
from jax import lax
from jax.experimental import pallas as pl
from jax.experimental.pallas import tpu as pltpu
from jax.sharding import PartitionSpec as P

STEP_NUM = 10
HIGH = lax.Precision.HIGHEST
MESH = pl.DeviceIdType.MESH
GC = math.sqrt(2.0 / math.pi)
F32 = jnp.float32
BF = jnp.bfloat16


def adamw(weight, grad, moment, second, rate, decay):
    moment_new = 0.9 * moment + 0.1 * grad
    second_new = 0.999 * second + 0.001 * grad * grad
    m_hat = moment_new / (1.0 - 0.9**STEP_NUM)
    v_hat = second_new / (1.0 - 0.999**STEP_NUM)
    new = weight - rate * (m_hat / (jnp.sqrt(v_hat) + 1e-08) + decay * weight)
    return (moment_new, second_new, new)


def gelu_pair(pre):
    square = pre * pre
    t = jnp.tanh(pre * (GC + (GC * 0.044715) * square))
    half = 0.5 * (1.0 + t)
    slope = half + 0.5 * pre * (1.0 - t * t) * (GC + (3 * GC * 0.044715) * square)
    return pre * half, slope


def dot(left, right, dims=((1,), (0,)), precision=None):
    return lax.dot_general(left, right, (dims, ((), ())), precision=precision, preferred_element_type=F32)


NT = ((1,), (1,))
TN = ((0,), (0,))


class Exchange:
    def __init__(self, axis, size, me, send, recv):
        self.axis, self.size, self.me, self.send, self.recv = axis, size, me, send, recv

    def copy(self, src, dst, p, slot):
        return pltpu.make_async_remote_copy(
            src_ref=src, dst_ref=dst, send_sem=self.send.at[p], recv_sem=self.recv.at[slot],
            device_id={self.axis: p}, device_id_type=MESH)

    def loop(self, body):
        def step(k, carry):
            body(lax.rem(self.me + k, self.size))
            return carry

        lax.fori_loop(1, self.size, step, 0)

    def gather(self, buf):
        self.loop(lambda p: self.copy(buf.at[self.me], buf.at[self.me], p, self.me).start())

    def scatter(self, src, buf):
        self.loop(lambda p: self.copy(src.at[p], buf.at[self.me], p, self.me).start())

    def wait(self, buf):
        self.loop(lambda p: self.copy(buf.at[p], buf.at[p], p, p).wait_recv())

    def drain(self, buf):
        self.loop(lambda p: self.copy(buf.at[p], buf.at[p], p, p).wait_send())


WIDE_EX = ("meta", "xbw", "hgw", "bfw", "gw", "kw", "ur", "uz", "nw")
NARROW_EX = ("xbn", "ad", "hbn", "gzr", "kn", "agr", "uzn", "dhr", "nn")


def step_kernel(W, N, names, *refs):
    r = SimpleNamespace(**dict(zip(names, refs)))
    wi, ni = lax.axis_index("wide"), lax.axis_index("narrow")
    A = W // 2
    a, b = wi // 2, lax.rem(wi, 2)
    pair = wi + 1 - 2 * b
    n1 = ni + 1 - 2 * lax.rem(ni, 2)
    n2 = lax.rem(ni + 2, N)
    n3 = lax.rem(n1 + 2, N)
    xg, hid, gd, xT, dpre = r.xg, r.hid, r.gd, r.xT, r.dpre
    w1b, w2b, om = r.w1b, r.w2b, r.om
    _, R, D = xg.shape
    Bg, S = r.targets.shape
    brow = r.batch_x.shape[0]
    Hn, Fn = w1b.shape[1], w2b.shape[1]
    H, F, M = w2b.shape[0], r.omega.shape[0], r.omega.shape[1]
    Mn = M // N
    B = W * Bg
    half = D // 2
    Ck = half // A
    scale = math.sqrt(2.0 / M)
    lsem = r.lsem
    ex = SimpleNamespace()
    for name in WIDE_EX:
        vars(ex)[name] = Exchange("wide", W, wi, getattr(r, name + "_s"), getattr(r, name + "_r"))
    for name in NARROW_EX:
        vars(ex)[name] = Exchange("narrow", N, ni, getattr(r, name + "_s"), getattr(r, name + "_r"))

    own_f = pl.ds(pl.multiple_of(ni * Fn, Fn), Fn)
    own_m = pl.ds(pl.multiple_of(ni * Mn, Mn), Mn)
    loads = [
        pltpu.make_async_copy(r.w1, r.w1f, lsem.at[0]),
        pltpu.make_async_copy(r.data_x, xg.at[ni], lsem.at[1]),
        pltpu.make_async_copy(r.w2, r.w2f, lsem.at[2]),
        pltpu.make_async_copy(r.omega.at[own_f], om, lsem.at[3]),
        pltpu.make_async_copy(r.prior_wt.at[:, own_m], r.pwt, lsem.at[4]),
    ]
    for load in loads:
        load.start()

    barrier = pltpu.get_barrier_semaphore()

    def greet(axis, size, me):
        def step(k, carry):
            pl.semaphore_signal(barrier, inc=1, device_id={axis: lax.rem(me + k, size)}, device_id_type=MESH)
            return carry

        lax.fori_loop(1, size, step, 0)

    greet("narrow", N, ni)
    greet("wide", W, wi)

    r.xbn[ni] = r.batch_x[...].astype(F32)
    lane = lax.broadcasted_iota(jnp.int32, (1, 128), 1)
    for k in range(Bg):
        prec_k = r.ptable[r.pindex[k]]
        r.meta[wi, k : k + 1, :] = jnp.where(
            lane == 0, r.bgroup[k].astype(F32),
            jnp.where(lane == 1, r.bindex[k].astype(F32), jnp.where(lane == 2, prec_k, 0.0)))
    r.meta[wi, :, S : 2 * S] = r.targets[...]
    r.ad[ni, 0:S, :] = r.alphat_own[...]
    r.ad[ni, S : S + 8, :] = jnp.broadcast_to(r.dgroup[...].astype(F32), (8, R))

    pl.semaphore_wait(barrier, W - 1 + N - 1)

    def xcopy(src, dst, k, p):
        return pltpu.make_async_remote_copy(
            src_ref=src, dst_ref=dst, send_sem=r.x_s.at[k], recv_sem=r.x_r.at[k],
            device_id={"narrow": p}, device_id_type=MESH)

    ex.xbn.gather(r.xbn)
    xcopy(r.data_x, xg.at[ni], 0, n1).start()
    xcopy(r.data_x, xg.at[ni], 1, n2).start()
    ex.meta.gather(r.meta)
    ex.ad.gather(r.ad)

    loads[0].wait()

    def cast1(k, carry):
        rows = pl.ds(pl.multiple_of(k * 128, 128), 128)
        w1b[rows, :] = r.w1f[rows, :].astype(BF)
        return carry

    lax.fori_loop(0, D // 128, cast1, 0)
    ex.xbn.wait(r.xbn)
    for n in range(N):
        r.xbg[n * brow : (n + 1) * brow, :] = r.xbn[n]
    xbg = r.xbg[...]
    hb, gb = gelu_pair(dot(xbg.astype(BF), w1b[...]))
    hb = hb.astype(BF).astype(F32)
    r.hbn[ni] = hb
    ex.hbn.gather(r.hbn)
    r.hgw[wi] = jnp.concatenate([hb, gb], axis=0).astype(BF)
    ex.hgw.gather(r.hgw)
    r.xbw[wi] = jnp.concatenate([xbg[:, : D // 2], xbg[:, D // 2 :]], axis=0).astype(BF)
    ex.xbw.gather(r.xbw)
    loads[2].wait()

    def cast2(k, carry):
        rows = pl.ds(pl.multiple_of(k * 128, 128), 128)
        w2b[rows, :] = r.w2f[rows, :].astype(BF)
        return carry

    lax.fori_loop(0, H // 128, cast2, 0)

    def block(q):
        base = q * R
        r.pre[...] = dot(xg[q], w1b[...])

        def part(k, carry):
            src = pl.ds(pl.multiple_of(k * 32, 32), 32)
            dst = pl.ds(pl.multiple_of(base + k * 32, 32), 32)
            out, slope = gelu_pair(r.pre[src, :])
            hid[dst, :] = out.astype(BF)
            gd[dst, :] = slope
            return carry

        lax.fori_loop(0, R // 32, part, 0)

    def turn(q):
        xT[:, pl.ds(pl.multiple_of(q * R, R), R)] = xg[q].T

    loads[3].wait()
    ex.hbn.wait(r.hbn)
    hid_g = jnp.concatenate([r.hbn[n] for n in range(N)], axis=1).astype(BF)
    bfeat = dot(hid_g, w2b[...]).astype(BF)
    gpart = dot(bfeat, w2b[...], NT)
    zpart = dot(bfeat, om[...])
    for n in range(N):
        r.gzs[n, :, :Hn] = gpart[:, n * Hn : (n + 1) * Hn]
        r.gzs[n, :, Hn:] = zpart[:, n * Mn : (n + 1) * Mn]
    ex.gzr.scatter(r.gzs, r.gzr)
    r.gzr[ni] = r.gzs[ni]
    bf32 = bfeat.astype(F32)
    r.bfw[wi] = jnp.concatenate([bf32[:, : Fn // 2], bf32[:, Fn // 2 :]], axis=0).astype(BF)
    ex.bfw.gather(r.bfw)
    loads[1].wait()
    block(ni)
    ex.gzr.wait(r.gzr)
    gz = jnp.sum(r.gzr[...], axis=0)
    r.gw[wi] = jnp.concatenate([gz[:, : Hn // 2], gz[:, Hn // 2 : Hn]], axis=0).astype(BF)
    ex.gw.gather(r.gw)
    own_b = pl.ds(pl.multiple_of(wi * Bg, Bg), Bg)
    angle = gz[:, Hn:] + r.phase[:, own_m]
    r.cz[...] = jnp.zeros_like(r.cz)
    r.cz[own_b, :] = scale * jnp.cos(angle)
    r.sz[...] = scale * jnp.sin(angle)
    loads[4].wait()
    r.prior[...] = dot(r.pwt[...], r.cz[...], NT, HIGH)

    xcopy(r.data_x, xg.at[n1], 0, n1).wait_recv()
    block(n1)
    xcopy(r.data_x, xg.at[n2], 1, n2).wait_recv()
    xcopy(xg.at[n2], xg.at[n2], 2, n1).start()
    block(n2)
    turn(ni)
    turn(n1)
    ex.meta.wait(r.meta)
    ex.ad.wait(r.ad)
    meta = r.meta[...].reshape(B, 128)
    r.metat[...] = meta.T
    alphat = jnp.concatenate([r.ad[n, 0:S, :] for n in range(N)], axis=1)
    r.alphat[...] = alphat
    group = jnp.concatenate([r.ad[n, S : S + 1, :] for n in range(N)], axis=1)
    pmask = (0.5 + (meta[:, 0:1] == group).astype(F32)) / F
    r.pmask[...] = pmask
    col = lax.broadcasted_iota(jnp.int32, (1, N * R), 1) + wi * (N * R)
    first = (ni == 0).astype(F32)
    r.amat[...] = jnp.where(meta[:, 1:2] == col.astype(F32), first / meta[:, 2:3], 0.0)
    xcopy(r.data_x, xg.at[n3], 2, n1).wait_recv()
    block(n3)

    ex.gw.wait(r.gw)
    gw = r.gw[...].astype(F32)
    gmat = jnp.concatenate([gw[:, :Bg].reshape(B, Hn // 2), gw[:, Bg:].reshape(B, Hn // 2)], axis=1).astype(BF)
    r.gmat[...] = gmat
    amat = r.pmask[...] * dot(gmat, hid[...], NT) + r.amat[...]
    r.amat[...] = amat
    r.kn[ni] = dot(r.alphat[...], amat, NT, HIGH) + r.prior[...]
    ex.kn.gather(r.kn)
    turn(n2)
    turn(n3)
    ex.kn.wait(r.kn)
    r.kw[wi] = jnp.sum(r.kn[...], axis=0)
    ex.kw.gather(r.kw)
    ex.xbw.wait(r.xbw)
    xbw = r.xbw[...].astype(F32)
    r.xbt[...] = jnp.concatenate([xbw[:, :Bg].reshape(B, D // 2), xbw[:, Bg:].reshape(B, D // 2)], axis=1).T.astype(BF)
    ex.kw.wait(r.kw)
    prec = r.metat[2:3, :]
    resid = r.metat[S : 2 * S, :] - jnp.sum(r.kw[...], axis=0)
    total = jnp.sum(prec, axis=1, keepdims=True)
    loss = 0.5 * jnp.sum(jnp.sum(prec * (resid * resid), axis=1, keepdims=True), axis=0, keepdims=True)
    grt = prec * resid / total

    ds = (-r.pmask[...] * dot(grt, r.alphat[...], TN, HIGH)).astype(BF)
    upart = dot(ds, hid[...])
    r.us[...] = upart.reshape(W, Bg, Hn)
    ex.ur.scatter(r.us, r.ur)
    for q in range(N):
        rows = slice(q * R, (q + 1) * R)
        dpre[rows, :] = (dot(ds[:, rows], r.gmat[...], TN) * gd[rows, :]).astype(BF)

    def wcopy(src, dst, kind, k, slot, p):
        return pltpu.make_async_remote_copy(
            src_ref=src, dst_ref=dst, send_sem=getattr(r, kind + "_s").at[k], recv_sem=getattr(r, kind + "_r").at[slot],
            device_id={"wide": p}, device_id_type=MESH)

    psend, precv, zsend, zrecv, gat = r.psend, r.precv, r.zsend, r.zrecv, r.gat

    def grad_rows(row):
        return dot(xT[pl.ds(pl.multiple_of(row, Ck), Ck), :], dpre[...])

    def pair_send(step, carry):
        ap = lax.rem(a + 1 + step, A)
        psend[ap] = grad_rows((1 - b) * half + ap * Ck).astype(BF)
        wcopy(psend.at[ap], precv.at[ap], "p", ap, ap, pair).start()
        return carry

    lax.fori_loop(0, A, pair_send, 0)

    def z_sum(ap):
        v = grad_rows(b * half + ap * Ck)
        wcopy(psend.at[ap], precv.at[ap], "p", ap, ap, pair).wait_recv()
        return v + precv[ap].astype(F32)

    def z_send(step, carry):
        ap = lax.rem(a + 1 + step, A)
        zsend[ap] = z_sum(ap).astype(BF)
        wcopy(zsend.at[ap], zrecv.at[a], "z", ap, a, 2 * ap + b).start()
        return carry

    agt = -dot(grt, r.amat[...], precision=HIGH)
    for n in range(N):
        r.ags[n] = agt[:, n * R : (n + 1) * R]
    ex.agr.scatter(r.ags, r.agr)
    r.agr[ni] = r.ags[ni]
    r.gp[...] = dot(grt, r.pwt[...], TN, HIGH)
    dz = r.sz[...] * r.gp[own_b, :]
    ex.ur.wait(r.ur)
    r.ur[wi] = r.us[wi]
    uown = jnp.sum(r.ur[...], axis=0)
    r.uz[wi] = jnp.concatenate([uown, dz], axis=0).astype(BF)
    ex.uz.gather(r.uz)

    lax.fori_loop(0, 1, z_send, 0)

    ex.hgw.wait(r.hgw)
    ex.bfw.wait(r.bfw)
    ex.uz.wait(r.uz)
    uz, hg = r.uz[...].astype(F32), r.hgw[...].astype(F32)
    r.uzn[ni] = jnp.concatenate(
        [uz[:, :Bg].reshape(B, Hn), uz[:, Bg:].reshape(B, Mn), hg[:, :Bg].reshape(B, Hn)], axis=1).astype(BF)
    ex.uzn.gather(r.uzn)

    lax.fori_loop(1, min(2, A - 1), z_send, 0)

    ex.uzn.wait(r.uzn)
    acc = jnp.zeros((B, Fn), F32)
    for n in range(N):
        acc = acc + dot(r.uzn[n, :, :Hn], w2b[n * Hn : (n + 1) * Hn, :])
        acc = acc + dot(r.uzn[n, :, Hn : Hn + Mn], om[:, n * Mn : (n + 1) * Mn], NT)
    bfw = r.bfw[...].astype(F32)
    bfall = jnp.concatenate([bfw[:, :Bg].reshape(B, Fn // 2), bfw[:, Bg:].reshape(B, Fn // 2)], axis=1)
    r.db[...] = jnp.concatenate([acc, bfall], axis=0).astype(BF)
    for n in range(N):
        r.dhs[n] = dot(r.db[:B, :], w2b[n * Hn : (n + 1) * Hn, :], NT).astype(BF)
    ex.dhr.scatter(r.dhs, r.dhr)
    r.dhr[ni] = r.dhs[ni]

    lax.fori_loop(min(2, A - 1), A - 1, z_send, 0)
    own_row = b * half + a * Ck
    fin = z_sum(a)

    ex.agr.wait(r.agr)
    agt = jnp.sum(r.agr[...], axis=0)
    r.agrad[...] = agt
    ex.dhr.wait(r.dhr)
    dhb = jnp.sum(r.dhr[...].astype(F32), axis=0)
    dpre_b = (dhb * hg[:, Bg:].reshape(B, Hn)).astype(BF)
    fin = fin + dot(r.xbt[pl.ds(pl.multiple_of(own_row, Ck), Ck), :], dpre_b)

    def z_gain(k, total_rows):
        ap = lax.rem(a + k, A)
        wcopy(zsend.at[ap], zrecv.at[ap], "z", ap, ap, 2 * ap + b).wait_recv()
        return total_rows + zrecv[ap].astype(F32)

    fin = lax.fori_loop(1, A, z_gain, fin)
    mine = b * A + a
    gat[mine] = fin.astype(BF)

    def fcopy(slot, k):
        return wcopy(gat.at[slot], gat.at[slot], "f", k, k, pair)

    fcopy(mine, a).start()

    def g_send(k, carry):
        ap = lax.rem(a + k, A)
        wcopy(gat.at[mine], gat.at[mine], "g", ap, a, 2 * ap + b).start()
        return carry

    lax.fori_loop(1, A, g_send, 0)

    def two(v):
        return jnp.sum(jnp.sum(v * v, axis=1, keepdims=True), axis=0, keepdims=True)

    square = jnp.zeros((1, 1), F32)
    for n in range(N):
        hu = jnp.concatenate([r.uzn[n, :, Hn + Mn :], r.uzn[n, :, :Hn]], axis=0)
        g2 = dot(hu, r.db[...], TN)
        r.w2f[n * Hn : (n + 1) * Hn, :] = g2
        square = square + two(g2)
    g2_out = pltpu.make_async_copy(r.w2f, r.g2, lsem.at[2])
    g2_out.start()
    square = square * (1.0 / W) + two(fin) + two(agt)
    r.nn[ni] = jnp.broadcast_to(square, (8, 128))
    ex.nn.gather(r.nn)

    def g_pass(k, carry):
        ap = lax.rem(a + k, A)
        wcopy(gat.at[b * A + ap], gat.at[b * A + ap], "g", ap, ap, 2 * ap + b).wait_recv()
        fcopy(b * A + ap, ap).start()
        return carry

    lax.fori_loop(1, min(2, A), g_pass, 0)
    ex.nn.wait(r.nn)
    r.nw[wi] = jnp.sum(r.nn[...], axis=0)
    ex.nw.gather(r.nw)
    lax.fori_loop(min(2, A), A, g_pass, 0)
    ex.nw.wait(r.nw)
    norm = jnp.sum(r.nw[...], axis=0)
    lanes = lax.broadcasted_iota(jnp.int32, (8, 128), 1)
    r.scal[...] = jnp.where(lanes == 0, loss, jnp.where(lanes == 1, total, norm))

    def g_last(k, carry):
        slot = (1 - b) * A + k
        wcopy(gat.at[slot], gat.at[slot], "f", k, k, pair).wait_recv()
        return carry

    lax.fori_loop(0, A, g_last, 0)
    g1_out = pltpu.make_async_copy(gat, r.g1, lsem.at[0])
    g1_out.start()

    for name in WIDE_EX:
        vars(ex)[name].drain(getattr(r, name))
    for name in NARROW_EX:
        vars(ex)[name].drain(getattr(r, name))
    xcopy(r.data_x, xg.at[ni], 0, n1).wait_send()
    xcopy(r.data_x, xg.at[ni], 1, n2).wait_send()
    xcopy(xg.at[n2], xg.at[n2], 2, n1).wait_send()

    def left(k, carry):
        wcopy(psend.at[k], precv.at[k], "p", k, k, pair).wait_send()
        fcopy(b * A + k, k).wait_send()
        return carry

    def left_z(k, carry):
        ap = lax.rem(a + k, A)
        wcopy(zsend.at[ap], zrecv.at[a], "z", ap, a, 2 * ap + b).wait_send()
        wcopy(gat.at[mine], gat.at[mine], "g", ap, a, 2 * ap + b).wait_send()
        return carry

    lax.fori_loop(0, A, left, 0)
    lax.fori_loop(1, A, left_z, 0)
    g2_out.wait()
    g1_out.wait()


def on_device(
    data_x, data_group, batch_x, batch_group, batch_index, prec_index, prec_table, targets,
    omega, phase, prior_w, w1_master, w1_moment, w1_second, w2_master, w2_moment, w2_second,
    alpha, alpha_moment, alpha_second,
):
    W, N = lax.axis_size("wide"), lax.axis_size("narrow")
    A = W // 2
    R, D = data_x.shape
    brow, Bg, S = batch_x.shape[0], targets.shape[0], targets.shape[1]
    F, M = omega.shape
    Hn, Fn, Mn, H = w1_master.shape[1], w2_master.shape[1], M // N, w2_master.shape[0]
    B, Ck = W * Bg, D // 2 // A
    hbm, vmem, smem = (pl.BlockSpec(memory_space=m) for m in (pl.ANY, pltpu.VMEM, pltpu.SMEM))
    args = dict(
        data_x=(data_x, hbm), dgroup=(data_group.reshape(1, R), vmem), batch_x=(batch_x, vmem),
        bgroup=(batch_group, smem), bindex=(batch_index, smem), pindex=(prec_index, smem),
        ptable=(prec_table, smem), targets=(targets, vmem), omega=(omega, hbm),
        phase=(phase.reshape(1, M), vmem), prior_wt=(prior_w.T, hbm), w1=(w1_master, hbm),
        w2=(w2_master, hbm), alphat_own=(alpha.T, vmem),
    )
    outs = dict(
        scal=((8, 128), F32, vmem), g1=((2 * A, Ck, Hn), BF, hbm), g2=((H, Fn), F32, hbm), agrad=((S, R), F32, vmem),
    )
    scratch = dict(
        xg=((N, R, D), BF), xT=((D, N * R), BF), hid=((N * R, Hn), BF), gd=((N * R, Hn), F32),
        dpre=((N * R, Hn), BF), pre=((R, Hn), F32), w1f=((D, Hn), F32), w1b=((D, Hn), BF),
        w2f=((H, Fn), F32), w2b=((H, Fn), BF), om=((Fn, M), BF), pwt=((S, Mn), F32),
        xbg=((Bg, D), F32), gzs=((N, Bg, Hn + Mn), F32), us=((W, Bg, Hn), F32), ags=((N, S, R), F32),
        dhs=((N, B, Hn), BF), cz=((B, Mn), F32), sz=((Bg, Mn), F32), prior=((S, B), F32), gp=((B, Mn), F32),
        metat=((128, B), F32), alphat=((S, N * R), F32), pmask=((B, N * R), F32), amat=((B, N * R), F32),
        gmat=((B, Hn), BF), xbt=((D, B), BF), db=((2 * B, Fn), BF),
        psend=((A, Ck, Hn), BF), precv=((A, Ck, Hn), BF), zsend=((A, Ck, Hn), BF), zrecv=((A, Ck, Hn), BF),
        gat=((2 * A, Ck, Hn), BF),
        meta=((W, Bg, 128), F32), xbw=((W, 2 * Bg, D // 2), BF), hgw=((W, 2 * Bg, Hn), BF),
        bfw=((W, 2 * Bg, Fn // 2), BF), gw=((W, 2 * Bg, Hn // 2), BF), kw=((W, S, B), F32),
        ur=((W, Bg, Hn), F32), uz=((W, 2 * Bg, Hn), BF), nw=((W, 8, 128), F32),
        xbn=((N, brow, D), F32), ad=((N, S + 8, R), F32), hbn=((N, Bg, Hn), F32), gzr=((N, Bg, Hn + Mn), F32),
        kn=((N, S, B), F32), agr=((N, S, R), F32), uzn=((N, B, 2 * Hn + Mn), BF), dhr=((N, B, Hn), BF),
        nn=((N, 8, 128), F32),
    )
    sems = [("lsem", 5), ("x_s", 3), ("x_r", 3)]
    sems += [(name + end, W) for name in WIDE_EX for end in ("_s", "_r")]
    sems += [(name + end, N) for name in NARROW_EX for end in ("_s", "_r")]
    sems += [(name + end, A) for name in ("p", "z", "g", "f") for end in ("_s", "_r")]
    names = [*args, *outs, *scratch] + [n for n, _ in sems]
    scal, g1, g2, agrad = pl.pallas_call(
        lambda *refs: step_kernel(W, N, names, *refs),
        out_shape=[jax.ShapeDtypeStruct(s, t) for s, t, _ in outs.values()],
        in_specs=[spec for _, spec in args.values()],
        out_specs=[spec for _, _, spec in outs.values()],
        scratch_shapes=[pltpu.VMEM(s, t) for s, t in scratch.values()] + [pltpu.SemaphoreType.DMA((k,)) for _, k in sems],
        compiler_params=pltpu.CompilerParams(collective_id=0, has_side_effects=True, vmem_limit_bytes=56 * 2**20),
        name="gradients",
    )(*[v for v, _ in args.values()])
    loss_sum, weight_total, norm_sq = scal[0, 0], scal[0, 1], scal[0, 2]
    clip = jnp.minimum(1.0, 0.1 / jnp.sqrt(norm_sq))
    w1_grad = g1.reshape(D, Hn).astype(F32)
    w1_mn, w1_sn, w1_new = adamw(w1_master, clip * w1_grad, w1_moment, w1_second, 0.03, 0.01)
    w2_mn, w2_sn, w2_new = adamw(w2_master, clip * g2, w2_moment, w2_second, 0.03, 0.01)
    al_mn, al_sn, al_new = adamw(alpha, clip * agrad.T, alpha_moment, alpha_second, 0.2, 0.0)
    return (
        loss_sum, weight_total, norm_sq,
        w1_mn, w1_sn, w1_new, w1_new.astype(BF),
        w2_mn, w2_sn, w2_new, w2_new.astype(BF),
        al_mn, al_sn, al_new,
    )


def solution(mesh):
    both = P(("wide", "narrow"))
    both2 = P(("wide", "narrow"), None)
    col = P(None, "narrow")
    return jax.shard_map(
        on_device,
        mesh=mesh,
        in_specs=(both2, both, both2, P("wide"), P("wide"), P("wide"), P(), P("wide", None), P(), P(), P())
        + (col,) * 6 + (both2,) * 3,
        out_specs=(P(), P(), P()) + (col,) * 8 + (both2,) * 3,
        check_vma=False,
    )
```

time: 388 us -> 116 us (0.30)
  the two profiles are of different devices: /device:TPU:0 before, /device:TPU:8 now
where the time goes in v2:
time: 116 us
  Pallas kernels  94.8 us (82%)
  other arithmetic  16.7 us (14%)
  local copies, waits for them, and re-layouts  2.7 us (2%)
  between operations  1.42 us (1%)
    pallas_call x1, Pallas kernels, on_device(): pl.pallas_call(lambda *refs: step_kernel(W, N, names, *refs), out_shape=[...  94.8 us
    convert_element_type x1, other arithmetic, on_device(): w2_new.astype(BF)  11.5 us
    convert_element_type x1, other arithmetic, on_device(): w1_new.astype(BF)  4.27 us

profile of v2, /device:TPU:8, one launch (start us, length us, event | category | flops | bytes accessed | tf_op | source)
XLA Modules:
  0.0 115.6 jit_solution(7911350051068123000)
XLA Ops:
  0.6 94.8 %gradients.1 = (f32[8,128]{1,0:T(8,128)}, bf16[8,128,512]{2,1,0:T(8,128)(2,1)}, f32[2048,512]{1,0:T(8,128)}, f32[16,256]{1,0:T(8,128)}) custom-call(bf16[256,1024]{1,0:T(8,128)(2,1)} %refs_0_.1, s32[1,256]{1,0:T(1,128)} %bitcast.24, bf16[2,1024]{1,0:T(2,128)(2,1)} %refs_2_.1, s32[8]{0:T(128)} %refs_3_.1, s32[8]{0:T(128)} %refs_4_.1, s32[8]{0:T(128)} %refs_5_.1, ...), custom_call_target="tpu_custom_call" | custom-call | tf_op jit(solution)/shard_map/gradients/pallas_call | solution.py:490
  95.4 1.4 %fusion.12 = (f32[1,1]{1,0:T(1,128)}, f32[1,1]{1,0:T(1,128)}, f32[1,1]{1,0:T(1,128)}) fusion(f32[8,128]{1,0:T(8,128)} %get-tuple-element.18), kind=kLoop, calls=%fused_computation.17 | loop fusion | bytes 24 | tf_op jit(solution)/shard_map/slice | solution.py:499
  97.5 0.0 copy-start.3
  97.5 0.0 copy-start.1
  97.5 0.0 copy-start.2
  97.5 11.5 %fusion.7 = (bf16[2048,512]{1,0:T(8,128)(2,1)}, f32[2048,512]{1,0:T(8,128)}, f32[2048,512]{1,0:T(8,128)}, f32[2048,512]{1,0:T(8,128)}) fusion(f32[2048,512]{1,0:T(8,128)} %refs_12_.1, f32[2048,512]{1,0:T(8,128)} %get-tuple-element.20, f32[]{:T(128)S(6)} %min_shard_map.3, f32[2048,512]{1,0:T(8,128)} %param.36, f32[2048,512]{1,0:T(8,128)} %param.35), kind=kLoop, calls=%fused_computation.15 | loop fusion | flops 17825792 | bytes 31457284 | tf_op jit(solution)/shard_map/convert_element_type | solution.py:508
  109.0 0.0 copy-start
  109.0 0.0 copy-done.3
  109.0 0.3 convert_multiply_fusion
  109.3 0.0 copy-done.1
  109.3 0.0 copy-done.2
  109.4 1.3 %copy-done = f32[1024,512]{1,0:T(8,128)S(1)} copy-done((f32[1024,512]{1,0:T(8,128)S(1)}, f32[1024,512]{1,0:T(8,128)}, u32[]{:S(2)}) %copy-start) | copy-done | bytes 2097176
  110.6 0.0 copy-start.4
  110.6 0.0 copy-start.5
  110.6 0.0 copy-start.6
  110.6 0.0 copy-start.7
  110.6 4.3 %fusion.9 = (bf16[1024,512]{1,0:T(8,128)(2,1)}, f32[1024,512]{1,0:T(8,128)}, f32[1024,512]{1,0:T(8,128)}, f32[1024,512]{1,0:T(8,128)}) fusion(f32[1024,512]{1,0:T(8,128)S(1)} %copy-done, f32[8,128,512]{2,1,0:T(8,128)S(1)} %convert_multiply_fusion, f32[1024,512]{1,0:T(8,128)S(1)} %copy-done.1, f32[1024,512]{1,0:T(8,128)S(1)} %copy-done.2), kind=kLoop, calls=%fused_computation.16 | loop fusion | flops 8388608 | bytes 15728640 | tf_op jit(solution)/shard_map/convert_element_type | solution.py:507
  114.9 0.0 copy-done.4
  114.9 0.0 copy-done.5
  114.9 0.0 copy-done.6
  114.9 0.0 copy-done.7
  114.9 0.6 multiply_subtract_fusion.2
Async XLA Ops:
  97.5 11.5 %copy-start.3 = (bf16[8,128,512]{2,1,0:T(8,128)(2,1)S(1)}, bf16[8,128,512]{2,1,0:T(8,128)(2,1)}, u32[]{:S(2)}) copy-start(bf16[8,128,512]{2,1,0:T(8,128)(2,1)} %get-tuple-element.19) | copy-start | bytes 3145732
  97.5 11.8 %copy-start.1 = (f32[1024,512]{1,0:T(8,128)S(1)}, f32[1024,512]{1,0:T(8,128)}, u32[]{:S(2)}) copy-start(f32[1024,512]{1,0:T(8,128)} %param.33) | copy-start | bytes 6291460
  97.5 11.8 %copy-start.2 = (f32[1024,512]{1,0:T(8,128)S(1)}, f32[1024,512]{1,0:T(8,128)}, u32[]{:S(2)}) copy-start(f32[1024,512]{1,0:T(8,128)} %param.32) | copy-start | bytes 6291460
  109.0 1.6 %copy-start = (f32[1024,512]{1,0:T(8,128)S(1)}, f32[1024,512]{1,0:T(8,128)}, u32[]{:S(2)}) copy-start(f32[1024,512]{1,0:T(8,128)} %refs_11_.1) | copy-start | bytes 6291460
  110.6 4.3 %copy-start.4 = (f32[256,16]{0,1:T(8,128)S(1)}, f32[256,16]{0,1:T(8,128)}, u32[]{:S(2)}) copy-start(f32[256,16]{0,1:T(8,128)} %param.37) | copy-start | bytes 49156
  110.6 4.3 %copy-start.5 = (f32[256,16]{0,1:T(8,128)S(1)}, f32[256,16]{0,1:T(8,128)}, u32[]{:S(2)}) copy-start(f32[256,16]{0,1:T(8,128)} %param.39) | copy-start | bytes 49156
  110.6 4.3 %copy-start.6 = (f32[256,16]{0,1:T(8,128)S(1)}, f32[256,16]{0,1:T(8,128)}, u32[]{:S(2)}) copy-start(f32[256,16]{0,1:T(8,128)} %param.38) | copy-start | bytes 49156
  110.6 4.3 %copy-start.7 = (f32[16,256]{1,0:T(8,128)S(1)}, f32[16,256]{1,0:T(8,128)}, u32[]{:S(2)}) copy-start(f32[16,256]{1,0:T(8,128)} %get-tuple-element.21) | copy-start | bytes 49156

commit v3 on v2

--- a/solution.py
+++ b/solution.py
@@ -71,7 +71,7 @@
 
 
 WIDE_EX = ("meta", "xbw", "hgw", "bfw", "gw", "kw", "ur", "uz", "nw")
-NARROW_EX = ("xbn", "ad", "hbn", "gzr", "kn", "agr", "uzn", "dhr", "nn")
+NARROW_EX = ("xbn", "ad", "hbn", "gzr", "kn", "agr", "uzn", "hbx", "dhr", "nn")
 
 
 def step_kernel(W, N, names, *refs):
@@ -144,9 +144,26 @@
             src_ref=src, dst_ref=dst, send_sem=r.x_s.at[k], recv_sem=r.x_r.at[k],
             device_id={"narrow": p}, device_id_type=MESH)
 
+    cut = R * 5 // 16 // 16 * 16
+    cuts = (0, cut, 2 * cut, R)
+
+    def piece(k, src=None, slot=None):
+        rows = pl.ds(cuts[k], cuts[k + 1] - cuts[k])
+        slot = ni if slot is None else slot
+        src = xg.at[slot, rows] if src is None else src.at[rows]
+        return src, xg.at[slot, rows]
+
+    def x_side():
+        return xcopy(r.data_x, xg.at[ni], 0, n1)
+
+    def x_over(k):
+        return xcopy(*piece(k, r.data_x), 1 + k, n2)
+
+    def x_pass(k):
+        return xcopy(*piece(k, slot=n2), 4 + k, n1)
+
     ex.xbn.gather(r.xbn)
-    xcopy(r.data_x, xg.at[ni], 0, n1).start()
-    xcopy(r.data_x, xg.at[ni], 1, n2).start()
+    x_over(0).start()
     ex.meta.gather(r.meta)
     ex.ad.gather(r.ad)
 
@@ -166,6 +183,8 @@
     hb = hb.astype(BF).astype(F32)
     r.hbn[ni] = hb
     ex.hbn.gather(r.hbn)
+    x_over(1).start()
+    x_side().start()
     r.hgw[wi] = jnp.concatenate([hb, gb], axis=0).astype(BF)
     ex.hgw.gather(r.hgw)
     r.xbw[wi] = jnp.concatenate([xbg[:, : D // 2], xbg[:, D // 2 :]], axis=0).astype(BF)
@@ -206,6 +225,10 @@
         r.gzs[n, :, :Hn] = gpart[:, n * Hn : (n + 1) * Hn]
         r.gzs[n, :, Hn:] = zpart[:, n * Mn : (n + 1) * Mn]
     ex.gzr.scatter(r.gzs, r.gzr)
+    x_over(2).start()
+    for k in range(2):
+        xcopy(*piece(k, slot=n2), 1 + k, n2).wait_recv()
+        x_pass(k).start()
     r.gzr[ni] = r.gzs[ni]
     bf32 = bfeat.astype(F32)
     r.bfw[wi] = jnp.concatenate([bf32[:, : Fn // 2], bf32[:, Fn // 2 :]], axis=0).astype(BF)
@@ -226,9 +249,6 @@
 
     xcopy(r.data_x, xg.at[n1], 0, n1).wait_recv()
     block(n1)
-    xcopy(r.data_x, xg.at[n2], 1, n2).wait_recv()
-    xcopy(xg.at[n2], xg.at[n2], 2, n1).start()
-    block(n2)
     turn(ni)
     turn(n1)
     ex.meta.wait(r.meta)
@@ -243,7 +263,11 @@
     col = lax.broadcasted_iota(jnp.int32, (1, N * R), 1) + wi * (N * R)
     first = (ni == 0).astype(F32)
     r.amat[...] = jnp.where(meta[:, 1:2] == col.astype(F32), first / meta[:, 2:3], 0.0)
-    xcopy(r.data_x, xg.at[n3], 2, n1).wait_recv()
+    xcopy(*piece(2, slot=n2), 3, n2).wait_recv()
+    x_pass(2).start()
+    block(n2)
+    for k in range(3):
+        xcopy(*piece(k, slot=n3), 4 + k, n1).wait_recv()
     block(n3)
 
     ex.gw.wait(r.gw)
@@ -259,6 +283,11 @@
     ex.kn.wait(r.kn)
     r.kw[wi] = jnp.sum(r.kn[...], axis=0)
     ex.kw.gather(r.kw)
+    ex.hgw.wait(r.hgw)
+    hg = r.hgw[...].astype(F32)
+    r.hbx[ni] = hg[:, :Bg].reshape(B, Hn).astype(BF)
+    r.gb[...] = hg[:, Bg:].reshape(B, Hn)
+    ex.hbx.gather(r.hbx)
     ex.xbw.wait(r.xbw)
     xbw = r.xbw[...].astype(F32)
     r.xbt[...] = jnp.concatenate([xbw[:, :Bg].reshape(B, D // 2), xbw[:, Bg:].reshape(B, D // 2)], axis=1).T.astype(BF)
@@ -270,8 +299,7 @@
     grt = prec * resid / total
 
     ds = (-r.pmask[...] * dot(grt, r.alphat[...], TN, HIGH)).astype(BF)
-    upart = dot(ds, hid[...])
-    r.us[...] = upart.reshape(W, Bg, Hn)
+    r.us[...] = dot(ds, hid[...]).reshape(W, Bg, Hn)
     ex.ur.scatter(r.us, r.ur)
     for q in range(N):
         rows = slice(q * R, (q + 1) * R)
@@ -287,13 +315,17 @@
     def grad_rows(row):
         return dot(xT[pl.ds(pl.multiple_of(row, Ck), Ck), :], dpre[...])
 
-    def pair_send(step, carry):
-        ap = lax.rem(a + 1 + step, A)
+    def target(step):
+        off = lax.rem(A // 2 + step - 1, max(A - 1, 1)) + 1
+        return lax.rem(a + off + lax.rem(a, 2) * (A - 2 * off), A)
+
+    def pair_chunk(ap):
         psend[ap] = grad_rows((1 - b) * half + ap * Ck).astype(BF)
         wcopy(psend.at[ap], precv.at[ap], "p", ap, ap, pair).start()
-        return carry
-
-    lax.fori_loop(0, A, pair_send, 0)
+
+    def pair_send(step, carry):
+        pair_chunk(target(step))
+        return carry
 
     def z_sum(ap):
         v = grad_rows(b * half + ap * Ck)
@@ -301,10 +333,12 @@
         return v + precv[ap].astype(F32)
 
     def z_send(step, carry):
-        ap = lax.rem(a + 1 + step, A)
+        ap = target(step)
         zsend[ap] = z_sum(ap).astype(BF)
         wcopy(zsend.at[ap], zrecv.at[a], "z", ap, a, 2 * ap + b).start()
         return carry
+
+    lax.fori_loop(0, min(1, A - 1), pair_send, 0)
 
     agt = -dot(grt, r.amat[...], precision=HIGH)
     for n in range(N):
@@ -318,24 +352,25 @@
     uown = jnp.sum(r.ur[...], axis=0)
     r.uz[wi] = jnp.concatenate([uown, dz], axis=0).astype(BF)
     ex.uz.gather(r.uz)
-
-    lax.fori_loop(0, 1, z_send, 0)
-
-    ex.hgw.wait(r.hgw)
+    lax.fori_loop(min(1, A - 1), A - 1, pair_send, 0)
+    pair_chunk(a)
+
+    lax.fori_loop(0, min(1, A - 1), z_send, 0)
+
     ex.bfw.wait(r.bfw)
     ex.uz.wait(r.uz)
-    uz, hg = r.uz[...].astype(F32), r.hgw[...].astype(F32)
-    r.uzn[ni] = jnp.concatenate(
-        [uz[:, :Bg].reshape(B, Hn), uz[:, Bg:].reshape(B, Mn), hg[:, :Bg].reshape(B, Hn)], axis=1).astype(BF)
+    uz = r.uz[...].astype(F32)
+    r.uzn[ni] = jnp.concatenate([uz[:, :Bg].reshape(B, Hn), uz[:, Bg:].reshape(B, Mn)], axis=1).astype(BF)
     ex.uzn.gather(r.uzn)
 
-    lax.fori_loop(1, min(2, A - 1), z_send, 0)
+    lax.fori_loop(min(1, A - 1), A - 1, z_send, 0)
+    fin = z_sum(a)
 
     ex.uzn.wait(r.uzn)
     acc = jnp.zeros((B, Fn), F32)
     for n in range(N):
         acc = acc + dot(r.uzn[n, :, :Hn], w2b[n * Hn : (n + 1) * Hn, :])
-        acc = acc + dot(r.uzn[n, :, Hn : Hn + Mn], om[:, n * Mn : (n + 1) * Mn], NT)
+        acc = acc + dot(r.uzn[n, :, Hn:], om[:, n * Mn : (n + 1) * Mn], NT)
     bfw = r.bfw[...].astype(F32)
     bfall = jnp.concatenate([bfw[:, :Bg].reshape(B, Fn // 2), bfw[:, Bg:].reshape(B, Fn // 2)], axis=1)
     r.db[...] = jnp.concatenate([acc, bfall], axis=0).astype(BF)
@@ -344,18 +379,6 @@
     ex.dhr.scatter(r.dhs, r.dhr)
     r.dhr[ni] = r.dhs[ni]
 
-    lax.fori_loop(min(2, A - 1), A - 1, z_send, 0)
-    own_row = b * half + a * Ck
-    fin = z_sum(a)
-
-    ex.agr.wait(r.agr)
-    agt = jnp.sum(r.agr[...], axis=0)
-    r.agrad[...] = agt
-    ex.dhr.wait(r.dhr)
-    dhb = jnp.sum(r.dhr[...].astype(F32), axis=0)
-    dpre_b = (dhb * hg[:, Bg:].reshape(B, Hn)).astype(BF)
-    fin = fin + dot(r.xbt[pl.ds(pl.multiple_of(own_row, Ck), Ck), :], dpre_b)
-
     def z_gain(k, total_rows):
         ap = lax.rem(a + k, A)
         wcopy(zsend.at[ap], zrecv.at[ap], "z", ap, ap, 2 * ap + b).wait_recv()
@@ -365,75 +388,131 @@
     mine = b * A + a
     gat[mine] = fin.astype(BF)
 
-    def fcopy(slot, k):
-        return wcopy(gat.at[slot], gat.at[slot], "f", k, k, pair)
-
-    fcopy(mine, a).start()
-
-    def g_send(k, carry):
-        ap = lax.rem(a + k, A)
-        wcopy(gat.at[mine], gat.at[mine], "g", ap, a, 2 * ap + b).start()
-        return carry
-
-    lax.fori_loop(1, A, g_send, 0)
+    def fcopy(ap, side):
+        slot = side * A + ap
+        return wcopy(gat.at[slot], gat.at[slot], "f", ap, ap, pair)
+
+    def gcopy(ap, way):
+        slot = b * A + ap
+        k = ap if way > 0 else A + ap
+        return wcopy(gat.at[slot], gat.at[slot], "g", k, k, 2 * (a + way) + b)
+
+    fcopy(a, b).start()
+
+    @pl.when(a + 1 < A)
+    def _():
+        gcopy(a, 1).start()
+
+    @pl.when(a > 0)
+    def _():
+        gcopy(a, -1).start()
+
+    def g_pass(step, carry):
+        below, above = a - 1 - step, a + 1 + step
+
+        @pl.when(below >= 0)
+        def _():
+            gcopy(below, 1).wait_recv()
+
+            @pl.when(a + 1 < A)
+            def _():
+                gcopy(below, 1).start()
+
+            fcopy(below, b).start()
+
+        @pl.when(above < A)
+        def _():
+            gcopy(above, -1).wait_recv()
+
+            @pl.when(a > 0)
+            def _():
+                gcopy(above, -1).start()
+
+            fcopy(above, b).start()
+
+        return carry
 
     def two(v):
         return jnp.sum(jnp.sum(v * v, axis=1, keepdims=True), axis=0, keepdims=True)
 
     square = jnp.zeros((1, 1), F32)
     for n in range(N):
-        hu = jnp.concatenate([r.uzn[n, :, Hn + Mn :], r.uzn[n, :, :Hn]], axis=0)
+        if n == 0:
+            ex.hbx.wait(r.hbx)
+        hu = jnp.concatenate([r.hbx[n], r.uzn[n, :, :Hn]], axis=0)
         g2 = dot(hu, r.db[...], TN)
         r.w2f[n * Hn : (n + 1) * Hn, :] = g2
         square = square + two(g2)
     g2_out = pltpu.make_async_copy(r.w2f, r.g2, lsem.at[2])
     g2_out.start()
-    square = square * (1.0 / W) + two(fin) + two(agt)
+
+    ex.agr.wait(r.agr)
+    agt = jnp.sum(r.agr[...], axis=0)
+    r.agrad[...] = agt
+    ex.dhr.wait(r.dhr)
+    r.dpb[...] = (jnp.sum(r.dhr[...].astype(F32), axis=0) * r.gb[...]).astype(BF)
+
+    def batch_part(slot):
+        return dot(r.xbt[pl.ds(pl.multiple_of(slot * Ck, Ck), Ck), :], r.dpb[...])
+
+    square = square * (1.0 / W) + two(fin + batch_part(mine)) + two(agt)
     r.nn[ni] = jnp.broadcast_to(square, (8, 128))
     ex.nn.gather(r.nn)
-
-    def g_pass(k, carry):
-        ap = lax.rem(a + k, A)
-        wcopy(gat.at[b * A + ap], gat.at[b * A + ap], "g", ap, ap, 2 * ap + b).wait_recv()
-        fcopy(b * A + ap, ap).start()
-        return carry
-
-    lax.fori_loop(1, min(2, A), g_pass, 0)
+    lax.fori_loop(0, min(1, A - 1), g_pass, 0)
     ex.nn.wait(r.nn)
     r.nw[wi] = jnp.sum(r.nn[...], axis=0)
     ex.nw.gather(r.nw)
-    lax.fori_loop(min(2, A), A, g_pass, 0)
+    lax.fori_loop(min(1, A - 1), A - 1, g_pass, 0)
+
+    def finish(slot):
+        r.w1f[pl.ds(pl.multiple_of(slot * Ck, Ck), Ck), :] = gat[slot].astype(F32) + batch_part(slot)
+
+    def own_side(k, carry):
+        finish(b * A + k)
+        return carry
+
+    lax.fori_loop(0, A, own_side, 0)
     ex.nw.wait(r.nw)
     norm = jnp.sum(r.nw[...], axis=0)
     lanes = lax.broadcasted_iota(jnp.int32, (8, 128), 1)
     r.scal[...] = jnp.where(lanes == 0, loss, jnp.where(lanes == 1, total, norm))
 
     def g_last(k, carry):
-        slot = (1 - b) * A + k
-        wcopy(gat.at[slot], gat.at[slot], "f", k, k, pair).wait_recv()
+        ap = lax.rem(a + k, A)
+        fcopy(ap, 1 - b).wait_recv()
+        finish((1 - b) * A + ap)
         return carry
 
     lax.fori_loop(0, A, g_last, 0)
-    g1_out = pltpu.make_async_copy(gat, r.g1, lsem.at[0])
+    g1_out = pltpu.make_async_copy(r.w1f, r.g1, lsem.at[0])
     g1_out.start()
 
     for name in WIDE_EX:
         vars(ex)[name].drain(getattr(r, name))
     for name in NARROW_EX:
         vars(ex)[name].drain(getattr(r, name))
-    xcopy(r.data_x, xg.at[ni], 0, n1).wait_send()
-    xcopy(r.data_x, xg.at[ni], 1, n2).wait_send()
-    xcopy(xg.at[n2], xg.at[n2], 2, n1).wait_send()
+    x_side().wait_send()
+    for k in range(3):
+        x_over(k).wait_send()
+        x_pass(k).wait_send()
 
     def left(k, carry):
         wcopy(psend.at[k], precv.at[k], "p", k, k, pair).wait_send()
-        fcopy(b * A + k, k).wait_send()
+        fcopy(k, b).wait_send()
+
+        @pl.when((k <= a) & (a + 1 < A))
+        def _():
+            gcopy(k, 1).wait_send()
+
+        @pl.when((k >= a) & (a > 0))
+        def _():
+            gcopy(k, -1).wait_send()
+
         return carry
 
     def left_z(k, carry):
         ap = lax.rem(a + k, A)
         wcopy(zsend.at[ap], zrecv.at[a], "z", ap, a, 2 * ap + b).wait_send()
-        wcopy(gat.at[mine], gat.at[mine], "g", ap, a, 2 * ap + b).wait_send()
         return carry
 
     lax.fori_loop(0, A, left, 0)
@@ -463,7 +542,7 @@
         w2=(w2_master, hbm), alphat_own=(alpha.T, vmem),
     )
     outs = dict(
-        scal=((8, 128), F32, vmem), g1=((2 * A, Ck, Hn), BF, hbm), g2=((H, Fn), F32, hbm), agrad=((S, R), F32, vmem),
+        scal=((8, 128), F32, vmem), g1=((D, Hn), F32, hbm), g2=((H, Fn), F32, hbm), agrad=((S, R), F32, vmem),
     )
     scratch = dict(
         xg=((N, R, D), BF), xT=((D, N * R), BF), hid=((N * R, Hn), BF), gd=((N * R, Hn), F32),
@@ -474,18 +553,19 @@
         metat=((128, B), F32), alphat=((S, N * R), F32), pmask=((B, N * R), F32), amat=((B, N * R), F32),
         gmat=((B, Hn), BF), xbt=((D, B), BF), db=((2 * B, Fn), BF),
         psend=((A, Ck, Hn), BF), precv=((A, Ck, Hn), BF), zsend=((A, Ck, Hn), BF), zrecv=((A, Ck, Hn), BF),
-        gat=((2 * A, Ck, Hn), BF),
+        gat=((2 * A, Ck, Hn), BF), dpb=((B, Hn), BF), gb=((B, Hn), F32),
         meta=((W, Bg, 128), F32), xbw=((W, 2 * Bg, D // 2), BF), hgw=((W, 2 * Bg, Hn), BF),
         bfw=((W, 2 * Bg, Fn // 2), BF), gw=((W, 2 * Bg, Hn // 2), BF), kw=((W, S, B), F32),
         ur=((W, Bg, Hn), F32), uz=((W, 2 * Bg, Hn), BF), nw=((W, 8, 128), F32),
         xbn=((N, brow, D), F32), ad=((N, S + 8, R), F32), hbn=((N, Bg, Hn), F32), gzr=((N, Bg, Hn + Mn), F32),
-        kn=((N, S, B), F32), agr=((N, S, R), F32), uzn=((N, B, 2 * Hn + Mn), BF), dhr=((N, B, Hn), BF),
+        kn=((N, S, B), F32), agr=((N, S, R), F32), uzn=((N, B, Hn + Mn), BF), hbx=((N, B, Hn), BF), dhr=((N, B, Hn), BF),
         nn=((N, 8, 128), F32),
     )
-    sems = [("lsem", 5), ("x_s", 3), ("x_r", 3)]
+    sems = [("lsem", 5), ("x_s", 7), ("x_r", 7)]
     sems += [(name + end, W) for name in WIDE_EX for end in ("_s", "_r")]
     sems += [(name + end, N) for name in NARROW_EX for end in ("_s", "_r")]
-    sems += [(name + end, A) for name in ("p", "z", "g", "f") for end in ("_s", "_r")]
+    sems += [(name + end, A) for name in ("p", "z", "f") for end in ("_s", "_r")]
+    sems += [("g_s", 2 * A), ("g_r", 2 * A)]
     names = [*args, *outs, *scratch] + [n for n, _ in sems]
     scal, g1, g2, agrad = pl.pallas_call(
         lambda *refs: step_kernel(W, N, names, *refs),
@@ -498,8 +578,7 @@
     )(*[v for v, _ in args.values()])
     loss_sum, weight_total, norm_sq = scal[0, 0], scal[0, 1], scal[0, 2]
     clip = jnp.minimum(1.0, 0.1 / jnp.sqrt(norm_sq))
-    w1_grad = g1.reshape(D, Hn).astype(F32)
-    w1_mn, w1_sn, w1_new = adamw(w1_master, clip * w1_grad, w1_moment, w1_second, 0.03, 0.01)
+    w1_mn, w1_sn, w1_new = adamw(w1_master, clip * g1, w1_moment, w1_second, 0.03, 0.01)
     w2_mn, w2_sn, w2_new = adamw(w2_master, clip * g2, w2_moment, w2_second, 0.03, 0.01)
     al_mn, al_sn, al_new = adamw(alpha, clip * agrad.T, alpha_moment, alpha_second, 0.2, 0.0)
     return (

time: 116 us -> 98.2 us (0.85)
  the two profiles are of different devices: /device:TPU:8 before, /device:TPU:0 now
where the time goes in v3:
time: 98.2 us; the launch traced here: 97.9 us
  Pallas kernels  77 us (78%)
  other arithmetic  16.6 us (17%)
  local copies, waits for them, and re-layouts  2.91 us (3%)
  between operations  1.41 us (1%)
    pallas_call x1, Pallas kernels, on_device(): pl.pallas_call(lambda *refs: step_kernel(W, N, names, *refs), out_shape=[...  77 us
    convert_element_type x1, other arithmetic, on_device(): w2_new.astype(BF)  11.8 us
    convert_element_type x1, other arithmetic, on_device(): w1_new.astype(BF)  4.18 us

profile of v3, /device:TPU:0, one launch (start us, length us, event | category | flops | bytes accessed | tf_op | source)
XLA Modules:
  0.0 97.9 jit_solution(9318376814855899694)
XLA Ops:
  0.6 77.0 %gradients.1 = (f32[8,128]{1,0:T(8,128)}, f32[1024,512]{1,0:T(8,128)}, f32[2048,512]{1,0:T(8,128)}, f32[16,256]{1,0:T(8,128)}) custom-call(bf16[256,1024]{1,0:T(8,128)(2,1)} %refs_0_.1, s32[1,256]{1,0:T(1,128)} %bitcast.17, bf16[2,1024]{1,0:T(2,128)(2,1)} %refs_2_.1, s32[8]{0:T(128)} %refs_3_.1, s32[8]{0:T(128)} %refs_4_.1, s32[8]{0:T(128)} %refs_5_.1, ...), custom_call_target="tpu_custom_call" | custom-call | tf_op jit(solution)/shard_map/gradients/pallas_call | solution.py:570
  77.7 1.4 %fusion.10 = (f32[1,1]{1,0:T(1,128)}, f32[1,1]{1,0:T(1,128)}, f32[1,1]{1,0:T(1,128)}) fusion(f32[8,128]{1,0:T(8,128)} %get-tuple-element.18), kind=kLoop, calls=%fused_computation.15 | loop fusion | bytes 24 | tf_op jit(solution)/shard_map/slice | solution.py:579
  79.8 0.0 copy-start
  79.8 0.0 copy-start.1
  79.8 0.0 copy-start.2
  79.8 0.0 copy-start.3
  79.8 11.8 %fusion.6 = (bf16[2048,512]{1,0:T(8,128)(2,1)}, f32[2048,512]{1,0:T(8,128)}, f32[2048,512]{1,0:T(8,128)}, f32[2048,512]{1,0:T(8,128)}) fusion(f32[2048,512]{1,0:T(8,128)} %refs_12_.1, f32[2048,512]{1,0:T(8,128)} %get-tuple-element.20, f32[]{:T(128)S(6)} %min_shard_map.3, f32[2048,512]{1,0:T(8,128)} %param.36, f32[2048,512]{1,0:T(8,128)} %param.35), kind=kLoop, calls=%fused_computation.13 | loop fusion | flops 17825792 | bytes 31457284 | tf_op jit(solution)/shard_map/convert_element_type | solution.py:587
  91.6 0.0 copy-done
  91.6 0.0 copy-done.1
  91.6 0.7 copy-done.2
  92.3 0.8 copy-done.3
  93.1 0.0 copy-start.4
  93.1 0.0 copy-start.5
  93.1 0.0 copy-start.6
  93.1 0.0 copy-start.7
  93.1 4.2 %fusion.8 = (bf16[1024,512]{1,0:T(8,128)(2,1)}, f32[1024,512]{1,0:T(8,128)}, f32[1024,512]{1,0:T(8,128)}, f32[1024,512]{1,0:T(8,128)}) fusion(f32[1024,512]{1,0:T(8,128)S(1)} %copy-done, f32[1024,512]{1,0:T(8,128)S(1)} %copy-done.3, f32[]{:T(128)S(6)} %min_shard_map.3, f32[1024,512]{1,0:T(8,128)S(1)} %copy-done.1, f32[1024,512]{1,0:T(8,128)S(1)} %copy-done.2), kind=kLoop, calls=%fused_computation.14 | loop fusion | flops 8912896 | bytes 15728644 | tf_op jit(solution)/shard_map/convert_element_type | solution.py:586
  97.3 0.0 copy-done.4
  97.3 0.0 copy-done.5
  97.3 0.0 copy-done.6
  97.3 0.0 copy-done.7
  97.3 0.6 multiply_subtract_fusion.2
Async XLA Ops:
  79.8 11.8 %copy-start = (f32[1024,512]{1,0:T(8,128)S(1)}, f32[1024,512]{1,0:T(8,128)}, u32[]{:S(2)}) copy-start(f32[1024,512]{1,0:T(8,128)} %refs_11_.1) | copy-start | bytes 6291460
  79.8 11.8 %copy-start.1 = (f32[1024,512]{1,0:T(8,128)S(1)}, f32[1024,512]{1,0:T(8,128)}, u32[]{:S(2)}) copy-start(f32[1024,512]{1,0:T(8,128)} %param.33) | copy-start | bytes 6291460
  79.8 12.5 %copy-start.2 = (f32[1024,512]{1,0:T(8,128)S(1)}, f32[1024,512]{1,0:T(8,128)}, u32[]{:S(2)}) copy-start(f32[1024,512]{1,0:T(8,128)} %param.32) | copy-start | bytes 6291460
  79.8 13.3 %copy-start.3 = (f32[1024,512]{1,0:T(8,128)S(1)}, f32[1024,512]{1,0:T(8,128)}, u32[]{:S(2)}) copy-start(f32[1024,512]{1,0:T(8,128)} %get-tuple-element.19) | copy-start | bytes 6291460
  93.1 4.2 %copy-start.4 = (f32[256,16]{0,1:T(8,128)S(1)}, f32[256,16]{0,1:T(8,128)}, u32[]{:S(2)}) copy-start(f32[256,16]{0,1:T(8,128)} %param.37) | copy-start | bytes 49156
  93.1 4.2 %copy-start.5 = (f32[256,16]{0,1:T(8,128)S(1)}, f32[256,16]{0,1:T(8,128)}, u32[]{:S(2)}) copy-start(f32[256,16]{0,1:T(8,128)} %param.39) | copy-start | bytes 49156
  93.1 4.2 %copy-start.6 = (f32[256,16]{0,1:T(8,128)S(1)}, f32[256,16]{0,1:T(8,128)}, u32[]{:S(2)}) copy-start(f32[256,16]{0,1:T(8,128)} %param.38) | copy-start | bytes 49156
  93.1 4.2 %copy-start.7 = (f32[16,256]{1,0:T(8,128)S(1)}, f32[16,256]{1,0:T(8,128)}, u32[]{:S(2)}) copy-start(f32[16,256]{1,0:T(8,128)} %get-tuple-element.21) | copy-start | bytes 49156

commit v4 on v3

--- a/solution.py
+++ b/solution.py
@@ -16,15 +16,6 @@
 BF = jnp.bfloat16
 
 
-def adamw(weight, grad, moment, second, rate, decay):
-    moment_new = 0.9 * moment + 0.1 * grad
-    second_new = 0.999 * second + 0.001 * grad * grad
-    m_hat = moment_new / (1.0 - 0.9**STEP_NUM)
-    v_hat = second_new / (1.0 - 0.999**STEP_NUM)
-    new = weight - rate * (m_hat / (jnp.sqrt(v_hat) + 1e-08) + decay * weight)
-    return (moment_new, second_new, new)
-
-
 def gelu_pair(pre):
     square = pre * pre
     t = jnp.tanh(pre * (GC + (GC * 0.044715) * square))
@@ -74,7 +65,7 @@
 NARROW_EX = ("xbn", "ad", "hbn", "gzr", "kn", "agr", "uzn", "hbx", "dhr", "nn")
 
 
-def step_kernel(W, N, names, *refs):
+def step_kernel(W, N, resident, names, *refs):
     r = SimpleNamespace(**dict(zip(names, refs)))
     wi, ni = lax.axis_index("wide"), lax.axis_index("narrow")
     A = W // 2
@@ -226,6 +217,12 @@
         r.gzs[n, :, Hn:] = zpart[:, n * Mn : (n + 1) * Mn]
     ex.gzr.scatter(r.gzs, r.gzr)
     x_over(2).start()
+    later = []
+    if resident:
+        pairs = ((r.w1_m, r.m1), (r.w1_v, r.v1), (r.w2_m, r.m2), (r.w2_v, r.v2))
+        later = [pltpu.make_async_copy(src, dst, lsem.at[5 + k]) for k, (src, dst) in enumerate(pairs)]
+    for load in later:
+        load.start()
     for k in range(2):
         xcopy(*piece(k, slot=n2), 1 + k, n2).wait_recv()
         x_pass(k).start()
@@ -386,16 +383,21 @@
 
     fin = lax.fori_loop(1, A, z_gain, fin)
     mine = b * A + a
-    gat[mine] = fin.astype(BF)
+
+
+    def shard(slot):
+        return pl.ds(pl.multiple_of(slot * Ck, Ck), Ck)
+
+    gat[shard(mine), :] = fin.astype(BF)
 
     def fcopy(ap, side):
-        slot = side * A + ap
-        return wcopy(gat.at[slot], gat.at[slot], "f", ap, ap, pair)
+        rows = shard(side * A + ap)
+        return wcopy(gat.at[rows], gat.at[rows], "f", ap, ap, pair)
 
     def gcopy(ap, way):
-        slot = b * A + ap
+        rows = shard(b * A + ap)
         k = ap if way > 0 else A + ap
-        return wcopy(gat.at[slot], gat.at[slot], "g", k, k, 2 * (a + way) + b)
+        return wcopy(gat.at[rows], gat.at[rows], "g", k, k, 2 * (a + way) + b)
 
     fcopy(a, b).start()
 
@@ -441,10 +443,8 @@
             ex.hbx.wait(r.hbx)
         hu = jnp.concatenate([r.hbx[n], r.uzn[n, :, :Hn]], axis=0)
         g2 = dot(hu, r.db[...], TN)
-        r.w2f[n * Hn : (n + 1) * Hn, :] = g2
+        r.g2[n * Hn : (n + 1) * Hn, :] = g2
         square = square + two(g2)
-    g2_out = pltpu.make_async_copy(r.w2f, r.g2, lsem.at[2])
-    g2_out.start()
 
     ex.agr.wait(r.agr)
     agt = jnp.sum(r.agr[...], axis=0)
@@ -452,10 +452,7 @@
     ex.dhr.wait(r.dhr)
     r.dpb[...] = (jnp.sum(r.dhr[...].astype(F32), axis=0) * r.gb[...]).astype(BF)
 
-    def batch_part(slot):
-        return dot(r.xbt[pl.ds(pl.multiple_of(slot * Ck, Ck), Ck), :], r.dpb[...])
-
-    square = square * (1.0 / W) + two(fin + batch_part(mine)) + two(agt)
+    square = square * (1.0 / W) + two(fin + dot(r.xbt[shard(mine), :], r.dpb[...])) + two(agt)
     r.nn[ni] = jnp.broadcast_to(square, (8, 128))
     ex.nn.gather(r.nn)
     lax.fori_loop(0, min(1, A - 1), g_pass, 0)
@@ -464,14 +461,6 @@
     ex.nw.gather(r.nw)
     lax.fori_loop(min(1, A - 1), A - 1, g_pass, 0)
 
-    def finish(slot):
-        r.w1f[pl.ds(pl.multiple_of(slot * Ck, Ck), Ck), :] = gat[slot].astype(F32) + batch_part(slot)
-
-    def own_side(k, carry):
-        finish(b * A + k)
-        return carry
-
-    lax.fori_loop(0, A, own_side, 0)
     ex.nw.wait(r.nw)
     norm = jnp.sum(r.nw[...], axis=0)
     lanes = lax.broadcasted_iota(jnp.int32, (8, 128), 1)
@@ -480,12 +469,9 @@
     def g_last(k, carry):
         ap = lax.rem(a + k, A)
         fcopy(ap, 1 - b).wait_recv()
-        finish((1 - b) * A + ap)
         return carry
 
     lax.fori_loop(0, A, g_last, 0)
-    g1_out = pltpu.make_async_copy(r.w1f, r.g1, lsem.at[0])
-    g1_out.start()
 
     for name in WIDE_EX:
         vars(ex)[name].drain(getattr(r, name))
@@ -517,8 +503,98 @@
 
     lax.fori_loop(0, A, left, 0)
     lax.fori_loop(1, A, left_z, 0)
-    g2_out.wait()
-    g1_out.wait()
+    for load in later:
+        load.wait()
+
+
+CORR1 = 1.0 - 0.9**STEP_NUM
+CORR2 = 1.0 - 0.999**STEP_NUM
+
+
+def adamw(weight, grad, moment, second, rate, decay):
+    moment_new = 0.9 * moment + 0.1 * grad
+    second_new = 0.999 * second + 0.001 * grad * grad
+    step = moment_new / (jnp.sqrt(second_new) * (1.0 / math.sqrt(CORR2)) + 1e-08)
+    new = weight * (1.0 - rate * decay) - (rate / CORR1) * step
+    return moment_new, second_new, new
+
+
+def update_kernel(resident, slots, C, names, *refs):
+    r = SimpleNamespace(**dict(zip(names, refs)))
+    if not resident:
+        pairs = ((r.w1, r.w1f), (r.w1_m, r.m1), (r.w1_v, r.v1), (r.w2, r.w2f), (r.w2_m, r.m2), (r.w2_v, r.v2))
+        loads = [pltpu.make_async_copy(src, dst, r.lsem.at[k]) for k, (src, dst) in enumerate(pairs)]
+        for load in loads:
+            load.start()
+        for load in loads:
+            load.wait()
+    small = [pltpu.make_async_copy(src, r.asl.at[k], r.asem.at[k]) for k, src in enumerate((r.at, r.atm, r.atv))]
+    for load in small:
+        load.start()
+    norm = r.scal[0:1, 2:3]
+    clip = jnp.minimum(1.0, 0.1 / jnp.sqrt(norm))
+    ring = (r.sm, r.sv, r.sn, r.sc)
+
+    def copies(outs, slot, rows):
+        return [pltpu.make_async_copy(buf.at[slot], out.at[rows], r.osem.at[slot, k]) for k, (buf, out) in enumerate(zip(ring, outs))]
+
+    def chunk(grad, state, outs, k, ahead):
+        w, m, v = state
+        slot = lax.rem(k + ahead, slots)
+        base = pl.multiple_of(k * C, C)
+        rows = pl.ds(base, C)
+
+        def drain():
+            for copy in copies(outs, slot, rows):
+                copy.wait()
+
+        if ahead:
+            drain()
+        else:
+            pl.when(k >= slots)(drain)
+
+        def part(j, carry):
+            src = pl.ds(pl.multiple_of(base + j * 16, 16), 16)
+            dst = pl.ds(pl.multiple_of(j * 16, 16), 16)
+            mn, vn, wn = adamw(w[src, :], clip * grad[src, :], m[src, :], v[src, :], 0.03, 0.01)
+            r.sm[slot, dst, :] = mn
+            r.sv[slot, dst, :] = vn
+            r.sn[slot, dst, :] = wn
+            r.sc[slot, dst, :] = wn.astype(BF)
+            return carry
+
+        lax.fori_loop(0, C // 16, part, 0, unroll=True)
+        for copy in copies(outs, slot, rows):
+            copy.start()
+
+    outs1 = (r.m1o, r.v1o, r.n1o, r.c1o)
+    outs2 = (r.m2o, r.v2o, r.n2o, r.c2o)
+    count1, count2 = r.w1f.shape[0] // C, r.w2f.shape[0] // C
+
+    def step2(k, carry):
+        chunk(r.g2, (r.w2f, r.m2, r.v2), outs2, k, 0)
+        return carry
+
+    def step1(k, carry):
+        chunk(r.gs, (r.w1f, r.m1, r.v1), outs1, k, count2)
+        return carry
+
+    lax.fori_loop(0, count2, step2, 0)
+    r.gs[...] = r.gat[...].astype(F32) + dot(r.xbt[...], r.dpb[...])
+    lax.fori_loop(0, count1, step1, 0)
+    for load in small:
+        load.wait()
+    am, av, an = adamw(r.asl[0], clip * r.agrad[...], r.asl[1], r.asl[2], 0.2, 0.0)
+    for k, v in enumerate((am, av, an)):
+        r.ast[k] = v
+    last = [pltpu.make_async_copy(r.ast.at[k], dst, r.asem.at[k]) for k, dst in enumerate((r.amo, r.avo, r.ano))]
+    for copy in last:
+        copy.start()
+    for k in range(slots):
+        for copy in copies(outs1, k, pl.ds(0, C)):
+            copy.wait()
+    for copy in last:
+        copy.wait()
 
 
 def on_device(
@@ -534,6 +610,7 @@
     Hn, Fn, Mn, H = w1_master.shape[1], w2_master.shape[1], M // N, w2_master.shape[0]
     B, Ck = W * Bg, D // 2 // A
     hbm, vmem, smem = (pl.BlockSpec(memory_space=m) for m in (pl.ANY, pltpu.VMEM, pltpu.SMEM))
+    resident = B <= 128
     args = dict(
         data_x=(data_x, hbm), dgroup=(data_group.reshape(1, R), vmem), batch_x=(batch_x, vmem),
         bgroup=(batch_group, smem), bindex=(batch_index, smem), pindex=(prec_index, smem),
@@ -541,19 +618,27 @@
         phase=(phase.reshape(1, M), vmem), prior_wt=(prior_w.T, hbm), w1=(w1_master, hbm),
         w2=(w2_master, hbm), alphat_own=(alpha.T, vmem),
     )
+    state = dict(
+        w1=(w1_master, hbm), w1_m=(w1_moment, hbm), w1_v=(w1_second, hbm),
+        w2=(w2_master, hbm), w2_m=(w2_moment, hbm), w2_v=(w2_second, hbm),
+    )
     outs = dict(
-        scal=((8, 128), F32, vmem), g1=((D, Hn), F32, hbm), g2=((H, Fn), F32, hbm), agrad=((S, R), F32, vmem),
+        scal=((8, 128), F32), agrad=((S, R), F32), gat=((D, Hn), BF), xbt=((D, B), BF), dpb=((B, Hn), BF),
+        g2=((H, Fn), F32),
+    )
+    held = dict(
+        w1f=((D, Hn), F32), m1=((D, Hn), F32), v1=((D, Hn), F32), w2f=((H, Fn), F32), m2=((H, Fn), F32), v2=((H, Fn), F32),
     )
     scratch = dict(
         xg=((N, R, D), BF), xT=((D, N * R), BF), hid=((N * R, Hn), BF), gd=((N * R, Hn), F32),
-        dpre=((N * R, Hn), BF), pre=((R, Hn), F32), w1f=((D, Hn), F32), w1b=((D, Hn), BF),
-        w2f=((H, Fn), F32), w2b=((H, Fn), BF), om=((Fn, M), BF), pwt=((S, Mn), F32),
+        dpre=((N * R, Hn), BF), pre=((R, Hn), F32), w1b=((D, Hn), BF),
+        w2b=((H, Fn), BF), om=((Fn, M), BF), pwt=((S, Mn), F32),
         xbg=((Bg, D), F32), gzs=((N, Bg, Hn + Mn), F32), us=((W, Bg, Hn), F32), ags=((N, S, R), F32),
         dhs=((N, B, Hn), BF), cz=((B, Mn), F32), sz=((Bg, Mn), F32), prior=((S, B), F32), gp=((B, Mn), F32),
         metat=((128, B), F32), alphat=((S, N * R), F32), pmask=((B, N * R), F32), amat=((B, N * R), F32),
-        gmat=((B, Hn), BF), xbt=((D, B), BF), db=((2 * B, Fn), BF),
+        gmat=((B, Hn), BF), db=((2 * B, Fn), BF),
         psend=((A, Ck, Hn), BF), precv=((A, Ck, Hn), BF), zsend=((A, Ck, Hn), BF), zrecv=((A, Ck, Hn), BF),
-        gat=((2 * A, Ck, Hn), BF), dpb=((B, Hn), BF), gb=((B, Hn), F32),
+        gb=((B, Hn), F32),
         meta=((W, Bg, 128), F32), xbw=((W, 2 * Bg, D // 2), BF), hgw=((W, 2 * Bg, Hn), BF),
         bfw=((W, 2 * Bg, Fn // 2), BF), gw=((W, 2 * Bg, Hn // 2), BF), kw=((W, S, B), F32),
         ur=((W, Bg, Hn), F32), uz=((W, 2 * Bg, Hn), BF), nw=((W, 8, 128), F32),
@@ -561,31 +646,59 @@
         kn=((N, S, B), F32), agr=((N, S, R), F32), uzn=((N, B, Hn + Mn), BF), hbx=((N, B, Hn), BF), dhr=((N, B, Hn), BF),
         nn=((N, 8, 128), F32),
     )
-    sems = [("lsem", 5), ("x_s", 7), ("x_r", 7)]
+    if resident:
+        args.update(state)
+        outs.update(held)
+    else:
+        scratch.update(w1f=held["w1f"], w2f=held["w2f"])
+    sems = [("lsem", 9), ("x_s", 7), ("x_r", 7)]
     sems += [(name + end, W) for name in WIDE_EX for end in ("_s", "_r")]
     sems += [(name + end, N) for name in NARROW_EX for end in ("_s", "_r")]
     sems += [(name + end, A) for name in ("p", "z", "f") for end in ("_s", "_r")]
     sems += [("g_s", 2 * A), ("g_r", 2 * A)]
     names = [*args, *outs, *scratch] + [n for n, _ in sems]
-    scal, g1, g2, agrad = pl.pallas_call(
-        lambda *refs: step_kernel(W, N, names, *refs),
-        out_shape=[jax.ShapeDtypeStruct(s, t) for s, t, _ in outs.values()],
+    grads = pl.pallas_call(
+        lambda *refs: step_kernel(W, N, resident, names, *refs),
+        out_shape=[(pltpu.VMEM if resident else jax.ShapeDtypeStruct)(s, t) for s, t in outs.values()],
         in_specs=[spec for _, spec in args.values()],
-        out_specs=[spec for _, _, spec in outs.values()],
+        out_specs=[vmem] * len(outs),
         scratch_shapes=[pltpu.VMEM(s, t) for s, t in scratch.values()] + [pltpu.SemaphoreType.DMA((k,)) for _, k in sems],
-        compiler_params=pltpu.CompilerParams(collective_id=0, has_side_effects=True, vmem_limit_bytes=56 * 2**20),
+        compiler_params=pltpu.CompilerParams(collective_id=0, has_side_effects=True, vmem_limit_bytes=(60 if not resident else 39) * 2**20),
         name="gradients",
     )(*[v for v, _ in args.values()])
-    loss_sum, weight_total, norm_sq = scal[0, 0], scal[0, 1], scal[0, 2]
-    clip = jnp.minimum(1.0, 0.1 / jnp.sqrt(norm_sq))
-    w1_mn, w1_sn, w1_new = adamw(w1_master, clip * g1, w1_moment, w1_second, 0.03, 0.01)
-    w2_mn, w2_sn, w2_new = adamw(w2_master, clip * g2, w2_moment, w2_second, 0.03, 0.01)
-    al_mn, al_sn, al_new = adamw(alpha, clip * agrad.T, alpha_moment, alpha_second, 0.2, 0.0)
+
+    args2 = {k: (v, vmem) for k, v in zip(outs, grads)}
+    args2.update(at=(alpha.T, hbm), atm=(alpha_moment.T, hbm), atv=(alpha_second.T, hbm))
+    C, slots = 256, 3
+    outs2 = dict(amo=((S, R), F32, hbm), avo=((S, R), F32, hbm), ano=((S, R), F32, hbm))
+    for k, shape in (("1", (D, Hn)), ("2", (H, Fn))):
+        outs2.update({"m" + k + "o": (shape, F32, hbm), "v" + k + "o": (shape, F32, hbm)})
+        outs2.update({"n" + k + "o": (shape, F32, hbm), "c" + k + "o": (shape, BF, hbm)})
+    scratch2 = dict(
+        gs=pltpu.VMEM((D, Hn), F32), sm=pltpu.VMEM((slots, C, Hn), F32), sv=pltpu.VMEM((slots, C, Hn), F32),
+        sn=pltpu.VMEM((slots, C, Hn), F32), sc=pltpu.VMEM((slots, C, Hn), BF), osem=pltpu.SemaphoreType.DMA((slots, 4)),
+        asl=pltpu.VMEM((3, S, R), F32), ast=pltpu.VMEM((3, S, R), F32), asem=pltpu.SemaphoreType.DMA((3,)),
+    )
+    if not resident:
+        args2.update(state)
+        scratch2.update({k: pltpu.VMEM(s, t) for k, (s, t) in held.items()}, lsem=pltpu.SemaphoreType.DMA((6,)))
+    names2 = [*args2, *outs2, *scratch2]
+    new = pl.pallas_call(
+        lambda *refs: update_kernel(resident, slots, C, names2, *refs),
+        out_shape=[jax.ShapeDtypeStruct(s, t) for s, t, _ in outs2.values()],
+        in_specs=[spec for _, spec in args2.values()],
+        out_specs=[spec for _, _, spec in outs2.values()],
+        scratch_shapes=list(scratch2.values()),
+        compiler_params=pltpu.CompilerParams(vmem_limit_bytes=(36 if not resident else 10) * 2**20),
+        name="adamw",
+    )(*[v for v, _ in args2.values()])
+    new = dict(zip(outs2, new))
+    scal = grads[0]
     return (
-        loss_sum, weight_total, norm_sq,
-        w1_mn, w1_sn, w1_new, w1_new.astype(BF),
-        w2_mn, w2_sn, w2_new, w2_new.astype(BF),
-        al_mn, al_sn, al_new,
+        scal[0, 0], scal[0, 1], scal[0, 2],
+        new["m1o"], new["v1o"], new["n1o"], new["c1o"],
+        new["m2o"], new["v2o"], new["n2o"], new["c2o"],
+        new["amo"].T, new["avo"].T, new["ano"].T,
     )
 
 

time: 98.2 us -> 86.1 us (0.88)
  other arithmetic: 16.6 us -> 0 us
  Pallas kernels: 77 us -> 84.6 us
  local copies, waits for them, and re-layouts: 2.91 us -> 0.6 us
    convert_element_type x2 -> x0, other arithmetic: 15.9 us -> none  [the longest x1 11.8 us: on_device(): w2_new.astype(BF)]
    pallas_call x1 -> x2, Pallas kernels: 77 us -> 84.6 us  [the longest x1 76.2 us: on_device(): pl.pallas_call(lambda *refs: step_kernel(W, N, resident, names, *refs), o...]
    unnamed x16 -> x6, local copies, waits for them, and re-layouts: 1.53 us -> 0.01 us
where the time goes in v4:
time: 86.1 us; the launch traced here: 85.9 us
  Pallas kernels  84.6 us (98%)
    pallas_call x1, Pallas kernels, on_device(): pl.pallas_call(lambda *refs: step_kernel(W, N, resident, names, *refs), o...  76.2 us
    pallas_call x1, Pallas kernels, on_device(): pl.pallas_call(lambda *refs: update_kernel(resident, slots, C, names2, *r...  8.41 us

profile of v4, /device:TPU:0, one launch (start us, length us, event | category | flops | bytes accessed | tf_op | source)
XLA Modules:
  0.0 85.9 jit_solution(15572393418623329723)
XLA Ops:
  0.7 0.0 copy-start
  0.7 0.0 copy-start.1
  0.7 0.0 copy-start.2
  0.7 76.2 %gradients.1 = (f32[8,128]{1,0:T(8,128)S(1)}, f32[16,256]{1,0:T(8,128)S(1)}, bf16[1024,512]{1,0:T(8,128)(2,1)S(1)}, bf16[1024,64]{1,0:T(8,128)(2,1)S(1)}, bf16[6...) custom-call(bf16[256,1024]{1,0:T(8,128)(2,1)} %refs_0_.1, ...), custom_call_target="tpu_custom_call" | custom-call | tf_op jit(solution)/shard_map/gradients/pallas_call | solution.py:660
  76.9 0.0 copy-done
  76.9 0.0 copy-done.1
  76.9 0.0 copy-done.2
  76.9 8.4 %adamw.1 = (f32[16,256]{1,0:T(8,128)}, f32[16,256]{1,0:T(8,128)}, f32[16,256]{1,0:T(8,128)}, f32[1024,512]{1,0:T(8,128)}, f32[1024,512]{1,0:T(8,128)}, /*index=5...) custom-call(f32[8,128]{1,0:T(8,128)S(1)} %get-tuple-element.37.refs_, ...), custom_call_target="tpu_custom_call" | custom-call | tf_op jit(solution)/shard_map/adamw/pallas_call | solution.py:686
  85.3 0.6 fusion
Async XLA Ops:
  0.7 76.2 %copy-start = (f32[256,16]{0,1:T(8,128)S(1)}, f32[256,16]{0,1:T(8,128)}, u32[]{:S(2)}) copy-start(f32[256,16]{0,1:T(8,128)} %param.37) | copy-start | bytes 49156
  0.7 76.2 %copy-start.1 = (f32[256,16]{0,1:T(8,128)S(1)}, f32[256,16]{0,1:T(8,128)}, u32[]{:S(2)}) copy-start(f32[256,16]{0,1:T(8,128)} %param.38) | copy-start | bytes 49156
  0.7 76.2 %copy-start.2 = (f32[256,16]{0,1:T(8,128)S(1)}, f32[256,16]{0,1:T(8,128)}, u32[]{:S(2)}) copy-start(f32[256,16]{0,1:T(8,128)} %param.39) | copy-start | bytes 49156

commit v5 on v4

--- a/solution.py
+++ b/solution.py
@@ -33,13 +33,13 @@
 
 
 class Exchange:
-    def __init__(self, axis, size, me, send, recv):
-        self.axis, self.size, self.me, self.send, self.recv = axis, size, me, send, recv
-
-    def copy(self, src, dst, p, slot):
+    def __init__(self, size, me, where, sems, k):
+        self.size, self.me, self.where, self.sems, self.k = size, me, where, sems, k
+
+    def copy(self, src, dst, p):
         return pltpu.make_async_remote_copy(
-            src_ref=src, dst_ref=dst, send_sem=self.send.at[p], recv_sem=self.recv.at[slot],
-            device_id={self.axis: p}, device_id_type=MESH)
+            src_ref=src, dst_ref=dst, send_sem=self.sems.at[self.k], recv_sem=self.sems.at[self.k + 1],
+            device_id=self.where(p), device_id_type=MESH)
 
     def loop(self, body):
         def step(k, carry):
@@ -48,21 +48,29 @@
 
         lax.fori_loop(1, self.size, step, 0)
 
+    def greet(self, barrier):
+        self.loop(lambda p: pl.semaphore_signal(barrier, inc=1, device_id=self.where(p), device_id_type=MESH))
+
     def gather(self, buf):
-        self.loop(lambda p: self.copy(buf.at[self.me], buf.at[self.me], p, self.me).start())
+        self.loop(lambda p: self.copy(buf.at[self.me], buf.at[self.me], p).start())
 
     def scatter(self, src, buf):
-        self.loop(lambda p: self.copy(src.at[p], buf.at[self.me], p, self.me).start())
+        self.loop(lambda p: self.copy(src.at[p], buf.at[self.me], p).start())
+
+    def all(self, buf):
+        others = buf.at[pl.ds(0, self.size - 1)]
+        return self.copy(others, others, lax.rem(self.me + 1, self.size))
 
     def wait(self, buf):
-        self.loop(lambda p: self.copy(buf.at[p], buf.at[p], p, p).wait_recv())
+        self.all(buf).wait_recv()
 
     def drain(self, buf):
-        self.loop(lambda p: self.copy(buf.at[p], buf.at[p], p, p).wait_send())
-
-
-WIDE_EX = ("meta", "xbw", "hgw", "bfw", "gw", "kw", "ur", "uz", "nw")
-NARROW_EX = ("xbn", "ad", "hbn", "gzr", "kn", "agr", "uzn", "hbx", "dhr", "nn")
+        self.all(buf).wait_send()
+
+
+WIDE_EX = ("meta", "xbw", "hgw", "bfw", "gw", "ur", "uz")
+NARROW_EX = ("xbn", "hbn", "ger", "zer", "agr", "uzn", "hbx", "dhr")
+CHIP_EX = ("kw", "nw")
 
 
 def step_kernel(W, N, resident, names, *refs):
@@ -87,11 +95,17 @@
     Ck = half // A
     scale = math.sqrt(2.0 / M)
     lsem = r.lsem
-    ex = SimpleNamespace()
-    for name in WIDE_EX:
-        vars(ex)[name] = Exchange("wide", W, wi, getattr(r, name + "_s"), getattr(r, name + "_r"))
-    for name in NARROW_EX:
-        vars(ex)[name] = Exchange("narrow", N, ni, getattr(r, name + "_s"), getattr(r, name + "_r"))
+    core, side = lax.rem(ni, 2), ni // 2
+    groups = (
+        (WIDE_EX, W, wi, lambda p: {"wide": p}),
+        (NARROW_EX, N, ni, lambda p: {"narrow": p}),
+        (CHIP_EX, W * N // 2, wi * (N // 2) + side, lambda p: {"wide": p // (N // 2), "narrow": lax.rem(p, N // 2) * 2 + core}),
+    )
+    ex, live = SimpleNamespace(), []
+    for group, size, me, where in groups:
+        for name in group:
+            vars(ex)[name] = Exchange(size, me, where, r.es, 2 * len(live))
+            live.append(name)
 
     own_f = pl.ds(pl.multiple_of(ni * Fn, Fn), Fn)
     own_m = pl.ds(pl.multiple_of(ni * Mn, Mn), Mn)
@@ -101,42 +115,43 @@
         pltpu.make_async_copy(r.w2, r.w2f, lsem.at[2]),
         pltpu.make_async_copy(r.omega.at[own_f], om, lsem.at[3]),
         pltpu.make_async_copy(r.prior_wt.at[:, own_m], r.pwt, lsem.at[4]),
+        pltpu.make_async_copy(r.phase.at[:, own_m], r.ph, lsem.at[9]),
     ]
-    for load in loads:
+    small = [
+        pltpu.make_async_copy(r.batch_x, r.xbs, lsem.at[10]),
+        pltpu.make_async_copy(r.targets, r.tgs, lsem.at[11]),
+        pltpu.make_async_copy(r.dgroup, r.dgs, lsem.at[12]),
+        pltpu.make_async_copy(r.alphat_own, r.als, lsem.at[13]),
+    ]
+    for load in small[:1] + loads[:1] + small[1:] + loads[1:]:
         load.start()
 
     barrier = pltpu.get_barrier_semaphore()
 
-    def greet(axis, size, me):
-        def step(k, carry):
-            pl.semaphore_signal(barrier, inc=1, device_id={axis: lax.rem(me + k, size)}, device_id_type=MESH)
-            return carry
-
-        lax.fori_loop(1, size, step, 0)
-
-    greet("narrow", N, ni)
-    greet("wide", W, wi)
-
-    r.xbn[ni] = r.batch_x[...].astype(F32)
+    ex.kw.greet(barrier)
+    ex.xbn.greet(barrier)
+    small[0].wait()
+    r.xbn[ni] = r.xbs[...].astype(F32)
     lane = lax.broadcasted_iota(jnp.int32, (1, 128), 1)
     for k in range(Bg):
         prec_k = r.ptable[r.pindex[k]]
         r.meta[wi, k : k + 1, :] = jnp.where(
             lane == 0, r.bgroup[k].astype(F32),
             jnp.where(lane == 1, r.bindex[k].astype(F32), jnp.where(lane == 2, prec_k, 0.0)))
-    r.meta[wi, :, S : 2 * S] = r.targets[...]
-    r.ad[ni, 0:S, :] = r.alphat_own[...]
-    r.ad[ni, S : S + 8, :] = jnp.broadcast_to(r.dgroup[...].astype(F32), (8, R))
-
-    pl.semaphore_wait(barrier, W - 1 + N - 1)
+    for load in small[1:]:
+        load.wait()
+    r.meta[wi, :, S : 2 * S] = r.tgs[...]
+    r.ad[ni, 0:S, :] = r.als[...]
+    r.ad[ni, S : S + 8, :] = jnp.broadcast_to(r.dgs[...].astype(F32), (8, R))
+
+    pl.semaphore_wait(barrier, W * N // 2 - 1 + N - 1)
 
     def xcopy(src, dst, k, p):
         return pltpu.make_async_remote_copy(
             src_ref=src, dst_ref=dst, send_sem=r.x_s.at[k], recv_sem=r.x_r.at[k],
             device_id={"narrow": p}, device_id_type=MESH)
 
-    cut = R * 5 // 16 // 16 * 16
-    cuts = (0, cut, 2 * cut, R)
+    cuts = (0, R * 4 // 16, R * 11 // 16, R)
 
     def piece(k, src=None, slot=None):
         rows = pl.ds(cuts[k], cuts[k + 1] - cuts[k])
@@ -156,7 +171,11 @@
     ex.xbn.gather(r.xbn)
     x_over(0).start()
     ex.meta.gather(r.meta)
-    ex.ad.gather(r.ad)
+
+    def ad_copy(slot, k, p):
+        return xcopy(r.ad.at[slot], r.ad.at[slot], 7 + k, p)
+
+    ad_copy(ni, 0, n1).start()
 
     loads[0].wait()
 
@@ -172,10 +191,11 @@
     xbg = r.xbg[...]
     hb, gb = gelu_pair(dot(xbg.astype(BF), w1b[...]))
     hb = hb.astype(BF).astype(F32)
-    r.hbn[ni] = hb
+    r.hbn[ni] = jnp.concatenate([hb[:, : Hn // 2], hb[:, Hn // 2 :]], axis=0).astype(BF)
     ex.hbn.gather(r.hbn)
     x_over(1).start()
     x_side().start()
+    ad_copy(ni, 1, n2).start()
     r.hgw[wi] = jnp.concatenate([hb, gb], axis=0).astype(BF)
     ex.hgw.gather(r.hgw)
     r.xbw[wi] = jnp.concatenate([xbg[:, : D // 2], xbg[:, D // 2 :]], axis=0).astype(BF)
@@ -206,16 +226,22 @@
     def turn(q):
         xT[:, pl.ds(pl.multiple_of(q * R, R), R)] = xg[q].T
 
+    ex.hbn.wait(r.hbn)
+    hbn = [r.hbn[n].astype(F32) for n in range(N)]
+    hid_g = jnp.concatenate([h[k * Bg : (k + 1) * Bg] for h in hbn for k in range(2)], axis=1).astype(BF)
+    bfeat = dot(hid_g, w2b[...]).astype(BF)
+    r.bfs[...] = bfeat.astype(F32)
+    gpart = dot(bfeat, w2b[...], NT)
+    for n in range(N):
+        r.ges[n] = gpart[:, n * Hn : (n + 1) * Hn]
+    ex.ger.scatter(r.ges, r.ger)
+    r.ger[ni] = r.ges[ni]
     loads[3].wait()
-    ex.hbn.wait(r.hbn)
-    hid_g = jnp.concatenate([r.hbn[n] for n in range(N)], axis=1).astype(BF)
-    bfeat = dot(hid_g, w2b[...]).astype(BF)
-    gpart = dot(bfeat, w2b[...], NT)
-    zpart = dot(bfeat, om[...])
+    zpart = dot(r.bfs[...].astype(BF), om[...])
     for n in range(N):
-        r.gzs[n, :, :Hn] = gpart[:, n * Hn : (n + 1) * Hn]
-        r.gzs[n, :, Hn:] = zpart[:, n * Mn : (n + 1) * Mn]
-    ex.gzr.scatter(r.gzs, r.gzr)
+        r.zes[n] = zpart[:, n * Mn : (n + 1) * Mn]
+    ex.zer.scatter(r.zes, r.zer)
+    r.zer[ni] = r.zes[ni]
     x_over(2).start()
     later = []
     if resident:
@@ -223,21 +249,24 @@
         later = [pltpu.make_async_copy(src, dst, lsem.at[5 + k]) for k, (src, dst) in enumerate(pairs)]
     for load in later:
         load.start()
-    for k in range(2):
-        xcopy(*piece(k, slot=n2), 1 + k, n2).wait_recv()
-        x_pass(k).start()
-    r.gzr[ni] = r.gzs[ni]
-    bf32 = bfeat.astype(F32)
+    bf32 = r.bfs[...]
     r.bfw[wi] = jnp.concatenate([bf32[:, : Fn // 2], bf32[:, Fn // 2 :]], axis=0).astype(BF)
     ex.bfw.gather(r.bfw)
     loads[1].wait()
     block(ni)
-    ex.gzr.wait(r.gzr)
-    gz = jnp.sum(r.gzr[...], axis=0)
+    ex.ger.wait(r.ger)
+    gz = jnp.sum(r.ger[...], axis=0)
     r.gw[wi] = jnp.concatenate([gz[:, : Hn // 2], gz[:, Hn // 2 : Hn]], axis=0).astype(BF)
     ex.gw.gather(r.gw)
+    for k in range(2):
+        xcopy(*piece(k, slot=n2), 1 + k, n2).wait_recv()
+        x_pass(k).start()
+    ad_copy(n2, 1, n2).wait_recv()
+    ad_copy(n2, 2, n1).start()
+    ex.zer.wait(r.zer)
     own_b = pl.ds(pl.multiple_of(wi * Bg, Bg), Bg)
-    angle = gz[:, Hn:] + r.phase[:, own_m]
+    loads[5].wait()
+    angle = jnp.sum(r.zer[...], axis=0) + r.ph[...]
     r.cz[...] = jnp.zeros_like(r.cz)
     r.cz[own_b, :] = scale * jnp.cos(angle)
     r.sz[...] = scale * jnp.sin(angle)
@@ -249,7 +278,8 @@
     turn(ni)
     turn(n1)
     ex.meta.wait(r.meta)
-    ex.ad.wait(r.ad)
+    ad_copy(n1, 0, n1).wait_recv()
+    ad_copy(n3, 2, n1).wait_recv()
     meta = r.meta[...].reshape(B, 128)
     r.metat[...] = meta.T
     alphat = jnp.concatenate([r.ad[n, 0:S, :] for n in range(N)], axis=1)
@@ -273,12 +303,20 @@
     r.gmat[...] = gmat
     amat = r.pmask[...] * dot(gmat, hid[...], NT) + r.amat[...]
     r.amat[...] = amat
-    r.kn[ni] = dot(r.alphat[...], amat, NT, HIGH) + r.prior[...]
-    ex.kn.gather(r.kn)
+    r.kn[core] = dot(r.alphat[...], amat, NT, HIGH) + r.prior[...]
+
+    def core_copy(buf, k):
+        return xcopy(buf.at[core], buf.at[core], 10 + k, n1)
+
+    def core_sum(buf, k):
+        xcopy(buf.at[1 - core], buf.at[1 - core], 10 + k, n1).wait_recv()
+        return buf[0] + buf[1]
+
+    core_copy(r.kn, 0).start()
     turn(n2)
     turn(n3)
-    ex.kn.wait(r.kn)
-    r.kw[wi] = jnp.sum(r.kn[...], axis=0)
+    chip = wi * (N // 2) + side
+    r.kw[chip] = core_sum(r.kn, 0)
     ex.kw.gather(r.kw)
     ex.hgw.wait(r.hgw)
     hg = r.hgw[...].astype(F32)
@@ -316,26 +354,40 @@
         off = lax.rem(A // 2 + step - 1, max(A - 1, 1)) + 1
         return lax.rem(a + off + lax.rem(a, 2) * (A - 2 * off), A)
 
+    Q = max(1, min(4, Ck // 16))
+    Cq = Ck // Q
+
+    def pcopy(ap, q):
+        rows = pl.ds(pl.multiple_of(ap * Ck + q * Cq, Cq), Cq)
+        return wcopy(psend.at[rows], precv.at[rows], "p", 0, ap * Q + q, pair)
+
     def pair_chunk(ap):
-        psend[ap] = grad_rows((1 - b) * half + ap * Ck).astype(BF)
-        wcopy(psend.at[ap], precv.at[ap], "p", ap, ap, pair).start()
+        psend[pl.ds(pl.multiple_of(ap * Ck, Ck), Ck), :] = grad_rows((1 - b) * half + ap * Ck).astype(BF)
+        for q in range(Q):
+            pcopy(ap, q).start()
 
     def pair_send(step, carry):
         pair_chunk(target(step))
         return carry
 
-    def z_sum(ap):
-        v = grad_rows(b * half + ap * Ck)
-        wcopy(psend.at[ap], precv.at[ap], "p", ap, ap, pair).wait_recv()
-        return v + precv[ap].astype(F32)
+    def zcopy(ap, q):
+        rows = pl.ds(q * Cq, Cq)
+        return wcopy(zsend.at[ap, rows], zrecv.at[a, rows], "z", 0, 0, 2 * ap + b)
+
+    def z_part(ap, q):
+        pcopy(ap, q).wait_recv()
+        rows = pl.ds(pl.multiple_of(ap * Ck + q * Cq, Cq), Cq)
+        return r.zf[q * Cq : (q + 1) * Cq, :] + precv[rows, :].astype(F32)
 
     def z_send(step, carry):
         ap = target(step)
-        zsend[ap] = z_sum(ap).astype(BF)
-        wcopy(zsend.at[ap], zrecv.at[a], "z", ap, a, 2 * ap + b).start()
+        r.zf[...] = grad_rows(b * half + ap * Ck)
+        for q in range(Q):
+            zsend[ap, q * Cq : (q + 1) * Cq, :] = z_part(ap, q).astype(BF)
+            zcopy(ap, q).start()
         return carry
 
-    lax.fori_loop(0, min(1, A - 1), pair_send, 0)
+    lax.fori_loop(0, min(2, A - 1), pair_send, 0)
 
     agt = -dot(grt, r.amat[...], precision=HIGH)
     for n in range(N):
@@ -349,10 +401,10 @@
     uown = jnp.sum(r.ur[...], axis=0)
     r.uz[wi] = jnp.concatenate([uown, dz], axis=0).astype(BF)
     ex.uz.gather(r.uz)
-    lax.fori_loop(min(1, A - 1), A - 1, pair_send, 0)
+    lax.fori_loop(min(2, A - 1), A - 1, pair_send, 0)
     pair_chunk(a)
 
-    lax.fori_loop(0, min(1, A - 1), z_send, 0)
+    lax.fori_loop(0, min(2, A - 1), z_send, 0)
 
     ex.bfw.wait(r.bfw)
     ex.uz.wait(r.uz)
@@ -360,9 +412,76 @@
     r.uzn[ni] = jnp.concatenate([uz[:, :Bg].reshape(B, Hn), uz[:, Bg:].reshape(B, Mn)], axis=1).astype(BF)
     ex.uzn.gather(r.uzn)
 
-    lax.fori_loop(min(1, A - 1), A - 1, z_send, 0)
-    fin = z_sum(a)
-
+    lax.fori_loop(min(2, A - 1), A - 1, z_send, 0)
+    r.zf[...] = grad_rows(b * half + a * Ck)
+    for q in range(Q):
+        r.zf[q * Cq : (q + 1) * Cq, :] = z_part(a, q)
+
+    if A > 1:
+        others = pl.ds(0, A - 1)
+        wcopy(zsend.at[others], zrecv.at[others], "z", 0, 0, pair).wait_recv()
+
+    def z_gain(k, carry):
+        r.zf[...] = r.zf[...] + zrecv[lax.rem(a + k, A)].astype(F32)
+        return carry
+
+    lax.fori_loop(1, A, z_gain, 0)
+    mine = b * A + a
+
+    def shard(slot, q=0, count=Ck):
+        return pl.ds(pl.multiple_of(slot * Ck + q * Cq, Cq), count)
+
+    gat[shard(mine), :] = r.zf[...].astype(BF)
+
+    def fcopy(ap, q):
+        rows = shard(b * A + ap, q, Cq)
+        return wcopy(gat.at[rows], gat.at[rows], "f", 0, 0, pair)
+
+    def gcopy(ap, q, way):
+        rows = shard(b * A + ap, q, Cq)
+        k = ap * Q + q if way > 0 else (A + ap) * Q + q
+        return wcopy(gat.at[rows], gat.at[rows], "g", 0 if way > 0 else 1, k, 2 * (a + way) + b)
+
+    for q in range(Q):
+
+        @pl.when(a + 1 < A)
+        def _():
+            gcopy(a, q, 1).start()
+
+        @pl.when(a > 0)
+        def _():
+            gcopy(a, q, -1).start()
+
+        fcopy(a, q).start()
+
+    def g_pass(step, carry):
+        below, above = a - 1 - step // Q, a + 1 + step // Q
+        q = lax.rem(step, Q)
+
+        @pl.when(below >= 0)
+        def _():
+            gcopy(below, q, 1).wait_recv()
+
+            @pl.when(a + 1 < A)
+            def _():
+                gcopy(below, q, 1).start()
+
+            fcopy(below, q).start()
+
+        @pl.when(above < A)
+        def _():
+            gcopy(above, q, -1).wait_recv()
+
+            @pl.when(a > 0)
+            def _():
+                gcopy(above, q, -1).start()
+
+            fcopy(above, q).start()
+
+        return carry
+
+    steps = (A - 1) * Q
+    third = min(Q, steps)
     ex.uzn.wait(r.uzn)
     acc = jnp.zeros((B, Fn), F32)
     for n in range(N):
@@ -376,63 +495,7 @@
     ex.dhr.scatter(r.dhs, r.dhr)
     r.dhr[ni] = r.dhs[ni]
 
-    def z_gain(k, total_rows):
-        ap = lax.rem(a + k, A)
-        wcopy(zsend.at[ap], zrecv.at[ap], "z", ap, ap, 2 * ap + b).wait_recv()
-        return total_rows + zrecv[ap].astype(F32)
-
-    fin = lax.fori_loop(1, A, z_gain, fin)
-    mine = b * A + a
-
-
-    def shard(slot):
-        return pl.ds(pl.multiple_of(slot * Ck, Ck), Ck)
-
-    gat[shard(mine), :] = fin.astype(BF)
-
-    def fcopy(ap, side):
-        rows = shard(side * A + ap)
-        return wcopy(gat.at[rows], gat.at[rows], "f", ap, ap, pair)
-
-    def gcopy(ap, way):
-        rows = shard(b * A + ap)
-        k = ap if way > 0 else A + ap
-        return wcopy(gat.at[rows], gat.at[rows], "g", k, k, 2 * (a + way) + b)
-
-    fcopy(a, b).start()
-
-    @pl.when(a + 1 < A)
-    def _():
-        gcopy(a, 1).start()
-
-    @pl.when(a > 0)
-    def _():
-        gcopy(a, -1).start()
-
-    def g_pass(step, carry):
-        below, above = a - 1 - step, a + 1 + step
-
-        @pl.when(below >= 0)
-        def _():
-            gcopy(below, 1).wait_recv()
-
-            @pl.when(a + 1 < A)
-            def _():
-                gcopy(below, 1).start()
-
-            fcopy(below, b).start()
-
-        @pl.when(above < A)
-        def _():
-            gcopy(above, -1).wait_recv()
-
-            @pl.when(a > 0)
-            def _():
-                gcopy(above, -1).start()
-
-            fcopy(above, b).start()
-
-        return carry
+    lax.fori_loop(0, third, g_pass, 0)
 
     def two(v):
         return jnp.sum(jnp.sum(v * v, axis=1, keepdims=True), axis=0, keepdims=True)
@@ -452,57 +515,47 @@
     ex.dhr.wait(r.dhr)
     r.dpb[...] = (jnp.sum(r.dhr[...].astype(F32), axis=0) * r.gb[...]).astype(BF)
 
-    square = square * (1.0 / W) + two(fin + dot(r.xbt[shard(mine), :], r.dpb[...])) + two(agt)
-    r.nn[ni] = jnp.broadcast_to(square, (8, 128))
-    ex.nn.gather(r.nn)
-    lax.fori_loop(0, min(1, A - 1), g_pass, 0)
-    ex.nn.wait(r.nn)
-    r.nw[wi] = jnp.sum(r.nn[...], axis=0)
+    square = square * (1.0 / W) + two(r.zf[...] + dot(r.xbt[shard(mine), :], r.dpb[...])) + two(agt)
+    r.nn[core] = jnp.broadcast_to(square, (8, 128))
+    core_copy(r.nn, 1).start()
+    lax.fori_loop(third, min(2 * third, steps), g_pass, 0)
+    r.nw[chip] = core_sum(r.nn, 1)
     ex.nw.gather(r.nw)
-    lax.fori_loop(min(1, A - 1), A - 1, g_pass, 0)
-
+    lax.fori_loop(min(2 * third, steps), steps, g_pass, 0)
     ex.nw.wait(r.nw)
     norm = jnp.sum(r.nw[...], axis=0)
     lanes = lax.broadcasted_iota(jnp.int32, (8, 128), 1)
     r.scal[...] = jnp.where(lanes == 0, loss, jnp.where(lanes == 1, total, norm))
 
-    def g_last(k, carry):
-        ap = lax.rem(a + k, A)
-        fcopy(ap, 1 - b).wait_recv()
-        return carry
-
-    lax.fori_loop(0, A, g_last, 0)
-
-    for name in WIDE_EX:
-        vars(ex)[name].drain(getattr(r, name))
-    for name in NARROW_EX:
+    theirs = pl.ds(pl.multiple_of((1 - b) * half, half), half)
+    ours = pl.ds(pl.multiple_of(b * half, half), half)
+    wcopy(gat.at[theirs], gat.at[theirs], "f", 0, 0, pair).wait_recv()
+
+    for name in live:
         vars(ex)[name].drain(getattr(r, name))
     x_side().wait_send()
     for k in range(3):
         x_over(k).wait_send()
         x_pass(k).wait_send()
-
-    def left(k, carry):
-        wcopy(psend.at[k], precv.at[k], "p", k, k, pair).wait_send()
-        fcopy(k, b).wait_send()
-
-        @pl.when((k <= a) & (a + 1 < A))
+    for slot, k, p in ((ni, 0, n1), (ni, 1, n2), (n2, 2, n1)):
+        ad_copy(slot, k, p).wait_send()
+    core_copy(r.kn, 0).wait_send()
+    core_copy(r.nn, 1).wait_send()
+    wcopy(psend, precv, "p", 0, 0, pair).wait_send()
+    wcopy(gat.at[ours], gat.at[ours], "f", 0, 0, pair).wait_send()
+    if A > 1:
+        wcopy(zsend.at[others], zrecv.at[others], "z", 0, 0, pair).wait_send()
+    for k in range(A):
+        up, down = (pl.ds(0, n * Ck) for n in (k + 1, A - k))
+
+        @pl.when((a == k) & (a + 1 < A))
         def _():
-            gcopy(k, 1).wait_send()
-
-        @pl.when((k >= a) & (a > 0))
+            wcopy(gat.at[up], gat.at[up], "g", 0, 0, pair).wait_send()
+
+        @pl.when((a == k) & (a > 0))
         def _():
-            gcopy(k, -1).wait_send()
-
-        return carry
-
-    def left_z(k, carry):
-        ap = lax.rem(a + k, A)
-        wcopy(zsend.at[ap], zrecv.at[a], "z", ap, a, 2 * ap + b).wait_send()
-        return carry
-
-    lax.fori_loop(0, A, left, 0)
-    lax.fori_loop(1, A, left_z, 0)
+            wcopy(gat.at[down], gat.at[down], "g", 1, 0, pair).wait_send()
+
     for load in later:
         load.wait()
 
@@ -612,11 +665,11 @@
     hbm, vmem, smem = (pl.BlockSpec(memory_space=m) for m in (pl.ANY, pltpu.VMEM, pltpu.SMEM))
     resident = B <= 128
     args = dict(
-        data_x=(data_x, hbm), dgroup=(data_group.reshape(1, R), vmem), batch_x=(batch_x, vmem),
+        data_x=(data_x, hbm), dgroup=(data_group.reshape(1, R), hbm), batch_x=(batch_x, hbm),
         bgroup=(batch_group, smem), bindex=(batch_index, smem), pindex=(prec_index, smem),
-        ptable=(prec_table, smem), targets=(targets, vmem), omega=(omega, hbm),
-        phase=(phase.reshape(1, M), vmem), prior_wt=(prior_w.T, hbm), w1=(w1_master, hbm),
-        w2=(w2_master, hbm), alphat_own=(alpha.T, vmem),
+        ptable=(prec_table, smem), targets=(targets, hbm), omega=(omega, hbm),
+        phase=(phase.reshape(1, M), hbm), prior_wt=(prior_w.T, hbm), w1=(w1_master, hbm),
+        w2=(w2_master, hbm), alphat_own=(alpha.T, hbm),
     )
     state = dict(
         w1=(w1_master, hbm), w1_m=(w1_moment, hbm), w1_v=(w1_second, hbm),
@@ -633,29 +686,28 @@
         xg=((N, R, D), BF), xT=((D, N * R), BF), hid=((N * R, Hn), BF), gd=((N * R, Hn), F32),
         dpre=((N * R, Hn), BF), pre=((R, Hn), F32), w1b=((D, Hn), BF),
         w2b=((H, Fn), BF), om=((Fn, M), BF), pwt=((S, Mn), F32),
-        xbg=((Bg, D), F32), gzs=((N, Bg, Hn + Mn), F32), us=((W, Bg, Hn), F32), ags=((N, S, R), F32),
+        xbg=((Bg, D), F32), xbs=((brow, D), BF), tgs=((Bg, S), F32), dgs=((1, R), jnp.int32), als=((S, R), F32), ph=((1, Mn), F32), ges=((N, Bg, Hn), F32), zes=((N, Bg, Mn), F32), bfs=((Bg, Fn), F32), zf=((Ck, Hn), F32), us=((W, Bg, Hn), F32), ags=((N, S, R), F32),
         dhs=((N, B, Hn), BF), cz=((B, Mn), F32), sz=((Bg, Mn), F32), prior=((S, B), F32), gp=((B, Mn), F32),
         metat=((128, B), F32), alphat=((S, N * R), F32), pmask=((B, N * R), F32), amat=((B, N * R), F32),
         gmat=((B, Hn), BF), db=((2 * B, Fn), BF),
-        psend=((A, Ck, Hn), BF), precv=((A, Ck, Hn), BF), zsend=((A, Ck, Hn), BF), zrecv=((A, Ck, Hn), BF),
+        psend=((A * Ck, Hn), BF), precv=((A * Ck, Hn), BF), zsend=((A, Ck, Hn), BF), zrecv=((A, Ck, Hn), BF),
         gb=((B, Hn), F32),
         meta=((W, Bg, 128), F32), xbw=((W, 2 * Bg, D // 2), BF), hgw=((W, 2 * Bg, Hn), BF),
-        bfw=((W, 2 * Bg, Fn // 2), BF), gw=((W, 2 * Bg, Hn // 2), BF), kw=((W, S, B), F32),
-        ur=((W, Bg, Hn), F32), uz=((W, 2 * Bg, Hn), BF), nw=((W, 8, 128), F32),
-        xbn=((N, brow, D), F32), ad=((N, S + 8, R), F32), hbn=((N, Bg, Hn), F32), gzr=((N, Bg, Hn + Mn), F32),
-        kn=((N, S, B), F32), agr=((N, S, R), F32), uzn=((N, B, Hn + Mn), BF), hbx=((N, B, Hn), BF), dhr=((N, B, Hn), BF),
-        nn=((N, 8, 128), F32),
+        bfw=((W, 2 * Bg, Fn // 2), BF), gw=((W, 2 * Bg, Hn // 2), BF), kw=((W * N // 2, S, B), F32),
+        ur=((W, Bg, Hn), F32), uz=((W, 2 * Bg, Hn), BF), nw=((W * N // 2, 8, 128), F32),
+        xbn=((N, brow, D), F32), ad=((N, S + 8, R), F32), hbn=((N, 2 * Bg, Hn // 2), BF), ger=((N, Bg, Hn), F32), zer=((N, Bg, Mn), F32),
+        kn=((2, S, B), F32), agr=((N, S, R), F32), uzn=((N, B, Hn + Mn), BF), hbx=((N, B, Hn), BF), dhr=((N, B, Hn), BF),
+        nn=((2, 8, 128), F32),
     )
     if resident:
         args.update(state)
         outs.update(held)
     else:
         scratch.update(w1f=held["w1f"], w2f=held["w2f"])
-    sems = [("lsem", 9), ("x_s", 7), ("x_r", 7)]
-    sems += [(name + end, W) for name in WIDE_EX for end in ("_s", "_r")]
-    sems += [(name + end, N) for name in NARROW_EX for end in ("_s", "_r")]
-    sems += [(name + end, A) for name in ("p", "z", "f") for end in ("_s", "_r")]
-    sems += [("g_s", 2 * A), ("g_r", 2 * A)]
+    Q = max(1, min(4, Ck // 16))
+    count = 2 * len(WIDE_EX + NARROW_EX + CHIP_EX)
+    sems = [("lsem", 14), ("x_s", 12), ("x_r", 12), ("es", count), ("p_s", 1), ("p_r", A * Q), ("z_s", 1), ("z_r", 1)]
+    sems += [("f_s", 1), ("f_r", 1), ("g_s", 2), ("g_r", 2 * A * Q)]
     names = [*args, *outs, *scratch] + [n for n, _ in sems]
     grads = pl.pallas_call(
         lambda *refs: step_kernel(W, N, resident, names, *refs),
@@ -663,7 +715,7 @@
         in_specs=[spec for _, spec in args.values()],
         out_specs=[vmem] * len(outs),
         scratch_shapes=[pltpu.VMEM(s, t) for s, t in scratch.values()] + [pltpu.SemaphoreType.DMA((k,)) for _, k in sems],
-        compiler_params=pltpu.CompilerParams(collective_id=0, has_side_effects=True, vmem_limit_bytes=(60 if not resident else 39) * 2**20),
+        compiler_params=pltpu.CompilerParams(collective_id=0, has_side_effects=True, vmem_limit_bytes=(62 if not resident else 39) * 2**20),
         name="gradients",
     )(*[v for v, _ in args.values()])
 

time: 86.1 us -> 79.3 us (0.921)
  Pallas kernels: 84.6 us -> 77.8 us
    pallas_call x1, Pallas kernels: 76.2 us -> 69.4 us  [on_device(): pl.pallas_call(lambda *refs: step_kernel(W, N, resident, names, *refs), o...]
where the time goes in v5:
time: 79.3 us; the launch traced here: 79.1 us
  Pallas kernels  77.8 us (98%)
    pallas_call x1, Pallas kernels, on_device(): pl.pallas_call(lambda *refs: step_kernel(W, N, resident, names, *refs), o...  69.4 us
    pallas_call x1, Pallas kernels, on_device(): pl.pallas_call(lambda *refs: update_kernel(resident, slots, C, names2, *r...  8.4 us

profile of v5, /device:TPU:0, one launch (start us, length us, event | category | flops | bytes accessed | tf_op | source)
XLA Modules:
  0.0 79.1 jit_solution(5783803610253382155)
XLA Ops:
  0.7 0.0 copy-start
  0.7 0.0 copy-start.1
  0.7 0.0 copy-start.2
  0.7 69.4 %gradients.1 = (f32[8,128]{1,0:T(8,128)S(1)}, f32[16,256]{1,0:T(8,128)S(1)}, bf16[1024,512]{1,0:T(8,128)(2,1)S(1)}, bf16[1024,64]{1,0:T(8,128)(2,1)S(1)}, bf16[6...) custom-call(bf16[256,1024]{1,0:T(8,128)(2,1)} %refs_0_.1, ...), custom_call_target="tpu_custom_call" | custom-call | tf_op jit(solution)/shard_map/gradients/pallas_call | solution.py:712
  70.1 0.0 copy-done
  70.1 0.0 copy-done.1
  70.1 0.0 copy-done.2
  70.1 8.4 %adamw.1 = (f32[16,256]{1,0:T(8,128)}, f32[16,256]{1,0:T(8,128)}, f32[16,256]{1,0:T(8,128)}, f32[1024,512]{1,0:T(8,128)}, f32[1024,512]{1,0:T(8,128)}, /*index=5...) custom-call(f32[8,128]{1,0:T(8,128)S(1)} %get-tuple-element.37.refs_, ...), custom_call_target="tpu_custom_call" | custom-call | tf_op jit(solution)/shard_map/adamw/pallas_call | solution.py:738
  78.6 0.6 fusion
Async XLA Ops:
  0.7 69.5 %copy-start = (f32[256,16]{0,1:T(8,128)S(1)}, f32[256,16]{0,1:T(8,128)}, u32[]{:S(2)}) copy-start(f32[256,16]{0,1:T(8,128)} %param.37) | copy-start | bytes 49156
  0.7 69.5 %copy-start.1 = (f32[256,16]{0,1:T(8,128)S(1)}, f32[256,16]{0,1:T(8,128)}, u32[]{:S(2)}) copy-start(f32[256,16]{0,1:T(8,128)} %param.38) | copy-start | bytes 49156
  0.7 69.5 %copy-start.2 = (f32[256,16]{0,1:T(8,128)S(1)}, f32[256,16]{0,1:T(8,128)}, u32[]{:S(2)}) copy-start(f32[256,16]{0,1:T(8,128)} %param.39) | copy-start | bytes 49156

commit v6 on v5

--- a/solution.py
+++ b/solution.py
@@ -68,8 +68,8 @@
         self.all(buf).wait_send()
 
 
-WIDE_EX = ("meta", "xbw", "hgw", "bfw", "gw", "ur", "uz")
-NARROW_EX = ("xbn", "hbn", "ger", "zer", "agr", "uzn", "hbx", "dhr")
+WIDE_EX = ("meta", "xbw", "hgw", "bfw", "gw", "szw", "ur", "uz")
+NARROW_EX = ("xbn", "hbn", "ger", "zer", "agr", "hbx", "dhr")
 CHIP_EX = ("kw", "nw")
 
 
@@ -151,7 +151,8 @@
             src_ref=src, dst_ref=dst, send_sem=r.x_s.at[k], recv_sem=r.x_r.at[k],
             device_id={"narrow": p}, device_id_type=MESH)
 
-    cuts = (0, R * 4 // 16, R * 11 // 16, R)
+    cuts = (0, R * 4 // 16, R * 10 // 16, R)
+    P = len(cuts) - 1
 
     def piece(k, src=None, slot=None):
         rows = pl.ds(cuts[k], cuts[k + 1] - cuts[k])
@@ -166,15 +167,16 @@
         return xcopy(*piece(k, r.data_x), 1 + k, n2)
 
     def x_pass(k):
-        return xcopy(*piece(k, slot=n2), 4 + k, n1)
+        return xcopy(*piece(k, slot=n2), 1 + P + k, n1)
 
     ex.xbn.gather(r.xbn)
     x_over(0).start()
     ex.meta.gather(r.meta)
 
     def ad_copy(slot, k, p):
-        return xcopy(r.ad.at[slot], r.ad.at[slot], 7 + k, p)
-
+        return xcopy(r.ad.at[slot], r.ad.at[slot], 9 + k, p)
+
+    ad_copy(ni, 1, n2).start()
     ad_copy(ni, 0, n1).start()
 
     loads[0].wait()
@@ -195,7 +197,6 @@
     ex.hbn.gather(r.hbn)
     x_over(1).start()
     x_side().start()
-    ad_copy(ni, 1, n2).start()
     r.hgw[wi] = jnp.concatenate([hb, gb], axis=0).astype(BF)
     ex.hgw.gather(r.hgw)
     r.xbw[wi] = jnp.concatenate([xbg[:, : D // 2], xbg[:, D // 2 :]], axis=0).astype(BF)
@@ -209,19 +210,21 @@
 
     lax.fori_loop(0, H // 128, cast2, 0)
 
-    def block(q):
-        base = q * R
-        r.pre[...] = dot(xg[q], w1b[...])
+    def block(q, first=0, last=P):
+        base = q * R + cuts[first]
+        size = cuts[last] - cuts[first]
+        r.pre[:size, :] = dot(xg[q, cuts[first] : cuts[last], :], w1b[...])
+        step = math.gcd(size, 32)
 
         def part(k, carry):
-            src = pl.ds(pl.multiple_of(k * 32, 32), 32)
-            dst = pl.ds(pl.multiple_of(base + k * 32, 32), 32)
+            src = pl.ds(pl.multiple_of(k * step, step), step)
+            dst = pl.ds(pl.multiple_of(base + k * step, step), step)
             out, slope = gelu_pair(r.pre[src, :])
             hid[dst, :] = out.astype(BF)
             gd[dst, :] = slope
             return carry
 
-        lax.fori_loop(0, R // 32, part, 0)
+        lax.fori_loop(0, size // step, part, 0)
 
     def turn(q):
         xT[:, pl.ds(pl.multiple_of(q * R, R), R)] = xg[q].T
@@ -269,19 +272,26 @@
     angle = jnp.sum(r.zer[...], axis=0) + r.ph[...]
     r.cz[...] = jnp.zeros_like(r.cz)
     r.cz[own_b, :] = scale * jnp.cos(angle)
-    r.sz[...] = scale * jnp.sin(angle)
+    sz = scale * jnp.sin(angle)
+    r.szw[wi] = jnp.concatenate([sz[:, : Mn // 2], sz[:, Mn // 2 :]], axis=0).astype(BF)
+    ex.szw.gather(r.szw)
     loads[4].wait()
     r.prior[...] = dot(r.pwt[...], r.cz[...], NT, HIGH)
 
+    def x_last(k):
+        xcopy(*piece(k, slot=n3), 1 + P + k, n1).wait_recv()
+
     xcopy(r.data_x, xg.at[n1], 0, n1).wait_recv()
     block(n1)
-    turn(ni)
-    turn(n1)
+    block(n2, 0, 2)
+    x_last(0)
+    x_last(1)
+    block(n3, 0, 2)
     ex.meta.wait(r.meta)
+    meta = r.meta[...].reshape(B, 128)
+    r.metat[...] = meta.T
     ad_copy(n1, 0, n1).wait_recv()
     ad_copy(n3, 2, n1).wait_recv()
-    meta = r.meta[...].reshape(B, 128)
-    r.metat[...] = meta.T
     alphat = jnp.concatenate([r.ad[n, 0:S, :] for n in range(N)], axis=1)
     r.alphat[...] = alphat
     group = jnp.concatenate([r.ad[n, S : S + 1, :] for n in range(N)], axis=1)
@@ -290,12 +300,13 @@
     col = lax.broadcasted_iota(jnp.int32, (1, N * R), 1) + wi * (N * R)
     first = (ni == 0).astype(F32)
     r.amat[...] = jnp.where(meta[:, 1:2] == col.astype(F32), first / meta[:, 2:3], 0.0)
+    turn(ni)
+    turn(n1)
     xcopy(*piece(2, slot=n2), 3, n2).wait_recv()
     x_pass(2).start()
-    block(n2)
-    for k in range(3):
-        xcopy(*piece(k, slot=n3), 4 + k, n1).wait_recv()
-    block(n3)
+    block(n2, 2, 3)
+    x_last(2)
+    block(n3, 2, 3)
 
     ex.gw.wait(r.gw)
     gw = r.gw[...].astype(F32)
@@ -303,21 +314,23 @@
     r.gmat[...] = gmat
     amat = r.pmask[...] * dot(gmat, hid[...], NT) + r.amat[...]
     r.amat[...] = amat
-    r.kn[core] = dot(r.alphat[...], amat, NT, HIGH) + r.prior[...]
+    kal = dot(r.alphat[...], amat, NT, HIGH) + r.prior[...]
+    fold = max(1, min(S // 8, 128 // B))
+    r.kn[core] = jnp.concatenate([kal[k * (S // fold) : (k + 1) * (S // fold)] for k in range(fold)], axis=1)
 
     def core_copy(buf, k):
-        return xcopy(buf.at[core], buf.at[core], 10 + k, n1)
+        return xcopy(buf.at[core], buf.at[core], 12 + k, n1)
 
     def core_sum(buf, k):
-        xcopy(buf.at[1 - core], buf.at[1 - core], 10 + k, n1).wait_recv()
+        xcopy(buf.at[1 - core], buf.at[1 - core], 12 + k, n1).wait_recv()
         return buf[0] + buf[1]
 
     core_copy(r.kn, 0).start()
-    turn(n2)
-    turn(n3)
     chip = wi * (N // 2) + side
     r.kw[chip] = core_sum(r.kn, 0)
     ex.kw.gather(r.kw)
+    turn(n2)
+    turn(n3)
     ex.hgw.wait(r.hgw)
     hg = r.hgw[...].astype(F32)
     r.hbx[ni] = hg[:, :Bg].reshape(B, Hn).astype(BF)
@@ -328,13 +341,15 @@
     r.xbt[...] = jnp.concatenate([xbw[:, :Bg].reshape(B, D // 2), xbw[:, Bg:].reshape(B, D // 2)], axis=1).T.astype(BF)
     ex.kw.wait(r.kw)
     prec = r.metat[2:3, :]
-    resid = r.metat[S : 2 * S, :] - jnp.sum(r.kw[...], axis=0)
+    kal = jnp.sum(r.kw[...], axis=0)
+    resid = r.metat[S : 2 * S, :] - jnp.concatenate([kal[:, k * B : (k + 1) * B] for k in range(fold)], axis=0)
     total = jnp.sum(prec, axis=1, keepdims=True)
     loss = 0.5 * jnp.sum(jnp.sum(prec * (resid * resid), axis=1, keepdims=True), axis=0, keepdims=True)
     grt = prec * resid / total
 
     ds = (-r.pmask[...] * dot(grt, r.alphat[...], TN, HIGH)).astype(BF)
-    r.us[...] = dot(ds, hid[...]).reshape(W, Bg, Hn)
+    upart = dot(ds, hid[...]).reshape(W, Bg, Hn)
+    r.us[...] = jnp.concatenate([upart[:, :, : Hn // 2], upart[:, :, Hn // 2 :]], axis=1).astype(BF)
     ex.ur.scatter(r.us, r.ur)
     for q in range(N):
         rows = slice(q * R, (q + 1) * R)
@@ -347,155 +362,213 @@
 
     psend, precv, zsend, zrecv, gat = r.psend, r.precv, r.zsend, r.zrecv, r.gat
 
+    NH = 2 if Ck % 32 == 0 else 1
+    Hk = Ck // NH
+    Q = 2 if Hk % 32 == 0 else 1
+    Cq = Hk // Q
+
     def grad_rows(row):
-        return dot(xT[pl.ds(pl.multiple_of(row, Ck), Ck), :], dpre[...])
+        return dot(xT[pl.ds(pl.multiple_of(row, Hk), Hk), :], dpre[...])
 
     def target(step):
-        off = lax.rem(A // 2 + step - 1, max(A - 1, 1)) + 1
-        return lax.rem(a + off + lax.rem(a, 2) * (A - 2 * off), A)
-
-    Q = max(1, min(4, Ck // 16))
-    Cq = Ck // Q
-
-    def pcopy(ap, q):
-        rows = pl.ds(pl.multiple_of(ap * Ck + q * Cq, Cq), Cq)
-        return wcopy(psend.at[rows], precv.at[rows], "p", 0, ap * Q + q, pair)
-
-    def pair_chunk(ap):
-        psend[pl.ds(pl.multiple_of(ap * Ck, Ck), Ck), :] = grad_rows((1 - b) * half + ap * Ck).astype(BF)
+        low = a // (A // 2)
+        m = a + low * (A - 1 - 2 * a)
+        single = A - 1 - 2 * m
+        late = (step // single + A - 1) // A
+        e = step - single
+        t = (1 - late) * (A - 1 - step) + late * (m + (1 - lax.rem(e + 2 * A, 2) * 2) * (m - (e + 2 * A) // 2 + A))
+        return t + low * (A - 1 - 2 * t)
+
+    def pcopy(ap, h, q):
+        rows = pl.ds(pl.multiple_of(ap * Ck + h * Hk + q * Cq, Cq), Cq)
+        return wcopy(psend.at[rows], precv.at[rows], "p", 0, ap * NH * Q + h * Q + q, pair)
+
+    def pair_chunk(h, ap):
+        base = ap * Ck + h * Hk
+        psend[pl.ds(pl.multiple_of(base, Hk), Hk), :] = grad_rows((1 - b) * half + base).astype(BF)
         for q in range(Q):
-            pcopy(ap, q).start()
-
-    def pair_send(step, carry):
-        pair_chunk(target(step))
-        return carry
-
-    def zcopy(ap, q):
-        rows = pl.ds(q * Cq, Cq)
-        return wcopy(zsend.at[ap, rows], zrecv.at[a, rows], "z", 0, 0, 2 * ap + b)
-
-    def z_part(ap, q):
-        pcopy(ap, q).wait_recv()
-        rows = pl.ds(pl.multiple_of(ap * Ck + q * Cq, Cq), Cq)
-        return r.zf[q * Cq : (q + 1) * Cq, :] + precv[rows, :].astype(F32)
-
-    def z_send(step, carry):
-        ap = target(step)
-        r.zf[...] = grad_rows(b * half + ap * Ck)
+            pcopy(ap, h, q).start()
+
+    def pair_sends(h, first, last):
+        def send(step, carry):
+            pair_chunk(h, target(step))
+            return carry
+
+        lax.fori_loop(min(first, A - 1), min(last, A - 1), send, 0)
+        if last >= A:
+            pair_chunk(h, a)
+
+    def zcopy(ap, h, q):
+        rows = pl.ds(h * Hk + q * Cq, Cq)
+        return wcopy(zsend.at[ap, rows], zrecv.at[a, rows], "z", 0, h, 2 * ap + b)
+
+    def z_part(ap, h, q):
+        pcopy(ap, h, q).wait_recv()
+        rows = pl.ds(pl.multiple_of(ap * Ck + h * Hk + q * Cq, Cq), Cq)
+        return r.zt[q * Cq : (q + 1) * Cq, :] + precv[rows, :].astype(F32)
+
+    def z_sends(h, first, last):
+        def send(step, carry):
+            ap = target(step)
+            r.zt[...] = grad_rows(b * half + ap * Ck + h * Hk)
+            for q in range(Q):
+                zsend[ap, h * Hk + q * Cq : h * Hk + (q + 1) * Cq, :] = z_part(ap, h, q).astype(BF)
+                zcopy(ap, h, q).start()
+            return carry
+
+        lax.fori_loop(min(first, A - 1), min(last, A - 1), send, 0)
+
+    def z_own(h):
+        r.zt[...] = grad_rows(b * half + a * Ck + h * Hk)
         for q in range(Q):
-            zsend[ap, q * Cq : (q + 1) * Cq, :] = z_part(ap, q).astype(BF)
-            zcopy(ap, q).start()
-        return carry
-
-    lax.fori_loop(0, min(2, A - 1), pair_send, 0)
+            r.zf[h * Hk + q * Cq : h * Hk + (q + 1) * Cq, :] = z_part(a, h, q)
+
+    pair_sends(0, 0, 2)
 
     agt = -dot(grt, r.amat[...], precision=HIGH)
     for n in range(N):
         r.ags[n] = agt[:, n * R : (n + 1) * R]
     ex.agr.scatter(r.ags, r.agr)
     r.agr[ni] = r.ags[ni]
-    r.gp[...] = dot(grt, r.pwt[...], TN, HIGH)
-    dz = r.sz[...] * r.gp[own_b, :]
+    ex.szw.wait(r.szw)
+
+    def unfold(buf):
+        v = buf[...].astype(F32)
+        return jnp.concatenate([v[:, :Bg].reshape(B, -1), v[:, Bg:].reshape(B, -1)], axis=1)
+
+    r.uzn[ni, :, Hn:] = (unfold(r.szw) * dot(grt, r.pwt[...], TN, HIGH)).astype(BF)
     ex.ur.wait(r.ur)
     r.ur[wi] = r.us[wi]
-    uown = jnp.sum(r.ur[...], axis=0)
-    r.uz[wi] = jnp.concatenate([uown, dz], axis=0).astype(BF)
+    r.uz[wi] = jnp.sum(r.ur[...].astype(F32), axis=0).astype(BF)
     ex.uz.gather(r.uz)
-    lax.fori_loop(min(2, A - 1), A - 1, pair_send, 0)
-    pair_chunk(a)
-
-    lax.fori_loop(0, min(2, A - 1), z_send, 0)
-
+    pair_sends(0, 2, A)
+    z_sends(0, 0, 1)
+    for h in range(1, NH):
+        pair_sends(h, 0, A)
+    z_sends(0, 1, 2)
     ex.bfw.wait(r.bfw)
     ex.uz.wait(r.uz)
-    uz = r.uz[...].astype(F32)
-    r.uzn[ni] = jnp.concatenate([uz[:, :Bg].reshape(B, Hn), uz[:, Bg:].reshape(B, Mn)], axis=1).astype(BF)
-    ex.uzn.gather(r.uzn)
-
-    lax.fori_loop(min(2, A - 1), A - 1, z_send, 0)
-    r.zf[...] = grad_rows(b * half + a * Ck)
-    for q in range(Q):
-        r.zf[q * Cq : (q + 1) * Cq, :] = z_part(a, q)
-
-    if A > 1:
-        others = pl.ds(0, A - 1)
-        wcopy(zsend.at[others], zrecv.at[others], "z", 0, 0, pair).wait_recv()
-
-    def z_gain(k, carry):
-        r.zf[...] = r.zf[...] + zrecv[lax.rem(a + k, A)].astype(F32)
-        return carry
-
-    lax.fori_loop(1, A, z_gain, 0)
+    r.uzn[ni, :, :Hn] = unfold(r.uz).astype(BF)
+
+    def u_copy(slot, k, p):
+        return xcopy(r.uzn.at[slot], r.uzn.at[slot], 14 + k, p)
+
+    u_copy(ni, 1, n2).start()
+    u_copy(ni, 0, n1).start()
+    z_sends(0, 2, A)
+    z_own(0)
+
+    others = pl.ds(0, A - 1)
     mine = b * A + a
 
-    def shard(slot, q=0, count=Ck):
-        return pl.ds(pl.multiple_of(slot * Ck + q * Cq, Cq), count)
-
-    gat[shard(mine), :] = r.zf[...].astype(BF)
-
-    def fcopy(ap, q):
-        rows = shard(b * A + ap, q, Cq)
+    def shard(slot, h=0, q=0, count=Ck):
+        return pl.ds(pl.multiple_of(slot * Ck + h * Hk + q * Cq, min(count, Cq)), count)
+
+    def fcopy(ap, h, q):
+        rows = shard(b * A + ap, h, q, Cq)
         return wcopy(gat.at[rows], gat.at[rows], "f", 0, 0, pair)
 
-    def gcopy(ap, q, way):
-        rows = shard(b * A + ap, q, Cq)
-        k = ap * Q + q if way > 0 else (A + ap) * Q + q
-        return wcopy(gat.at[rows], gat.at[rows], "g", 0 if way > 0 else 1, k, 2 * (a + way) + b)
-
-    for q in range(Q):
-
-        @pl.when(a + 1 < A)
-        def _():
-            gcopy(a, q, 1).start()
-
-        @pl.when(a > 0)
-        def _():
-            gcopy(a, q, -1).start()
-
-        fcopy(a, q).start()
-
-    def g_pass(step, carry):
-        below, above = a - 1 - step // Q, a + 1 + step // Q
-        q = lax.rem(step, Q)
-
-        @pl.when(below >= 0)
-        def _():
-            gcopy(below, q, 1).wait_recv()
-
-            @pl.when(a + 1 < A)
+    def gcopy(ap, h, q, way):
+        rows = shard(b * A + ap, h, q, Cq)
+        k = ap if way > 0 else A + ap
+        return wcopy(gat.at[rows], gat.at[rows], "g", 0 if way > 0 else 1, (k * NH + h) * Q + q, 2 * (a + way) + b)
+
+    def straight(h):
+        return h > 0
+
+    def gdirect(ap, h, q):
+        rows = shard(mine, h, q, Cq)
+        k = a + (1 - (ap - a + A) // (A + 1)) * A
+        return wcopy(gat.at[rows], gat.at[rows], "g", 2, (k * NH + h) * Q + q, 2 * ap + b)
+
+    def z_done(h):
+        rows = slice(h * Hk, (h + 1) * Hk)
+        part = pl.ds(h * Hk, Hk)
+        wcopy(zsend.at[others, part], zrecv.at[others, part], "z", 0, h, pair).wait_recv()
+
+        def gain(k, carry):
+            r.zf[rows, :] = r.zf[rows, :] + zrecv[lax.rem(a + k, A), rows, :].astype(F32)
+            return carry
+
+        lax.fori_loop(1, A, gain, 0)
+        gat[shard(mine, h, 0, Hk), :] = r.zf[rows, :].astype(BF)
+        for q in range(Q):
+            fcopy(a, h, q).start()
+        if straight(h):
+
+            def send(step, carry):
+                for q in range(Q):
+                    gdirect(target(step), h, q).start()
+                return carry
+
+            lax.fori_loop(0, A - 1, send, 0)
+        else:
+            for q in range(Q):
+
+                @pl.when(a + 1 < A)
+                def _():
+                    gcopy(a, h, q, 1).start()
+
+                @pl.when(a > 0)
+                def _():
+                    gcopy(a, h, q, -1).start()
+
+    def g_pass(h, first, last):
+        def step(k, carry):
+            below, above = a - 1 - k // Q, a + 1 + k // Q
+            q = lax.rem(k, Q)
+
+            @pl.when(below >= 0)
             def _():
-                gcopy(below, q, 1).start()
-
-            fcopy(below, q).start()
-
-        @pl.when(above < A)
-        def _():
-            gcopy(above, q, -1).wait_recv()
-
-            @pl.when(a > 0)
+                gcopy(below, h, q, 1).wait_recv()
+
+                if not straight(h):
+
+                    @pl.when(a + 1 < A)
+                    def _():
+                        gcopy(below, h, q, 1).start()
+
+                fcopy(below, h, q).start()
+
+            @pl.when(above < A)
             def _():
-                gcopy(above, q, -1).start()
-
-            fcopy(above, q).start()
-
-        return carry
-
-    steps = (A - 1) * Q
-    third = min(Q, steps)
-    ex.uzn.wait(r.uzn)
+                gcopy(above, h, q, -1).wait_recv()
+
+                if not straight(h):
+
+                    @pl.when(a > 0)
+                    def _():
+                        gcopy(above, h, q, -1).start()
+
+                fcopy(above, h, q).start()
+
+            return carry
+
+        lax.fori_loop(min(first, A - 1) * Q, min(last, A - 1) * Q, step, 0)
+
+    if NH > 1:
+        z_sends(1, 0, 1)
+    z_done(0)
+    u_copy(n2, 1, n2).wait_recv()
+    u_copy(n2, 2, n1).start()
+    if NH > 1:
+        z_sends(1, 1, A)
+        z_own(1)
+    g_pass(0, 0, 1)
+    u_copy(n1, 0, n1).wait_recv()
+    u_copy(n3, 2, n1).wait_recv()
     acc = jnp.zeros((B, Fn), F32)
     for n in range(N):
         acc = acc + dot(r.uzn[n, :, :Hn], w2b[n * Hn : (n + 1) * Hn, :])
         acc = acc + dot(r.uzn[n, :, Hn:], om[:, n * Mn : (n + 1) * Mn], NT)
-    bfw = r.bfw[...].astype(F32)
-    bfall = jnp.concatenate([bfw[:, :Bg].reshape(B, Fn // 2), bfw[:, Bg:].reshape(B, Fn // 2)], axis=1)
-    r.db[...] = jnp.concatenate([acc, bfall], axis=0).astype(BF)
+    r.db[...] = jnp.concatenate([acc, unfold(r.bfw)], axis=0).astype(BF)
     for n in range(N):
         r.dhs[n] = dot(r.db[:B, :], w2b[n * Hn : (n + 1) * Hn, :], NT).astype(BF)
     ex.dhr.scatter(r.dhs, r.dhr)
     r.dhr[ni] = r.dhs[ni]
-
-    lax.fori_loop(0, third, g_pass, 0)
+    if NH > 1:
+        z_done(1)
+    g_pass(0, 1, 2)
 
     def two(v):
         return jnp.sum(jnp.sum(v * v, axis=1, keepdims=True), axis=0, keepdims=True)
@@ -518,10 +591,11 @@
     square = square * (1.0 / W) + two(r.zf[...] + dot(r.xbt[shard(mine), :], r.dpb[...])) + two(agt)
     r.nn[core] = jnp.broadcast_to(square, (8, 128))
     core_copy(r.nn, 1).start()
-    lax.fori_loop(third, min(2 * third, steps), g_pass, 0)
+    g_pass(0, 2, A)
     r.nw[chip] = core_sum(r.nn, 1)
     ex.nw.gather(r.nw)
-    lax.fori_loop(min(2 * third, steps), steps, g_pass, 0)
+    if NH > 1:
+        g_pass(1, 0, A)
     ex.nw.wait(r.nw)
     norm = jnp.sum(r.nw[...], axis=0)
     lanes = lax.broadcasted_iota(jnp.int32, (8, 128), 1)
@@ -534,19 +608,22 @@
     for name in live:
         vars(ex)[name].drain(getattr(r, name))
     x_side().wait_send()
-    for k in range(3):
+    for k in range(P):
         x_over(k).wait_send()
         x_pass(k).wait_send()
     for slot, k, p in ((ni, 0, n1), (ni, 1, n2), (n2, 2, n1)):
         ad_copy(slot, k, p).wait_send()
+        u_copy(slot, k, p).wait_send()
     core_copy(r.kn, 0).wait_send()
     core_copy(r.nn, 1).wait_send()
     wcopy(psend, precv, "p", 0, 0, pair).wait_send()
     wcopy(gat.at[ours], gat.at[ours], "f", 0, 0, pair).wait_send()
-    if A > 1:
-        wcopy(zsend.at[others], zrecv.at[others], "z", 0, 0, pair).wait_send()
+    wcopy(zsend.at[others], zrecv.at[others], "z", 0, 0, pair).wait_send()
+    if NH > 1:
+        direct = pl.ds(0, (A - 1) * Hk)
+        wcopy(gat.at[direct], gat.at[direct], "g", 2, 0, pair).wait_send()
     for k in range(A):
-        up, down = (pl.ds(0, n * Ck) for n in (k + 1, A - k))
+        up, down = (pl.ds(0, n * Hk) for n in (k + 1, A - k))
 
         @pl.when((a == k) & (a + 1 < A))
         def _():
@@ -664,6 +741,7 @@
     B, Ck = W * Bg, D // 2 // A
     hbm, vmem, smem = (pl.BlockSpec(memory_space=m) for m in (pl.ANY, pltpu.VMEM, pltpu.SMEM))
     resident = B <= 128
+    fold = max(1, min(S // 8, 128 // B))
     args = dict(
         data_x=(data_x, hbm), dgroup=(data_group.reshape(1, R), hbm), batch_x=(batch_x, hbm),
         bgroup=(batch_group, smem), bindex=(batch_index, smem), pindex=(prec_index, smem),
@@ -686,17 +764,17 @@
         xg=((N, R, D), BF), xT=((D, N * R), BF), hid=((N * R, Hn), BF), gd=((N * R, Hn), F32),
         dpre=((N * R, Hn), BF), pre=((R, Hn), F32), w1b=((D, Hn), BF),
         w2b=((H, Fn), BF), om=((Fn, M), BF), pwt=((S, Mn), F32),
-        xbg=((Bg, D), F32), xbs=((brow, D), BF), tgs=((Bg, S), F32), dgs=((1, R), jnp.int32), als=((S, R), F32), ph=((1, Mn), F32), ges=((N, Bg, Hn), F32), zes=((N, Bg, Mn), F32), bfs=((Bg, Fn), F32), zf=((Ck, Hn), F32), us=((W, Bg, Hn), F32), ags=((N, S, R), F32),
-        dhs=((N, B, Hn), BF), cz=((B, Mn), F32), sz=((Bg, Mn), F32), prior=((S, B), F32), gp=((B, Mn), F32),
+        xbg=((Bg, D), F32), xbs=((brow, D), BF), tgs=((Bg, S), F32), dgs=((1, R), jnp.int32), als=((S, R), F32), ph=((1, Mn), F32), ges=((N, Bg, Hn), F32), zes=((N, Bg, Mn), F32), bfs=((Bg, Fn), F32), zf=((Ck, Hn), F32), zt=((Ck // (2 if Ck % 32 == 0 else 1), Hn), F32), us=((W, 2 * Bg, Hn // 2), BF), ags=((N, S, R), F32),
+        dhs=((N, B, Hn), BF), cz=((B, Mn), F32), prior=((S, B), F32),
         metat=((128, B), F32), alphat=((S, N * R), F32), pmask=((B, N * R), F32), amat=((B, N * R), F32),
         gmat=((B, Hn), BF), db=((2 * B, Fn), BF),
-        psend=((A * Ck, Hn), BF), precv=((A * Ck, Hn), BF), zsend=((A, Ck, Hn), BF), zrecv=((A, Ck, Hn), BF),
+        psend=((A * Ck, Hn), BF), precv=((A * Ck, Hn), BF), zsend=((A, Ck, Hn), BF), zrecv=((A + 1, Ck, Hn), BF),
         gb=((B, Hn), F32),
         meta=((W, Bg, 128), F32), xbw=((W, 2 * Bg, D // 2), BF), hgw=((W, 2 * Bg, Hn), BF),
-        bfw=((W, 2 * Bg, Fn // 2), BF), gw=((W, 2 * Bg, Hn // 2), BF), kw=((W * N // 2, S, B), F32),
-        ur=((W, Bg, Hn), F32), uz=((W, 2 * Bg, Hn), BF), nw=((W * N // 2, 8, 128), F32),
+        bfw=((W, 2 * Bg, Fn // 2), BF), gw=((W, 2 * Bg, Hn // 2), BF), kw=((W * N // 2, S // fold, fold * B), F32),
+        ur=((W, 2 * Bg, Hn // 2), BF), uz=((W, 2 * Bg, Hn // 2), BF), szw=((W, 2 * Bg, Mn // 2), BF), nw=((W * N // 2, 8, 128), F32),
         xbn=((N, brow, D), F32), ad=((N, S + 8, R), F32), hbn=((N, 2 * Bg, Hn // 2), BF), ger=((N, Bg, Hn), F32), zer=((N, Bg, Mn), F32),
-        kn=((2, S, B), F32), agr=((N, S, R), F32), uzn=((N, B, Hn + Mn), BF), hbx=((N, B, Hn), BF), dhr=((N, B, Hn), BF),
+        kn=((2, S // fold, fold * B), F32), agr=((N, S, R), F32), uzn=((N, B, Hn + Mn), BF), hbx=((N, B, Hn), BF), dhr=((N, B, Hn), BF),
         nn=((2, 8, 128), F32),
     )
     if resident:
@@ -704,10 +782,10 @@
         outs.update(held)
     else:
         scratch.update(w1f=held["w1f"], w2f=held["w2f"])
-    Q = max(1, min(4, Ck // 16))
+    pieces = A * math.gcd(Ck // 16, 4)
     count = 2 * len(WIDE_EX + NARROW_EX + CHIP_EX)
-    sems = [("lsem", 14), ("x_s", 12), ("x_r", 12), ("es", count), ("p_s", 1), ("p_r", A * Q), ("z_s", 1), ("z_r", 1)]
-    sems += [("f_s", 1), ("f_r", 1), ("g_s", 2), ("g_r", 2 * A * Q)]
+    sems = [("lsem", 14), ("x_s", 17), ("x_r", 17), ("es", count), ("p_s", 1), ("p_r", pieces), ("z_s", 1), ("z_r", pieces + pieces // A)]
+    sems += [("f_s", 1), ("f_r", 1), ("g_s", 3), ("g_r", 2 * pieces)]
     names = [*args, *outs, *scratch] + [n for n, _ in sems]
     grads = pl.pallas_call(
         lambda *refs: step_kernel(W, N, resident, names, *refs),

time: 79.3 us -> 75.2 us (0.948)
  Pallas kernels: 77.8 us -> 73.7 us
    pallas_call x1, Pallas kernels: 69.4 us -> 65.3 us  [on_device(): pl.pallas_call(lambda *refs: step_kernel(W, N, resident, names, *refs), o...]
where the time goes in v6:
time: 75.2 us; the launch traced here: 75 us
  Pallas kernels  73.7 us (98%)
    pallas_call x1, Pallas kernels, on_device(): pl.pallas_call(lambda *refs: step_kernel(W, N, resident, names, *refs), o...  65.3 us
    pallas_call x1, Pallas kernels, on_device(): pl.pallas_call(lambda *refs: update_kernel(resident, slots, C, names2, *r...  8.4 us

profile of v6, /device:TPU:0, one launch (start us, length us, event | category | flops | bytes accessed | tf_op | source)
XLA Modules:
  0.0 75.0 jit_solution(15707313133445101988)
XLA Ops:
  0.7 0.0 copy-start
  0.7 0.0 copy-start.1
  0.7 0.0 copy-start.2
  0.7 65.3 %gradients.1 = (f32[8,128]{1,0:T(8,128)S(1)}, f32[16,256]{1,0:T(8,128)S(1)}, bf16[1024,512]{1,0:T(8,128)(2,1)S(1)}, bf16[1024,64]{1,0:T(8,128)(2,1)S(1)}, bf16[6...) custom-call(bf16[256,1024]{1,0:T(8,128)(2,1)} %refs_0_.1, ...), custom_call_target="tpu_custom_call" | custom-call | tf_op jit(solution)/shard_map/gradients/pallas_call | solution.py:790
  66.0 0.0 copy-done
  66.0 0.0 copy-done.1
  66.0 0.0 copy-done.2
  66.0 8.4 %adamw.1 = (f32[16,256]{1,0:T(8,128)}, f32[16,256]{1,0:T(8,128)}, f32[16,256]{1,0:T(8,128)}, f32[1024,512]{1,0:T(8,128)}, f32[1024,512]{1,0:T(8,128)}, /*index=5...) custom-call(f32[8,128]{1,0:T(8,128)S(1)} %get-tuple-element.37.refs_, ...), custom_call_target="tpu_custom_call" | custom-call | tf_op jit(solution)/shard_map/adamw/pallas_call | solution.py:816
  74.4 0.6 fusion
Async XLA Ops:
  0.7 65.4 %copy-start = (f32[256,16]{0,1:T(8,128)S(1)}, f32[256,16]{0,1:T(8,128)}, u32[]{:S(2)}) copy-start(f32[256,16]{0,1:T(8,128)} %param.37) | copy-start | bytes 49156
  0.7 65.4 %copy-start.1 = (f32[256,16]{0,1:T(8,128)S(1)}, f32[256,16]{0,1:T(8,128)}, u32[]{:S(2)}) copy-start(f32[256,16]{0,1:T(8,128)} %param.38) | copy-start | bytes 49156
  0.7 65.4 %copy-start.2 = (f32[256,16]{0,1:T(8,128)S(1)}, f32[256,16]{0,1:T(8,128)}, u32[]{:S(2)}) copy-start(f32[256,16]{0,1:T(8,128)} %param.39) | copy-start | bytes 49156

commit v7 on v6

--- a/solution.py
+++ b/solution.py
@@ -122,28 +122,18 @@
         pltpu.make_async_copy(r.targets, r.tgs, lsem.at[11]),
         pltpu.make_async_copy(r.dgroup, r.dgs, lsem.at[12]),
         pltpu.make_async_copy(r.alphat_own, r.als, lsem.at[13]),
+        pltpu.make_async_copy(r.bgroup, r.sm_g, lsem.at[14]),
+        pltpu.make_async_copy(r.bindex, r.sm_i, lsem.at[15]),
+        pltpu.make_async_copy(r.pindex, r.sm_p, lsem.at[16]),
+        pltpu.make_async_copy(r.ptable, r.sm_t, lsem.at[17]),
     ]
-    for load in small[:1] + loads[:1] + small[1:] + loads[1:]:
+    for load in small[:1] + loads[:1]:
         load.start()
-
     barrier = pltpu.get_barrier_semaphore()
-
     ex.kw.greet(barrier)
     ex.xbn.greet(barrier)
-    small[0].wait()
-    r.xbn[ni] = r.xbs[...].astype(F32)
-    lane = lax.broadcasted_iota(jnp.int32, (1, 128), 1)
-    for k in range(Bg):
-        prec_k = r.ptable[r.pindex[k]]
-        r.meta[wi, k : k + 1, :] = jnp.where(
-            lane == 0, r.bgroup[k].astype(F32),
-            jnp.where(lane == 1, r.bindex[k].astype(F32), jnp.where(lane == 2, prec_k, 0.0)))
-    for load in small[1:]:
-        load.wait()
-    r.meta[wi, :, S : 2 * S] = r.tgs[...]
-    r.ad[ni, 0:S, :] = r.als[...]
-    r.ad[ni, S : S + 8, :] = jnp.broadcast_to(r.dgs[...].astype(F32), (8, R))
-
+    for load in small[1:] + loads[1:]:
+        load.start()
     pl.semaphore_wait(barrier, W * N // 2 - 1 + N - 1)
 
     def xcopy(src, dst, k, p):
@@ -151,7 +141,7 @@
             src_ref=src, dst_ref=dst, send_sem=r.x_s.at[k], recv_sem=r.x_r.at[k],
             device_id={"narrow": p}, device_id_type=MESH)
 
-    cuts = (0, R * 4 // 16, R * 10 // 16, R)
+    cuts = (0, R * 4 // 16, R * 8 // 16, R * 10 // 16, R)
     P = len(cuts) - 1
 
     def piece(k, src=None, slot=None):
@@ -169,15 +159,27 @@
     def x_pass(k):
         return xcopy(*piece(k, slot=n2), 1 + P + k, n1)
 
+    small[0].wait()
+    r.xbn[ni] = r.xbs[...].astype(F32)
     ex.xbn.gather(r.xbn)
     x_over(0).start()
-    ex.meta.gather(r.meta)
+    for load in small[1:]:
+        load.wait()
+    r.ad[ni, 0:S, :] = r.als[...]
+    r.ad[ni, S : S + 8, :] = jnp.broadcast_to(r.dgs[...].astype(F32), (8, R))
 
     def ad_copy(slot, k, p):
         return xcopy(r.ad.at[slot], r.ad.at[slot], 9 + k, p)
 
     ad_copy(ni, 1, n2).start()
     ad_copy(ni, 0, n1).start()
+    lane = lax.broadcasted_iota(jnp.int32, (1, 128), 1)
+    for k in range(Bg):
+        prec_k = r.sm_t[r.sm_p[k]]
+        r.meta[wi, k : k + 1, :] = jnp.where(
+            lane == 0, r.sm_g[k].astype(F32), jnp.where(lane == 1, r.sm_i[k].astype(F32), jnp.where(lane == 2, prec_k, 0.0)))
+    r.meta[wi, :, S : 2 * S] = r.tgs[...]
+    ex.meta.gather(r.meta)
 
     loads[0].wait()
 
@@ -196,6 +198,7 @@
     r.hbn[ni] = jnp.concatenate([hb[:, : Hn // 2], hb[:, Hn // 2 :]], axis=0).astype(BF)
     ex.hbn.gather(r.hbn)
     x_over(1).start()
+    x_over(2).start()
     x_side().start()
     r.hgw[wi] = jnp.concatenate([hb, gb], axis=0).astype(BF)
     ex.hgw.gather(r.hgw)
@@ -236,7 +239,8 @@
     r.bfs[...] = bfeat.astype(F32)
     gpart = dot(bfeat, w2b[...], NT)
     for n in range(N):
-        r.ges[n] = gpart[:, n * Hn : (n + 1) * Hn]
+        g = gpart[:, n * Hn : (n + 1) * Hn]
+        r.ges[n] = jnp.concatenate([g[:, : Hn // 2], g[:, Hn // 2 :]], axis=0).astype(BF)
     ex.ger.scatter(r.ges, r.ger)
     r.ger[ni] = r.ges[ni]
     loads[3].wait()
@@ -245,7 +249,7 @@
         r.zes[n] = zpart[:, n * Mn : (n + 1) * Mn]
     ex.zer.scatter(r.zes, r.zer)
     r.zer[ni] = r.zes[ni]
-    x_over(2).start()
+    x_over(3).start()
     later = []
     if resident:
         pairs = ((r.w1_m, r.m1), (r.w1_v, r.v1), (r.w2_m, r.m2), (r.w2_v, r.v2))
@@ -257,11 +261,14 @@
     ex.bfw.gather(r.bfw)
     loads[1].wait()
     block(ni)
+    xcopy(r.data_x, xg.at[n1], 0, n1).wait_recv()
+    block(n1)
+    turn(ni)
+    turn(n1)
     ex.ger.wait(r.ger)
-    gz = jnp.sum(r.ger[...], axis=0)
-    r.gw[wi] = jnp.concatenate([gz[:, : Hn // 2], gz[:, Hn // 2 : Hn]], axis=0).astype(BF)
+    r.gw[wi] = jnp.sum(r.ger[...].astype(F32), axis=0).astype(BF)
     ex.gw.gather(r.gw)
-    for k in range(2):
+    for k in range(3):
         xcopy(*piece(k, slot=n2), 1 + k, n2).wait_recv()
         x_pass(k).start()
     ad_copy(n2, 1, n2).wait_recv()
@@ -281,8 +288,6 @@
     def x_last(k):
         xcopy(*piece(k, slot=n3), 1 + P + k, n1).wait_recv()
 
-    xcopy(r.data_x, xg.at[n1], 0, n1).wait_recv()
-    block(n1)
     block(n2, 0, 2)
     x_last(0)
     x_last(1)
@@ -300,21 +305,36 @@
     col = lax.broadcasted_iota(jnp.int32, (1, N * R), 1) + wi * (N * R)
     first = (ni == 0).astype(F32)
     r.amat[...] = jnp.where(meta[:, 1:2] == col.astype(F32), first / meta[:, 2:3], 0.0)
-    turn(ni)
-    turn(n1)
-    xcopy(*piece(2, slot=n2), 3, n2).wait_recv()
-    x_pass(2).start()
-    block(n2, 2, 3)
-    x_last(2)
-    block(n3, 2, 3)
-
     ex.gw.wait(r.gw)
     gw = r.gw[...].astype(F32)
-    gmat = jnp.concatenate([gw[:, :Bg].reshape(B, Hn // 2), gw[:, Bg:].reshape(B, Hn // 2)], axis=1).astype(BF)
-    r.gmat[...] = gmat
-    amat = r.pmask[...] * dot(gmat, hid[...], NT) + r.amat[...]
-    r.amat[...] = amat
-    kal = dot(r.alphat[...], amat, NT, HIGH) + r.prior[...]
+    r.gmat[...] = jnp.concatenate([gw[:, :Bg].reshape(B, Hn // 2), gw[:, Bg:].reshape(B, Hn // 2)], axis=1).astype(BF)
+
+    def columns(q, first=0, last=P):
+        size = cuts[last] - cuts[first]
+        return pl.ds(pl.multiple_of(q * R + cuts[first], size), size)
+
+    def kernel_block(cols):
+        r.amat[:, cols] = r.pmask[:, cols] * dot(r.gmat[...], hid[cols, :], NT) + r.amat[:, cols]
+
+    def kalpha(cols):
+        return dot(r.alphat[:, cols], r.amat[:, cols], NT, HIGH)
+
+    for q in (ni, n1):
+        kernel_block(columns(q))
+    for q in (n2, n3):
+        kernel_block(columns(q, 0, 2))
+    xcopy(*piece(3, slot=n2), 4, n2).wait_recv()
+    x_pass(3).start()
+    block(n2, 2, 4)
+    kernel_block(columns(n2, 2, 4))
+    kal = r.prior[...] + (kalpha(columns(ni)) + kalpha(columns(n1))) + (kalpha(columns(n2)) + kalpha(columns(n3, 0, 2)))
+    r.prior[...] = kal
+    x_last(2)
+    x_last(3)
+    block(n3, 2, 4)
+
+    kernel_block(columns(n3, 2, 4))
+    kal = r.prior[...] + kalpha(columns(n3, 2, 4))
     fold = max(1, min(S // 8, 128 // B))
     r.kn[core] = jnp.concatenate([kal[k * (S // fold) : (k + 1) * (S // fold)] for k in range(fold)], axis=1)
 
@@ -339,12 +359,11 @@
     ex.xbw.wait(r.xbw)
     xbw = r.xbw[...].astype(F32)
     r.xbt[...] = jnp.concatenate([xbw[:, :Bg].reshape(B, D // 2), xbw[:, Bg:].reshape(B, D // 2)], axis=1).T.astype(BF)
+    prec = r.metat[2:3, :]
+    total = jnp.sum(prec, axis=1, keepdims=True)
     ex.kw.wait(r.kw)
-    prec = r.metat[2:3, :]
     kal = jnp.sum(r.kw[...], axis=0)
     resid = r.metat[S : 2 * S, :] - jnp.concatenate([kal[:, k * B : (k + 1) * B] for k in range(fold)], axis=0)
-    total = jnp.sum(prec, axis=1, keepdims=True)
-    loss = 0.5 * jnp.sum(jnp.sum(prec * (resid * resid), axis=1, keepdims=True), axis=0, keepdims=True)
     grt = prec * resid / total
 
     ds = (-r.pmask[...] * dot(grt, r.alphat[...], TN, HIGH)).astype(BF)
@@ -425,6 +444,7 @@
 
     pair_sends(0, 0, 2)
 
+    loss = 0.5 * jnp.sum(jnp.sum(prec * (resid * resid), axis=1, keepdims=True), axis=0, keepdims=True)
     agt = -dot(grt, r.amat[...], precision=HIGH)
     for n in range(N):
         r.ags[n] = agt[:, n * R : (n + 1) * R]
@@ -436,7 +456,13 @@
         v = buf[...].astype(F32)
         return jnp.concatenate([v[:, :Bg].reshape(B, -1), v[:, Bg:].reshape(B, -1)], axis=1)
 
-    r.uzn[ni, :, Hn:] = (unfold(r.szw) * dot(grt, r.pwt[...], TN, HIGH)).astype(BF)
+    r.dzn[ni] = (unfold(r.szw) * dot(grt, r.pwt[...], TN, HIGH)).astype(BF)
+
+    def dz_copy(slot, k, p):
+        return xcopy(r.dzn.at[slot], r.dzn.at[slot], 17 + k, p)
+
+    dz_copy(ni, 1, n2).start()
+    dz_copy(ni, 0, n1).start()
     ex.ur.wait(r.ur)
     r.ur[wi] = r.us[wi]
     r.uz[wi] = jnp.sum(r.ur[...].astype(F32), axis=0).astype(BF)
@@ -448,13 +474,15 @@
     z_sends(0, 1, 2)
     ex.bfw.wait(r.bfw)
     ex.uz.wait(r.uz)
-    r.uzn[ni, :, :Hn] = unfold(r.uz).astype(BF)
+    r.uzn[ni] = unfold(r.uz).astype(BF)
 
     def u_copy(slot, k, p):
         return xcopy(r.uzn.at[slot], r.uzn.at[slot], 14 + k, p)
 
     u_copy(ni, 1, n2).start()
     u_copy(ni, 0, n1).start()
+    dz_copy(n2, 1, n2).wait_recv()
+    dz_copy(n2, 2, n1).start()
     z_sends(0, 2, A)
     z_own(0)
 
@@ -470,16 +498,14 @@
 
     def gcopy(ap, h, q, way):
         rows = shard(b * A + ap, h, q, Cq)
-        k = ap if way > 0 else A + ap
-        return wcopy(gat.at[rows], gat.at[rows], "g", 0 if way > 0 else 1, (k * NH + h) * Q + q, 2 * (a + way) + b)
+        return wcopy(gat.at[rows], gat.at[rows], "g", 0 if way > 0 else 1, (ap * NH + h) * Q + q, 2 * (a + way) + b)
 
     def straight(h):
         return h > 0
 
     def gdirect(ap, h, q):
         rows = shard(mine, h, q, Cq)
-        k = a + (1 - (ap - a + A) // (A + 1)) * A
-        return wcopy(gat.at[rows], gat.at[rows], "g", 2, (k * NH + h) * Q + q, 2 * ap + b)
+        return wcopy(gat.at[rows], gat.at[rows], "g", 2, (a * NH + h) * Q + q, 2 * ap + b)
 
     def z_done(h):
         rows = slice(h * Hk, (h + 1) * Hk)
@@ -548,24 +574,26 @@
 
     if NH > 1:
         z_sends(1, 0, 1)
-    z_done(0)
     u_copy(n2, 1, n2).wait_recv()
     u_copy(n2, 2, n1).start()
+    z_done(0)
     if NH > 1:
         z_sends(1, 1, A)
         z_own(1)
-    g_pass(0, 0, 1)
     u_copy(n1, 0, n1).wait_recv()
     u_copy(n3, 2, n1).wait_recv()
+    dz_copy(n1, 0, n1).wait_recv()
+    dz_copy(n3, 2, n1).wait_recv()
     acc = jnp.zeros((B, Fn), F32)
     for n in range(N):
-        acc = acc + dot(r.uzn[n, :, :Hn], w2b[n * Hn : (n + 1) * Hn, :])
-        acc = acc + dot(r.uzn[n, :, Hn:], om[:, n * Mn : (n + 1) * Mn], NT)
+        acc = acc + dot(r.uzn[n], w2b[n * Hn : (n + 1) * Hn, :])
+        acc = acc + dot(r.dzn[n], om[:, n * Mn : (n + 1) * Mn], NT)
     r.db[...] = jnp.concatenate([acc, unfold(r.bfw)], axis=0).astype(BF)
     for n in range(N):
         r.dhs[n] = dot(r.db[:B, :], w2b[n * Hn : (n + 1) * Hn, :], NT).astype(BF)
     ex.dhr.scatter(r.dhs, r.dhr)
     r.dhr[ni] = r.dhs[ni]
+    g_pass(0, 0, 1)
     if NH > 1:
         z_done(1)
     g_pass(0, 1, 2)
@@ -577,7 +605,7 @@
     for n in range(N):
         if n == 0:
             ex.hbx.wait(r.hbx)
-        hu = jnp.concatenate([r.hbx[n], r.uzn[n, :, :Hn]], axis=0)
+        hu = jnp.concatenate([r.hbx[n], r.uzn[n]], axis=0)
         g2 = dot(hu, r.db[...], TN)
         r.g2[n * Hn : (n + 1) * Hn, :] = g2
         square = square + two(g2)
@@ -591,11 +619,13 @@
     square = square * (1.0 / W) + two(r.zf[...] + dot(r.xbt[shard(mine), :], r.dpb[...])) + two(agt)
     r.nn[core] = jnp.broadcast_to(square, (8, 128))
     core_copy(r.nn, 1).start()
+    if NH > 1:
+        g_pass(1, 0, 1)
     g_pass(0, 2, A)
     r.nw[chip] = core_sum(r.nn, 1)
     ex.nw.gather(r.nw)
     if NH > 1:
-        g_pass(1, 0, A)
+        g_pass(1, 1, A)
     ex.nw.wait(r.nw)
     norm = jnp.sum(r.nw[...], axis=0)
     lanes = lax.broadcasted_iota(jnp.int32, (8, 128), 1)
@@ -614,6 +644,7 @@
     for slot, k, p in ((ni, 0, n1), (ni, 1, n2), (n2, 2, n1)):
         ad_copy(slot, k, p).wait_send()
         u_copy(slot, k, p).wait_send()
+        dz_copy(slot, k, p).wait_send()
     core_copy(r.kn, 0).wait_send()
     core_copy(r.nn, 1).wait_send()
     wcopy(psend, precv, "p", 0, 0, pair).wait_send()
@@ -658,6 +689,11 @@
             load.start()
         for load in loads:
             load.wait()
+    for k in range(3):
+        r.s3[k] = r.scal[0:1, k : k + 1]
+    last = [pltpu.make_async_copy(r.s3.at[k], dst, r.asem.at[3 + k]) for k, dst in enumerate((r.loss, r.total, r.normsq))]
+    for copy in last:
+        copy.start()
     small = [pltpu.make_async_copy(src, r.asl.at[k], r.asem.at[k]) for k, src in enumerate((r.at, r.atm, r.atv))]
     for load in small:
         load.start()
@@ -717,13 +753,13 @@
     am, av, an = adamw(r.asl[0], clip * r.agrad[...], r.asl[1], r.asl[2], 0.2, 0.0)
     for k, v in enumerate((am, av, an)):
         r.ast[k] = v
-    last = [pltpu.make_async_copy(r.ast.at[k], dst, r.asem.at[k]) for k, dst in enumerate((r.amo, r.avo, r.ano))]
-    for copy in last:
+    alphas = [pltpu.make_async_copy(r.ast.at[k], dst, r.asem.at[k]) for k, dst in enumerate((r.amo, r.avo, r.ano))]
+    for copy in alphas:
         copy.start()
     for k in range(slots):
         for copy in copies(outs1, k, pl.ds(0, C)):
             copy.wait()
-    for copy in last:
+    for copy in last + alphas:
         copy.wait()
 
 
@@ -739,13 +775,13 @@
     F, M = omega.shape
     Hn, Fn, Mn, H = w1_master.shape[1], w2_master.shape[1], M // N, w2_master.shape[0]
     B, Ck = W * Bg, D // 2 // A
-    hbm, vmem, smem = (pl.BlockSpec(memory_space=m) for m in (pl.ANY, pltpu.VMEM, pltpu.SMEM))
+    hbm, vmem = (pl.BlockSpec(memory_space=m) for m in (pl.ANY, pltpu.VMEM))
     resident = B <= 128
     fold = max(1, min(S // 8, 128 // B))
     args = dict(
         data_x=(data_x, hbm), dgroup=(data_group.reshape(1, R), hbm), batch_x=(batch_x, hbm),
-        bgroup=(batch_group, smem), bindex=(batch_index, smem), pindex=(prec_index, smem),
-        ptable=(prec_table, smem), targets=(targets, hbm), omega=(omega, hbm),
+        bgroup=(batch_group, hbm), bindex=(batch_index, hbm), pindex=(prec_index, hbm),
+        ptable=(prec_table, hbm), targets=(targets, hbm), omega=(omega, hbm),
         phase=(phase.reshape(1, M), hbm), prior_wt=(prior_w.T, hbm), w1=(w1_master, hbm),
         w2=(w2_master, hbm), alphat_own=(alpha.T, hbm),
     )
@@ -764,7 +800,7 @@
         xg=((N, R, D), BF), xT=((D, N * R), BF), hid=((N * R, Hn), BF), gd=((N * R, Hn), F32),
         dpre=((N * R, Hn), BF), pre=((R, Hn), F32), w1b=((D, Hn), BF),
         w2b=((H, Fn), BF), om=((Fn, M), BF), pwt=((S, Mn), F32),
-        xbg=((Bg, D), F32), xbs=((brow, D), BF), tgs=((Bg, S), F32), dgs=((1, R), jnp.int32), als=((S, R), F32), ph=((1, Mn), F32), ges=((N, Bg, Hn), F32), zes=((N, Bg, Mn), F32), bfs=((Bg, Fn), F32), zf=((Ck, Hn), F32), zt=((Ck // (2 if Ck % 32 == 0 else 1), Hn), F32), us=((W, 2 * Bg, Hn // 2), BF), ags=((N, S, R), F32),
+        xbg=((Bg, D), F32), xbs=((brow, D), BF), tgs=((Bg, S), F32), dgs=((1, R), jnp.int32), als=((S, R), F32), ph=((1, Mn), F32), ges=((N, 2 * Bg, Hn // 2), BF), zes=((N, Bg, Mn), F32), bfs=((Bg, Fn), F32), zf=((Ck, Hn), F32), zt=((Ck // (2 if Ck % 32 == 0 else 1), Hn), F32), us=((W, 2 * Bg, Hn // 2), BF), ags=((N, S, R), F32),
         dhs=((N, B, Hn), BF), cz=((B, Mn), F32), prior=((S, B), F32),
         metat=((128, B), F32), alphat=((S, N * R), F32), pmask=((B, N * R), F32), amat=((B, N * R), F32),
         gmat=((B, Hn), BF), db=((2 * B, Fn), BF),
@@ -773,8 +809,8 @@
         meta=((W, Bg, 128), F32), xbw=((W, 2 * Bg, D // 2), BF), hgw=((W, 2 * Bg, Hn), BF),
         bfw=((W, 2 * Bg, Fn // 2), BF), gw=((W, 2 * Bg, Hn // 2), BF), kw=((W * N // 2, S // fold, fold * B), F32),
         ur=((W, 2 * Bg, Hn // 2), BF), uz=((W, 2 * Bg, Hn // 2), BF), szw=((W, 2 * Bg, Mn // 2), BF), nw=((W * N // 2, 8, 128), F32),
-        xbn=((N, brow, D), F32), ad=((N, S + 8, R), F32), hbn=((N, 2 * Bg, Hn // 2), BF), ger=((N, Bg, Hn), F32), zer=((N, Bg, Mn), F32),
-        kn=((2, S // fold, fold * B), F32), agr=((N, S, R), F32), uzn=((N, B, Hn + Mn), BF), hbx=((N, B, Hn), BF), dhr=((N, B, Hn), BF),
+        xbn=((N, brow, D), F32), ad=((N, S + 8, R), F32), hbn=((N, 2 * Bg, Hn // 2), BF), ger=((N, 2 * Bg, Hn // 2), BF), zer=((N, Bg, Mn), F32),
+        kn=((2, S // fold, fold * B), F32), agr=((N, S, R), F32), uzn=((N, B, Hn), BF), dzn=((N, B, Mn), BF), hbx=((N, B, Hn), BF), dhr=((N, B, Hn), BF),
         nn=((2, 8, 128), F32),
     )
     if resident:
@@ -784,30 +820,34 @@
         scratch.update(w1f=held["w1f"], w2f=held["w2f"])
     pieces = A * math.gcd(Ck // 16, 4)
     count = 2 * len(WIDE_EX + NARROW_EX + CHIP_EX)
-    sems = [("lsem", 14), ("x_s", 17), ("x_r", 17), ("es", count), ("p_s", 1), ("p_r", pieces), ("z_s", 1), ("z_r", pieces + pieces // A)]
-    sems += [("f_s", 1), ("f_r", 1), ("g_s", 3), ("g_r", 2 * pieces)]
-    names = [*args, *outs, *scratch] + [n for n, _ in sems]
+    sems = [("lsem", 18), ("x_s", 20), ("x_r", 20), ("es", count), ("p_s", 1), ("p_r", pieces), ("z_s", 1), ("z_r", pieces + pieces // A)]
+    sems += [("f_s", 1), ("f_r", 1), ("g_s", 3), ("g_r", pieces)]
+    smem = dict(sm_g=(Bg, jnp.int32), sm_i=(Bg, jnp.int32), sm_p=(Bg, jnp.int32), sm_t=(prec_table.shape[0], F32))
+    names = [*args, *outs, *scratch, *smem] + [n for n, _ in sems]
     grads = pl.pallas_call(
         lambda *refs: step_kernel(W, N, resident, names, *refs),
         out_shape=[(pltpu.VMEM if resident else jax.ShapeDtypeStruct)(s, t) for s, t in outs.values()],
         in_specs=[spec for _, spec in args.values()],
         out_specs=[vmem] * len(outs),
-        scratch_shapes=[pltpu.VMEM(s, t) for s, t in scratch.values()] + [pltpu.SemaphoreType.DMA((k,)) for _, k in sems],
+        scratch_shapes=[pltpu.VMEM(s, t) for s, t in scratch.values()]
+        + [pltpu.SMEM((k,), t) for k, t in smem.values()]
+        + [pltpu.SemaphoreType.DMA((k,)) for _, k in sems],
         compiler_params=pltpu.CompilerParams(collective_id=0, has_side_effects=True, vmem_limit_bytes=(62 if not resident else 39) * 2**20),
         name="gradients",
     )(*[v for v, _ in args.values()])
 
     args2 = {k: (v, vmem) for k, v in zip(outs, grads)}
     args2.update(at=(alpha.T, hbm), atm=(alpha_moment.T, hbm), atv=(alpha_second.T, hbm))
-    C, slots = 256, 3
+    C, slots = 256, 4
     outs2 = dict(amo=((S, R), F32, hbm), avo=((S, R), F32, hbm), ano=((S, R), F32, hbm))
+    outs2.update(loss=((1, 1), F32, hbm), total=((1, 1), F32, hbm), normsq=((1, 1), F32, hbm))
     for k, shape in (("1", (D, Hn)), ("2", (H, Fn))):
         outs2.update({"m" + k + "o": (shape, F32, hbm), "v" + k + "o": (shape, F32, hbm)})
         outs2.update({"n" + k + "o": (shape, F32, hbm), "c" + k + "o": (shape, BF, hbm)})
     scratch2 = dict(
         gs=pltpu.VMEM((D, Hn), F32), sm=pltpu.VMEM((slots, C, Hn), F32), sv=pltpu.VMEM((slots, C, Hn), F32),
         sn=pltpu.VMEM((slots, C, Hn), F32), sc=pltpu.VMEM((slots, C, Hn), BF), osem=pltpu.SemaphoreType.DMA((slots, 4)),
-        asl=pltpu.VMEM((3, S, R), F32), ast=pltpu.VMEM((3, S, R), F32), asem=pltpu.SemaphoreType.DMA((3,)),
+        asl=pltpu.VMEM((3, S, R), F32), ast=pltpu.VMEM((3, S, R), F32), asem=pltpu.SemaphoreType.DMA((6,)), s3=pltpu.VMEM((3, 1, 1), F32),
     )
     if not resident:
         args2.update(state)
@@ -819,13 +859,12 @@
         in_specs=[spec for _, spec in args2.values()],
         out_specs=[spec for _, _, spec in outs2.values()],
         scratch_shapes=list(scratch2.values()),
-        compiler_params=pltpu.CompilerParams(vmem_limit_bytes=(36 if not resident else 10) * 2**20),
+        compiler_params=pltpu.CompilerParams(vmem_limit_bytes=(36 if not resident else 12) * 2**20),
         name="adamw",
     )(*[v for v, _ in args2.values()])
     new = dict(zip(outs2, new))
-    scal = grads[0]
     return (
-        scal[0, 0], scal[0, 1], scal[0, 2],
+        new["loss"].reshape(()), new["total"].reshape(()), new["normsq"].reshape(()),
         new["m1o"], new["v1o"], new["n1o"], new["c1o"],
         new["m2o"], new["v2o"], new["n2o"], new["c2o"],
         new["amo"].T, new["avo"].T, new["ano"].T,

time: 75.2 us -> 72.8 us (0.968)
  Pallas kernels: 73.7 us -> 71.9 us
    pallas_call x1, Pallas kernels: 65.3 us -> 63.7 us  [on_device(): pl.pallas_call(lambda *refs: step_kernel(W, N, resident, names, *refs), o...]
where the time goes in v7:
time: 72.8 us; the launch traced here: 72.6 us
  Pallas kernels  71.9 us (99%)
    pallas_call x1, Pallas kernels, on_device(): pl.pallas_call(lambda *refs: step_kernel(W, N, resident, names, *refs), o...  63.7 us
    pallas_call x1, Pallas kernels, on_device(): pl.pallas_call(lambda *refs: update_kernel(resident, slots, C, names2, *r...  8.17 us

profile of v7, /device:TPU:0, one launch (start us, length us, event | category | flops | bytes accessed | tf_op | source)
XLA Modules:
  0.0 72.6 jit_solution(5015677553606199095)
XLA Ops:
  0.7 0.0 copy-start
  0.7 0.0 copy-start.1
  0.7 0.0 copy-start.2
  0.7 63.7 %gradients.1 = (f32[8,128]{1,0:T(8,128)S(1)}, f32[16,256]{1,0:T(8,128)S(1)}, bf16[1024,512]{1,0:T(8,128)(2,1)S(1)}, bf16[1024,64]{1,0:T(8,128)(2,1)S(1)}, bf16[6...) custom-call(bf16[256,1024]{1,0:T(8,128)(2,1)} %refs_0_.1, ...), custom_call_target="tpu_custom_call" | custom-call | tf_op jit(solution)/shard_map/gradients/pallas_call | solution.py:827
  64.4 0.0 copy-done
  64.4 0.0 copy-done.1
  64.4 0.0 copy-done.2
  64.4 8.2 %adamw.1 = (f32[16,256]{1,0:T(8,128)}, f32[16,256]{1,0:T(8,128)}, f32[16,256]{1,0:T(8,128)}, f32[1,1]{1,0:T(1,128)}, f32[1,1]{1,0:T(1,128)}, /*index=5*/f32[1,1]...) custom-call(f32[8,128]{1,0:T(8,128)S(1)} %get-tuple-element.40.refs_, ...), custom_call_target="tpu_custom_call" | custom-call | tf_op jit(solution)/shard_map/adamw/pallas_call | solution.py:856
Async XLA Ops:
  0.7 63.7 %copy-start = (f32[256,16]{0,1:T(8,128)S(1)}, f32[256,16]{0,1:T(8,128)}, u32[]{:S(2)}) copy-start(f32[256,16]{0,1:T(8,128)} %param.37) | copy-start | bytes 49156
  0.7 63.7 %copy-start.1 = (f32[256,16]{0,1:T(8,128)S(1)}, f32[256,16]{0,1:T(8,128)}, u32[]{:S(2)}) copy-start(f32[256,16]{0,1:T(8,128)} %param.38) | copy-start | bytes 49156
  0.7 63.7 %copy-start.2 = (f32[256,16]{0,1:T(8,128)S(1)}, f32[256,16]{0,1:T(8,128)}, u32[]{:S(2)}) copy-start(f32[256,16]{0,1:T(8,128)} %param.39) | copy-start | bytes 49156

commit v8 on v7

--- a/solution.py
+++ b/solution.py
@@ -14,6 +14,7 @@
 GC = math.sqrt(2.0 / math.pi)
 F32 = jnp.float32
 BF = jnp.bfloat16
+DIRECT = 1
 
 
 def gelu_pair(pre):
@@ -166,7 +167,7 @@
     for load in small[1:]:
         load.wait()
     r.ad[ni, 0:S, :] = r.als[...]
-    r.ad[ni, S : S + 8, :] = jnp.broadcast_to(r.dgs[...].astype(F32), (8, R))
+    r.ad[ni, S : S + 1, :] = r.dgs[...].astype(F32)
 
     def ad_copy(slot, k, p):
         return xcopy(r.ad.at[slot], r.ad.at[slot], 9 + k, p)
@@ -246,7 +247,8 @@
     loads[3].wait()
     zpart = dot(r.bfs[...].astype(BF), om[...])
     for n in range(N):
-        r.zes[n] = zpart[:, n * Mn : (n + 1) * Mn]
+        z = zpart[:, n * Mn : (n + 1) * Mn]
+        r.zes[n] = jnp.concatenate([z[:, : Mn // 2], z[:, Mn // 2 :]], axis=0).astype(BF)
     ex.zer.scatter(r.zes, r.zer)
     r.zer[ni] = r.zes[ni]
     x_over(3).start()
@@ -258,7 +260,6 @@
         load.start()
     bf32 = r.bfs[...]
     r.bfw[wi] = jnp.concatenate([bf32[:, : Fn // 2], bf32[:, Fn // 2 :]], axis=0).astype(BF)
-    ex.bfw.gather(r.bfw)
     loads[1].wait()
     block(ni)
     xcopy(r.data_x, xg.at[n1], 0, n1).wait_recv()
@@ -276,7 +277,8 @@
     ex.zer.wait(r.zer)
     own_b = pl.ds(pl.multiple_of(wi * Bg, Bg), Bg)
     loads[5].wait()
-    angle = jnp.sum(r.zer[...], axis=0) + r.ph[...]
+    zeta = jnp.sum(r.zer[...].astype(F32), axis=0)
+    angle = jnp.concatenate([zeta[:Bg], zeta[Bg:]], axis=1) + r.ph[...]
     r.cz[...] = jnp.zeros_like(r.cz)
     r.cz[own_b, :] = scale * jnp.cos(angle)
     sz = scale * jnp.sin(angle)
@@ -321,10 +323,10 @@
 
     for q in (ni, n1):
         kernel_block(columns(q))
+    xcopy(*piece(3, slot=n2), 4, n2).wait_recv()
+    x_pass(3).start()
     for q in (n2, n3):
         kernel_block(columns(q, 0, 2))
-    xcopy(*piece(3, slot=n2), 4, n2).wait_recv()
-    x_pass(3).start()
     block(n2, 2, 4)
     kernel_block(columns(n2, 2, 4))
     kal = r.prior[...] + (kalpha(columns(ni)) + kalpha(columns(n1))) + (kalpha(columns(n2)) + kalpha(columns(n3, 0, 2)))
@@ -349,6 +351,7 @@
     chip = wi * (N // 2) + side
     r.kw[chip] = core_sum(r.kn, 0)
     ex.kw.gather(r.kw)
+    ex.bfw.gather(r.bfw)
     turn(n2)
     turn(n3)
     ex.hgw.wait(r.hgw)
@@ -381,13 +384,12 @@
 
     psend, precv, zsend, zrecv, gat = r.psend, r.precv, r.zsend, r.zrecv, r.gat
 
-    NH = 2 if Ck % 32 == 0 else 1
+    NH = math.gcd(Ck // 16, 4)
     Hk = Ck // NH
-    Q = 2 if Hk % 32 == 0 else 1
-    Cq = Hk // Q
+    Q, Cq = 1, Hk
 
     def grad_rows(row):
-        return dot(xT[pl.ds(pl.multiple_of(row, Hk), Hk), :], dpre[...])
+        return dot(xT[pl.ds(pl.multiple_of(row, Ck), Ck), :], dpre[...])
 
     def target(step):
         low = a // (A // 2)
@@ -402,47 +404,57 @@
         rows = pl.ds(pl.multiple_of(ap * Ck + h * Hk + q * Cq, Cq), Cq)
         return wcopy(psend.at[rows], precv.at[rows], "p", 0, ap * NH * Q + h * Q + q, pair)
 
-    def pair_chunk(h, ap):
-        base = ap * Ck + h * Hk
-        psend[pl.ds(pl.multiple_of(base, Hk), Hk), :] = grad_rows((1 - b) * half + base).astype(BF)
-        for q in range(Q):
-            pcopy(ap, h, q).start()
+    def rows_of(ap):
+        return pl.ds(pl.multiple_of(ap * Ck, Ck), Ck)
+
+    def pair_first(ap):
+        psend[rows_of(ap), :] = grad_rows((1 - b) * half + ap * Ck).astype(BF)
+        pcopy(ap, 0, 0).start()
 
     def pair_sends(h, first, last):
         def send(step, carry):
-            pair_chunk(h, target(step))
+            pcopy(target(step), h, 0).start()
             return carry
 
-        lax.fori_loop(min(first, A - 1), min(last, A - 1), send, 0)
-        if last >= A:
-            pair_chunk(h, a)
+        if h < NH:
+            lax.fori_loop(min(first, A - 1), min(last, A - 1), send, 0)
+            if last >= A:
+                pcopy(a, h, 0).start()
 
     def zcopy(ap, h, q):
         rows = pl.ds(h * Hk + q * Cq, Cq)
         return wcopy(zsend.at[ap, rows], zrecv.at[a, rows], "z", 0, h, 2 * ap + b)
 
-    def z_part(ap, h, q):
-        pcopy(ap, h, q).wait_recv()
-        rows = pl.ds(pl.multiple_of(ap * Ck + h * Hk + q * Cq, Cq), Cq)
-        return r.zt[q * Cq : (q + 1) * Cq, :] + precv[rows, :].astype(F32)
+    def own_part(ap, carry):
+        gd[rows_of(ap), :] = grad_rows(b * half + ap * Ck)
+        return carry
+
+    def z_part(ap, h):
+        pcopy(ap, h, 0).wait_recv()
+        rows = pl.ds(pl.multiple_of(ap * Ck + h * Hk, Hk), Hk)
+        return gd[rows, :] + precv[rows, :].astype(F32)
 
     def z_sends(h, first, last):
         def send(step, carry):
             ap = target(step)
-            r.zt[...] = grad_rows(b * half + ap * Ck + h * Hk)
-            for q in range(Q):
-                zsend[ap, h * Hk + q * Cq : h * Hk + (q + 1) * Cq, :] = z_part(ap, h, q).astype(BF)
-                zcopy(ap, h, q).start()
+            zsend[ap, h * Hk : (h + 1) * Hk, :] = z_part(ap, h).astype(BF)
+            zcopy(ap, h, 0).start()
             return carry
 
-        lax.fori_loop(min(first, A - 1), min(last, A - 1), send, 0)
+        if h < NH:
+            lax.fori_loop(min(first, A - 1), min(last, A - 1), send, 0)
 
     def z_own(h):
-        r.zt[...] = grad_rows(b * half + a * Ck + h * Hk)
-        for q in range(Q):
-            r.zf[h * Hk + q * Cq : h * Hk + (q + 1) * Cq, :] = z_part(a, h, q)
-
-    pair_sends(0, 0, 2)
+        if h < NH:
+            r.zf[h * Hk : (h + 1) * Hk, :] = z_part(a, h)
+
+    def first_sends(step, carry):
+        pair_first(target(step))
+        return carry
+
+    lax.fori_loop(0, A - 1, first_sends, 0)
+    pair_first(a)
+    pair_sends(1, 0, 2)
 
     loss = 0.5 * jnp.sum(jnp.sum(prec * (resid * resid), axis=1, keepdims=True), axis=0, keepdims=True)
     agt = -dot(grt, r.amat[...], precision=HIGH)
@@ -463,15 +475,17 @@
 
     dz_copy(ni, 1, n2).start()
     dz_copy(ni, 0, n1).start()
+    lax.fori_loop(0, A, own_part, 0)
     ex.ur.wait(r.ur)
     r.ur[wi] = r.us[wi]
     r.uz[wi] = jnp.sum(r.ur[...].astype(F32), axis=0).astype(BF)
     ex.uz.gather(r.uz)
-    pair_sends(0, 2, A)
-    z_sends(0, 0, 1)
-    for h in range(1, NH):
+    pair_sends(1, 2, A)
+    for h in range(2, NH):
         pair_sends(h, 0, A)
-    z_sends(0, 1, 2)
+    z_sends(0, 0, A)
+    z_own(0)
+    z_sends(1, 0, 1)
     ex.bfw.wait(r.bfw)
     ex.uz.wait(r.uz)
     r.uzn[ni] = unfold(r.uz).astype(BF)
@@ -483,8 +497,8 @@
     u_copy(ni, 0, n1).start()
     dz_copy(n2, 1, n2).wait_recv()
     dz_copy(n2, 2, n1).start()
-    z_sends(0, 2, A)
-    z_own(0)
+    z_sends(1, 1, A)
+    z_own(1)
 
     others = pl.ds(0, A - 1)
     mine = b * A + a
@@ -501,13 +515,15 @@
         return wcopy(gat.at[rows], gat.at[rows], "g", 0 if way > 0 else 1, (ap * NH + h) * Q + q, 2 * (a + way) + b)
 
     def straight(h):
-        return h > 0
+        return NH > 1 and h >= NH - DIRECT
 
     def gdirect(ap, h, q):
         rows = shard(mine, h, q, Cq)
         return wcopy(gat.at[rows], gat.at[rows], "g", 2, (a * NH + h) * Q + q, 2 * ap + b)
 
     def z_done(h):
+        if h >= NH:
+            return
         rows = slice(h * Hk, (h + 1) * Hk)
         part = pl.ds(h * Hk, Hk)
         wcopy(zsend.at[others, part], zrecv.at[others, part], "z", 0, h, pair).wait_recv()
@@ -540,6 +556,9 @@
                     gcopy(a, h, q, -1).start()
 
     def g_pass(h, first, last):
+        if h >= NH:
+            return
+
         def step(k, carry):
             below, above = a - 1 - k // Q, a + 1 + k // Q
             q = lax.rem(k, Q)
@@ -572,14 +591,17 @@
 
         lax.fori_loop(min(first, A - 1) * Q, min(last, A - 1) * Q, step, 0)
 
-    if NH > 1:
-        z_sends(1, 0, 1)
+    z_done(0)
+    z_sends(2, 0, A)
+    z_own(2)
     u_copy(n2, 1, n2).wait_recv()
     u_copy(n2, 2, n1).start()
-    z_done(0)
-    if NH > 1:
-        z_sends(1, 1, A)
-        z_own(1)
+    z_done(1)
+    g_pass(0, 0, 1)
+    z_sends(3, 0, 2)
+    z_done(2)
+    z_sends(3, 2, A)
+    z_own(3)
     u_copy(n1, 0, n1).wait_recv()
     u_copy(n3, 2, n1).wait_recv()
     dz_copy(n1, 0, n1).wait_recv()
@@ -593,10 +615,11 @@
         r.dhs[n] = dot(r.db[:B, :], w2b[n * Hn : (n + 1) * Hn, :], NT).astype(BF)
     ex.dhr.scatter(r.dhs, r.dhr)
     r.dhr[ni] = r.dhs[ni]
-    g_pass(0, 0, 1)
-    if NH > 1:
-        z_done(1)
+    g_pass(1, 0, 1)
     g_pass(0, 1, 2)
+    g_pass(2, 0, 1)
+    z_done(3)
+    g_pass(1, 1, 2)
 
     def two(v):
         return jnp.sum(jnp.sum(v * v, axis=1, keepdims=True), axis=0, keepdims=True)
@@ -619,13 +642,14 @@
     square = square * (1.0 / W) + two(r.zf[...] + dot(r.xbt[shard(mine), :], r.dpb[...])) + two(agt)
     r.nn[core] = jnp.broadcast_to(square, (8, 128))
     core_copy(r.nn, 1).start()
-    if NH > 1:
-        g_pass(1, 0, 1)
     g_pass(0, 2, A)
     r.nw[chip] = core_sum(r.nn, 1)
     ex.nw.gather(r.nw)
-    if NH > 1:
-        g_pass(1, 1, A)
+    g_pass(2, 1, 2)
+    g_pass(3, 0, 1)
+    g_pass(1, 2, A)
+    g_pass(2, 2, A)
+    g_pass(3, 1, A)
     ex.nw.wait(r.nw)
     norm = jnp.sum(r.nw[...], axis=0)
     lanes = lax.broadcasted_iota(jnp.int32, (8, 128), 1)
@@ -650,11 +674,12 @@
     wcopy(psend, precv, "p", 0, 0, pair).wait_send()
     wcopy(gat.at[ours], gat.at[ours], "f", 0, 0, pair).wait_send()
     wcopy(zsend.at[others], zrecv.at[others], "z", 0, 0, pair).wait_send()
-    if NH > 1:
-        direct = pl.ds(0, (A - 1) * Hk)
+    straights = sum(straight(h) for h in range(NH))
+    if straights:
+        direct = pl.ds(0, (A - 1) * Hk * straights)
         wcopy(gat.at[direct], gat.at[direct], "g", 2, 0, pair).wait_send()
     for k in range(A):
-        up, down = (pl.ds(0, n * Hk) for n in (k + 1, A - k))
+        up, down = (pl.ds(0, n * Hk * (NH - straights)) for n in (k + 1, A - k))
 
         @pl.when((a == k) & (a + 1 < A))
         def _():
@@ -800,7 +825,7 @@
         xg=((N, R, D), BF), xT=((D, N * R), BF), hid=((N * R, Hn), BF), gd=((N * R, Hn), F32),
         dpre=((N * R, Hn), BF), pre=((R, Hn), F32), w1b=((D, Hn), BF),
         w2b=((H, Fn), BF), om=((Fn, M), BF), pwt=((S, Mn), F32),
-        xbg=((Bg, D), F32), xbs=((brow, D), BF), tgs=((Bg, S), F32), dgs=((1, R), jnp.int32), als=((S, R), F32), ph=((1, Mn), F32), ges=((N, 2 * Bg, Hn // 2), BF), zes=((N, Bg, Mn), F32), bfs=((Bg, Fn), F32), zf=((Ck, Hn), F32), zt=((Ck // (2 if Ck % 32 == 0 else 1), Hn), F32), us=((W, 2 * Bg, Hn // 2), BF), ags=((N, S, R), F32),
+        xbg=((Bg, D), F32), xbs=((brow, D), BF), tgs=((Bg, S), F32), dgs=((1, R), jnp.int32), als=((S, R), F32), ph=((1, Mn), F32), ges=((N, 2 * Bg, Hn // 2), BF), zes=((N, 2 * Bg, Mn // 2), BF), bfs=((Bg, Fn), F32), zf=((Ck, Hn), F32), us=((W, 2 * Bg, Hn // 2), BF), ags=((N, S, R), F32),
         dhs=((N, B, Hn), BF), cz=((B, Mn), F32), prior=((S, B), F32),
         metat=((128, B), F32), alphat=((S, N * R), F32), pmask=((B, N * R), F32), amat=((B, N * R), F32),
         gmat=((B, Hn), BF), db=((2 * B, Fn), BF),
@@ -809,7 +834,7 @@
         meta=((W, Bg, 128), F32), xbw=((W, 2 * Bg, D // 2), BF), hgw=((W, 2 * Bg, Hn), BF),
         bfw=((W, 2 * Bg, Fn // 2), BF), gw=((W, 2 * Bg, Hn // 2), BF), kw=((W * N // 2, S // fold, fold * B), F32),
         ur=((W, 2 * Bg, Hn // 2), BF), uz=((W, 2 * Bg, Hn // 2), BF), szw=((W, 2 * Bg, Mn // 2), BF), nw=((W * N // 2, 8, 128), F32),
-        xbn=((N, brow, D), F32), ad=((N, S + 8, R), F32), hbn=((N, 2 * Bg, Hn // 2), BF), ger=((N, 2 * Bg, Hn // 2), BF), zer=((N, Bg, Mn), F32),
+        xbn=((N, brow, D), F32), ad=((N, S + 1, R), F32), hbn=((N, 2 * Bg, Hn // 2), BF), ger=((N, 2 * Bg, Hn // 2), BF), zer=((N, 2 * Bg, Mn // 2), BF),
         kn=((2, S // fold, fold * B), F32), agr=((N, S, R), F32), uzn=((N, B, Hn), BF), dzn=((N, B, Mn), BF), hbx=((N, B, Hn), BF), dhr=((N, B, Hn), BF),
         nn=((2, 8, 128), F32),
     )
@@ -820,7 +845,7 @@
         scratch.update(w1f=held["w1f"], w2f=held["w2f"])
     pieces = A * math.gcd(Ck // 16, 4)
     count = 2 * len(WIDE_EX + NARROW_EX + CHIP_EX)
-    sems = [("lsem", 18), ("x_s", 20), ("x_r", 20), ("es", count), ("p_s", 1), ("p_r", pieces), ("z_s", 1), ("z_r", pieces + pieces // A)]
+    sems = [("lsem", 18), ("x_s", 20), ("x_r", 20), ("es", count), ("p_s", 1), ("p_r", pieces), ("z_s", 1), ("z_r", 4)]
     sems += [("f_s", 1), ("f_r", 1), ("g_s", 3), ("g_r", pieces)]
     smem = dict(sm_g=(Bg, jnp.int32), sm_i=(Bg, jnp.int32), sm_p=(Bg, jnp.int32), sm_t=(prec_table.shape[0], F32))
     names = [*args, *outs, *scratch, *smem] + [n for n, _ in sems]

time: 72.8 us -> 72.2 us (level)
  no operation moved by 1% of the time
where the time goes in v8:
time: 72.2 us; the launch traced here: 72.1 us
  Pallas kernels  71.3 us (99%)
    pallas_call x1, Pallas kernels, on_device(): pl.pallas_call(lambda *refs: step_kernel(W, N, resident, names, *refs), o...  63.2 us
    pallas_call x1, Pallas kernels, on_device(): pl.pallas_call(lambda *refs: update_kernel(resident, slots, C, names2, *r...  8.17 us

profile of v8, /device:TPU:0, one launch (start us, length us, event | category | flops | bytes accessed | tf_op | source)
XLA Modules:
  0.0 72.1 jit_solution(7302808708253138493)
XLA Ops:
  0.7 0.0 copy-start
  0.7 0.0 copy-start.1
  0.7 0.0 copy-start.2
  0.7 63.2 %gradients.1 = (f32[8,128]{1,0:T(8,128)S(1)}, f32[16,256]{1,0:T(8,128)S(1)}, bf16[1024,512]{1,0:T(8,128)(2,1)S(1)}, bf16[1024,64]{1,0:T(8,128)(2,1)S(1)}, bf16[6...) custom-call(bf16[256,1024]{1,0:T(8,128)(2,1)} %refs_0_.1, ...), custom_call_target="tpu_custom_call" | custom-call | tf_op jit(solution)/shard_map/gradients/pallas_call | solution.py:852
  63.9 0.0 copy-done
  63.9 0.0 copy-done.1
  63.9 0.0 copy-done.2
  63.9 8.2 %adamw.1 = (f32[16,256]{1,0:T(8,128)}, f32[16,256]{1,0:T(8,128)}, f32[16,256]{1,0:T(8,128)}, f32[1,1]{1,0:T(1,128)}, f32[1,1]{1,0:T(1,128)}, /*index=5*/f32[1,1]...) custom-call(f32[8,128]{1,0:T(8,128)S(1)} %get-tuple-element.40.refs_, ...), custom_call_target="tpu_custom_call" | custom-call | tf_op jit(solution)/shard_map/adamw/pallas_call | solution.py:881
Async XLA Ops:
  0.7 63.2 %copy-start = (f32[256,16]{0,1:T(8,128)S(1)}, f32[256,16]{0,1:T(8,128)}, u32[]{:S(2)}) copy-start(f32[256,16]{0,1:T(8,128)} %param.37) | copy-start | bytes 49156
  0.7 63.2 %copy-start.1 = (f32[256,16]{0,1:T(8,128)S(1)}, f32[256,16]{0,1:T(8,128)}, u32[]{:S(2)}) copy-start(f32[256,16]{0,1:T(8,128)} %param.38) | copy-start | bytes 49156
  0.7 63.2 %copy-start.2 = (f32[256,16]{0,1:T(8,128)S(1)}, f32[256,16]{0,1:T(8,128)}, u32[]{:S(2)}) copy-start(f32[256,16]{0,1:T(8,128)} %param.39) | copy-start | bytes 49156

commit v9 on v8

--- a/solution.py
+++ b/solution.py
@@ -729,7 +729,7 @@
     def copies(outs, slot, rows):
         return [pltpu.make_async_copy(buf.at[slot], out.at[rows], r.osem.at[slot, k]) for k, (buf, out) in enumerate(zip(ring, outs))]
 
-    def chunk(grad, state, outs, k, ahead):
+    def chunk(grad, state, outs, k, ahead, split=1):
         w, m, v = state
         slot = lax.rem(k + ahead, slots)
         base = pl.multiple_of(k * C, C)
@@ -741,7 +741,7 @@
 
         if ahead:
             drain()
-        else:
+        elif split == 1:
             pl.when(k >= slots)(drain)
 
         def part(j, carry):
@@ -754,9 +754,17 @@
             r.sc[slot, dst, :] = wn.astype(BF)
             return carry
 
-        lax.fori_loop(0, C // 16, part, 0, unroll=True)
-        for copy in copies(outs, slot, rows):
-            copy.start()
+        if split == 1:
+            lax.fori_loop(0, C // 16, part, 0, unroll=True)
+            for copy in copies(outs, slot, rows):
+                copy.start()
+            return
+        size = C // split
+        for n in range(split):
+            lax.fori_loop(n * size // 16, (n + 1) * size // 16, part, 0, unroll=True)
+            here = pl.ds(n * size, size)
+            for i, (buf, out) in enumerate(zip(ring, outs)):
+                pltpu.make_async_copy(buf.at[slot, here], out.at[here], r.osem.at[slot, i]).start()
 
     outs1 = (r.m1o, r.v1o, r.n1o, r.c1o)
     outs2 = (r.m2o, r.v2o, r.n2o, r.c2o)
@@ -770,7 +778,8 @@
         chunk(r.gs, (r.w1f, r.m1, r.v1), outs1, k, count2)
         return carry
 
-    lax.fori_loop(0, count2, step2, 0)
+    chunk(r.g2, (r.w2f, r.m2, r.v2), outs2, 0, 0, split=C // 64)
+    lax.fori_loop(1, count2, step2, 0)
     r.gs[...] = r.gat[...].astype(F32) + dot(r.xbt[...], r.dpb[...])
     lax.fori_loop(0, count1, step1, 0)
     for load in small:

time: 72.2 us -> 72 us (level)
  no operation moved by 1% of the time
where the time goes in v9:
time: 72 us; the launch traced here: 71.8 us
  Pallas kernels  71.1 us (99%)
    pallas_call x1, Pallas kernels, on_device(): pl.pallas_call(lambda *refs: step_kernel(W, N, resident, names, *refs), o...  63.2 us
    pallas_call x1, Pallas kernels, on_device(): pl.pallas_call(lambda *refs: update_kernel(resident, slots, C, names2, *r...  7.95 us

profile of v9, /device:TPU:0, one launch (start us, length us, event | category | flops | bytes accessed | tf_op | source)
XLA Modules:
  0.0 71.8 jit_solution(7615651418022509783)
XLA Ops:
  0.7 0.0 copy-start
  0.7 0.0 copy-start.1
  0.7 0.0 copy-start.2
  0.7 63.2 %gradients.1 = (f32[8,128]{1,0:T(8,128)S(1)}, f32[16,256]{1,0:T(8,128)S(1)}, bf16[1024,512]{1,0:T(8,128)(2,1)S(1)}, bf16[1024,64]{1,0:T(8,128)(2,1)S(1)}, bf16[6...) custom-call(bf16[256,1024]{1,0:T(8,128)(2,1)} %refs_0_.1, ...), custom_call_target="tpu_custom_call" | custom-call | tf_op jit(solution)/shard_map/gradients/pallas_call | solution.py:861
  63.9 0.0 copy-done
  63.9 0.0 copy-done.1
  63.9 0.0 copy-done.2
  63.9 7.9 %adamw.1 = (f32[16,256]{1,0:T(8,128)}, f32[16,256]{1,0:T(8,128)}, f32[16,256]{1,0:T(8,128)}, f32[1,1]{1,0:T(1,128)}, f32[1,1]{1,0:T(1,128)}, /*index=5*/f32[1,1]...) custom-call(f32[8,128]{1,0:T(8,128)S(1)} %get-tuple-element.40.refs_, ...), custom_call_target="tpu_custom_call" | custom-call | tf_op jit(solution)/shard_map/adamw/pallas_call | solution.py:890
Async XLA Ops:
  0.7 63.2 %copy-start = (f32[256,16]{0,1:T(8,128)S(1)}, f32[256,16]{0,1:T(8,128)}, u32[]{:S(2)}) copy-start(f32[256,16]{0,1:T(8,128)} %param.37) | copy-start | bytes 49156
  0.7 63.2 %copy-start.1 = (f32[256,16]{0,1:T(8,128)S(1)}, f32[256,16]{0,1:T(8,128)}, u32[]{:S(2)}) copy-start(f32[256,16]{0,1:T(8,128)} %param.38) | copy-start | bytes 49156
  0.7 63.2 %copy-start.2 = (f32[256,16]{0,1:T(8,128)S(1)}, f32[256,16]{0,1:T(8,128)}, u32[]{:S(2)}) copy-start(f32[256,16]{0,1:T(8,128)} %param.39) | copy-start | bytes 49156

commit v10 on v8

--- a/solution.py
+++ b/solution.py
@@ -137,9 +137,12 @@
         load.start()
     pl.semaphore_wait(barrier, W * N // 2 - 1 + N - 1)
 
+    def kind_of(k):
+        return 0 if k < 9 else 1 if k < 12 else k - 10 if k < 14 else 4 if k < 17 else 5
+
     def xcopy(src, dst, k, p):
         return pltpu.make_async_remote_copy(
-            src_ref=src, dst_ref=dst, send_sem=r.x_s.at[k], recv_sem=r.x_r.at[k],
+            src_ref=src, dst_ref=dst, send_sem=r.x_s.at[kind_of(k)], recv_sem=r.x_r.at[k],
             device_id={"narrow": p}, device_id_type=MESH)
 
     cuts = (0, R * 4 // 16, R * 8 // 16, R * 10 // 16, R)
@@ -661,14 +664,8 @@
 
     for name in live:
         vars(ex)[name].drain(getattr(r, name))
-    x_side().wait_send()
-    for k in range(P):
-        x_over(k).wait_send()
-        x_pass(k).wait_send()
-    for slot, k, p in ((ni, 0, n1), (ni, 1, n2), (n2, 2, n1)):
-        ad_copy(slot, k, p).wait_send()
-        u_copy(slot, k, p).wait_send()
-        dz_copy(slot, k, p).wait_send()
+    for buf, k in ((xg, 0), (r.ad, 9), (r.uzn, 14), (r.dzn, 17)):
+        xcopy(buf.at[pl.ds(0, 3)], buf.at[pl.ds(0, 3)], k, n1).wait_send()
     core_copy(r.kn, 0).wait_send()
     core_copy(r.nn, 1).wait_send()
     wcopy(psend, precv, "p", 0, 0, pair).wait_send()
@@ -845,7 +842,7 @@
         scratch.update(w1f=held["w1f"], w2f=held["w2f"])
     pieces = A * math.gcd(Ck // 16, 4)
     count = 2 * len(WIDE_EX + NARROW_EX + CHIP_EX)
-    sems = [("lsem", 18), ("x_s", 20), ("x_r", 20), ("es", count), ("p_s", 1), ("p_r", pieces), ("z_s", 1), ("z_r", 4)]
+    sems = [("lsem", 18), ("x_s", 6), ("x_r", 20), ("es", count), ("p_s", 1), ("p_r", pieces), ("z_s", 1), ("z_r", 4)]
     sems += [("f_s", 1), ("f_r", 1), ("g_s", 3), ("g_r", pieces)]
     smem = dict(sm_g=(Bg, jnp.int32), sm_i=(Bg, jnp.int32), sm_p=(Bg, jnp.int32), sm_t=(prec_table.shape[0], F32))
     names = [*args, *outs, *scratch, *smem] + [n for n, _ in sems]

time: 72.2 us -> 72.1 us (level)
  no operation moved by 1% of the time
where the time goes in v10:
time: 72.1 us; the launch traced here: 71.9 us
  Pallas kernels  71.2 us (99%)
    pallas_call x1, Pallas kernels, on_device(): pl.pallas_call(lambda *refs: step_kernel(W, N, resident, names, *refs), o...  63 us
    pallas_call x1, Pallas kernels, on_device(): pl.pallas_call(lambda *refs: update_kernel(resident, slots, C, names2, *r...  8.17 us

profile of v10, /device:TPU:0, one launch (start us, length us, event | category | flops | bytes accessed | tf_op | source)
XLA Modules:
  0.0 71.9 jit_solution(11190270489954410300)
XLA Ops:
  0.7 0.0 copy-start
  0.7 0.0 copy-start.1
  0.7 0.0 copy-start.2
  0.7 63.0 %gradients.1 = (f32[8,128]{1,0:T(8,128)S(1)}, f32[16,256]{1,0:T(8,128)S(1)}, bf16[1024,512]{1,0:T(8,128)(2,1)S(1)}, bf16[1024,64]{1,0:T(8,128)(2,1)S(1)}, bf16[6...) custom-call(bf16[256,1024]{1,0:T(8,128)(2,1)} %refs_0_.1, ...), custom_call_target="tpu_custom_call" | custom-call | tf_op jit(solution)/shard_map/gradients/pallas_call | solution.py:849
  63.7 0.0 copy-done
  63.7 0.0 copy-done.1
  63.7 0.0 copy-done.2
  63.7 8.2 %adamw.1 = (f32[16,256]{1,0:T(8,128)}, f32[16,256]{1,0:T(8,128)}, f32[16,256]{1,0:T(8,128)}, f32[1,1]{1,0:T(1,128)}, f32[1,1]{1,0:T(1,128)}, /*index=5*/f32[1,1]...) custom-call(f32[8,128]{1,0:T(8,128)S(1)} %get-tuple-element.40.refs_, ...), custom_call_target="tpu_custom_call" | custom-call | tf_op jit(solution)/shard_map/adamw/pallas_call | solution.py:878
Async XLA Ops:
  0.7 63.1 %copy-start = (f32[256,16]{0,1:T(8,128)S(1)}, f32[256,16]{0,1:T(8,128)}, u32[]{:S(2)}) copy-start(f32[256,16]{0,1:T(8,128)} %param.37) | copy-start | bytes 49156
  0.7 63.1 %copy-start.1 = (f32[256,16]{0,1:T(8,128)S(1)}, f32[256,16]{0,1:T(8,128)}, u32[]{:S(2)}) copy-start(f32[256,16]{0,1:T(8,128)} %param.38) | copy-start | bytes 49156
  0.7 63.1 %copy-start.2 = (f32[256,16]{0,1:T(8,128)S(1)}, f32[256,16]{0,1:T(8,128)}, u32[]{:S(2)}) copy-start(f32[256,16]{0,1:T(8,128)} %param.39) | copy-start | bytes 49156
